TPU v7x, 512 devices: a whole 4x8x8 slice. The times are simulated.
512 devices in a mesh: row: 32 (over x, y), col: 16 (over z, core).
Axes of the slice: x: 4, y: 8, z: 8, core: 2. Of those that a mesh axis runs over, the one named last changes fastest.
Arguments:
- matrix: float32 [16384, 16384], P('row', 'col'), may hold values from -16 to 16, as said below
Outputs:
- banded: float32 [16384, 16384], P('row', 'col')
- reflectors: float32 [2, 16384, 64], P(None, 'row')
- tfactors: float32 [2, 64, 64], replicated
Inputs may be any that keep to these rules, and one draw needn't show every extreme that they name: matrix is exactly symmetric.
All inputs are finite; a program needn't handle non-finite values.
Results may differ from a plain program's by a relative error of at most 0.0003.
Values sent between devices are 32-bit elements; how exact they have to be, the bound alone decides.
No kernel may reach another device: no remote copies, remote signals or barrier semaphores. Data moves between devices by JAX's collectives and lax.ppermute only.
A program may use at most 64 MiB of HBM per device.

v0:
```python
import functools

import jax
import jax.numpy as jnp
from jax import lax
from jax.experimental import pallas as pl
from jax.experimental.pallas import tpu as pltpu
from jax.sharding import PartitionSpec as P

NB = 64
precise = lax.Precision.HIGHEST


def nn(a, b):
    return lax.dot_general(
        a, b, (((1,), (0,)), ((), ())), precision=precise, preferred_element_type=jnp.float32
    )


def tn(a, b):
    return lax.dot_general(
        a, b, (((0,), (0,)), ((), ())), precision=precise, preferred_element_type=jnp.float32
    )


def nt(a, b):
    return lax.dot_general(
        a, b, (((1,), (1,)), ((), ())), precision=precise, preferred_element_type=jnp.float32
    )


def places():
    sub = lax.broadcasted_iota(jnp.int32, (NB, 2 * NB), 0)
    lane = lax.broadcasted_iota(jnp.int32, (NB, 2 * NB), 1)
    return sub, lane


def inverse_root(gram):
    sub, lane = places()
    eye = (sub + NB == lane).astype(jnp.float32)
    work = jnp.concatenate([gram, jnp.zeros_like(gram)], axis=1) + eye
    scales = jnp.zeros((NB, 2 * NB), jnp.float32)
    for step in range(NB):
        row = work[step : step + 1, :]
        pivot = row[:, step : step + 1]
        scales = jnp.where(sub == step, pivot, scales)
        if step + 1 < NB:
            scaled = row * (1.0 / pivot)
            column = jnp.where(sub > step, work[:, step : step + 1], 0.0)
            work = work - column * scaled
    return (work * lax.rsqrt(scales))[:, NB:]


def signed_lu(negated_top):
    sub, lane = places()
    eye = (sub + NB == lane).astype(jnp.float32)
    work = jnp.concatenate([negated_top, jnp.zeros_like(negated_top)], axis=1) + eye
    lower = jnp.zeros((NB, 2 * NB), jnp.float32)
    upper = jnp.zeros((NB, 2 * NB), jnp.float32)
    signs = jnp.zeros((1, 2 * NB), jnp.float32)
    lane_row = lax.broadcasted_iota(jnp.int32, (1, 2 * NB), 1)
    for step in range(NB):
        row = work[step : step + 1, :]
        raw = row[:, step : step + 1]
        flip = jnp.where(raw > 0, 1.0, -1.0)
        signs = jnp.where(lane_row == step, flip, signs)
        pivot = raw + flip
        inverse = 1.0 / pivot
        row = jnp.where(lane_row == step, pivot, row)
        upper = jnp.where((sub == step) & (lane >= step), row, upper)
        column = work[:, step : step + 1]
        lower = jnp.where(
            lane == step, jnp.where(sub > step, column * inverse, jnp.where(sub == step, 1.0, 0.0)), lower
        )
        scaled = row * inverse
        work = jnp.where(sub == step, scaled, work - column * scaled)
    return lower[:, :NB], upper[:, :NB], work[:, NB:], signs[:, :NB]


def near_root(gram):
    sub = lax.broadcasted_iota(jnp.int32, (NB, NB), 0)
    lane = lax.broadcasted_iota(jnp.int32, (NB, NB), 1)
    eye = (sub == lane).astype(jnp.float32)
    off = gram - eye
    first_order = eye - jnp.where(sub > lane, off, jnp.where(sub == lane, 0.5 * off, 0.0))
    close = jnp.sum(off * off) < 2e-8
    return lax.cond(close, lambda: first_order, lambda: inverse_root(gram))


def fold(x, chunk):
    x = x.reshape(-1, chunk, NB)
    return jnp.concatenate([x[:, : chunk // 2], x[:, chunk // 2 :]], axis=2)


def unfold(x):
    return jnp.concatenate([x[:, :, :NB], x[:, :, NB:]], axis=1).reshape(-1, NB)


def pack_symmetric(g):
    h = NB // 2
    rows = []
    for quadrant in (g[:h, :h], g[:h, h:], g[h:, h:]):
        rows.append(jnp.concatenate([quadrant[k : k + 8] for k in range(0, h, 8)], axis=1))
    return jnp.concatenate(rows, axis=0)


def unpack_symmetric(x):
    h = NB // 2
    first, cross, last = [
        jnp.concatenate([x[q : q + 8, k : k + h] for k in range(0, 4 * h, h)], axis=0)
        for q in (0, 8, 16)
    ]
    upper = jnp.concatenate([first, cross], axis=1)
    return jnp.concatenate([upper, jnp.concatenate([cross.T, last], axis=1)], axis=0)


PACKED = 24


def put_pairs(out_ref, pairs):
    peers, rows = out_ref.shape[:2]
    per = NB // peers
    for q, pair in enumerate(pairs):
        for t in range(per):
            out_ref[:, q * per + t, :] = pair[t * peers : (t + 1) * peers]
    for k in range(len(pairs) * per, rows):
        out_ref[:, k, :] = jnp.zeros((peers, 2 * NB), jnp.float32)


def get_pairs(ref, first, count):
    per = NB // ref.shape[0]
    pairs = []
    for q in range(count):
        slots = [ref[:, first + q * per + t, :] for t in range(per)]
        pair = jnp.concatenate(slots, axis=0)
        pairs += [pair[:, :NB], pair[:, NB:]]
    return pairs


def beside(*parts):
    return jnp.concatenate(parts, axis=1)


def below(x, index, start):
    place = lax.broadcasted_iota(jnp.int32, x.shape, 0)
    return jnp.where((place >= start) | (index > 0), x, 0.0)


def plain_start_kernel(chunk, matrix_ref, raw_ref):
    raw_ref[:, :chunk, :] = matrix_ref[:, : 2 * NB].reshape(-1, chunk, 2 * NB)
    raw_ref[:, chunk:, :] = fold(matrix_ref[:, 2 * NB : 3 * NB], chunk)


def start_kernel(chunk, index_ref, matrix_ref, raw_ref, out_ref):
    plain_start_kernel(chunk, matrix_ref, raw_ref)
    panel = below(matrix_ref[:, :NB], index_ref[0], NB)
    packed = pack_symmetric(tn(panel, panel))
    out_ref[...] = jnp.broadcast_to(packed[None], out_ref.shape)


def relay_kernel(raw_ref, got_ref, out_ref):
    block = jnp.concatenate([raw_ref[...], jnp.sum(got_ref[...], axis=0)], axis=0)
    out_ref[...] = jnp.broadcast_to(block[None], out_ref.shape)


def last_raw(raw_ref, chunk):
    return unfold(raw_ref[:, chunk : chunk + chunk // 2, :])


def first_pairs(chunk, index, raw_ref, root, once_ref, small_ref):
    pair = raw_ref[:, :chunk, :].reshape(-1, 2 * NB)
    following = pair[:, NB:]
    once = below(pair[:, :NB], index, NB)
    if root is not None:
        once = nt(once, root)
    once_ref[...] = once
    last = last_raw(raw_ref, chunk)
    gram = tn(once, once)
    image_top = tn(following, once)

    def top(x, k):
        return jnp.where(index == 0, x[k * NB : (k + 1) * NB], 0.0)

    put_pairs(
        small_ref,
        [
            beside(gram, image_top),
            beside(top(once, 1), top(following, 1)),
            beside(top(last, 2), jnp.zeros((NB, NB), jnp.float32)),
        ],
    )


def plain_first_kernel(chunk, index_ref, raw_ref, panel_ref, small_ref):
    first_pairs(chunk, index_ref[0], raw_ref, None, panel_ref, small_ref)


def first_once_kernel(chunk, index_ref, raw_ref, root_ref, once_ref, small_ref):
    root = inverse_root(unpack_symmetric(raw_ref[0, chunk + chunk // 2 :, :]))
    root_ref[...] = root
    first_pairs(chunk, index_ref[0], raw_ref, root, once_ref, small_ref)


def second_pairs(index, once, last, vec, wide, small_ref):
    def top(x):
        return jnp.where(index == 0, x[2 * NB : 3 * NB], 0.0)

    put_pairs(
        small_ref,
        [
            beside(tn(once, once), tn(last, once)),
            beside(tn(vec, once), tn(wide, once)),
            beside(top(once), top(vec)),
            beside(top(wide), jnp.zeros((NB, NB), jnp.float32)),
        ],
    )


def second_once_kernel(
    chunk, index_ref, got_ref, raw_ref, panel_ref, pair_ref, root_ref, once_ref, small_ref
):
    root = inverse_root(unpack_symmetric(jnp.sum(got_ref[...], axis=0)))
    root_ref[...] = root
    once = nt(panel_ref[...], root)
    once_ref[...] = once
    last = last_raw(raw_ref, chunk)
    second_pairs(index_ref[0], once, last, pair_ref[:, :NB], pair_ref[:, NB:], small_ref)


def sum_kernel(got_ref, out_ref, chunk_ref):
    summed = jnp.sum(got_ref[...], axis=0)
    out_ref[...] = jnp.broadcast_to(summed[None], out_ref.shape)
    chunk_ref[...] = summed[: chunk_ref.shape[0]]


def inner_kernel(gathered_ref, once_ref, chunk_ref, out_ref):
    half = chunk_ref.shape[0]
    inner = tn(once_ref[...], unfold(gathered_ref[:, :half, :]))
    block = jnp.concatenate([pack_symmetric(inner), chunk_ref[...]], axis=0)
    out_ref[...] = jnp.broadcast_to(block[None], out_ref.shape)


PICK, COEF, PICK_T, COEF_T, LOWER, FACTOR, INNER, WIDE = range(8)


def factor_small(near, gram, top, next_top, image_top, small_ref):
    root = near_root(gram) if near else inverse_root(gram)
    lower, upper, inverse, signs = signed_lu(-nt(top, root))
    sub = lax.broadcasted_iota(jnp.int32, (NB, NB), 0)
    lane = lax.broadcasted_iota(jnp.int32, (NB, NB), 1)
    triangle = lane >= sub
    upper_inverse = jnp.where(triangle, nn(inverse, lower), 0.0)
    lower_inverse = nn(upper, inverse)
    factor = jnp.where(triangle, nt(upper * signs, lower_inverse), 0.0)
    pick = nn(jnp.where(sub == lane, signs, 0.0), upper_inverse)
    coef = tn(root, upper_inverse)
    crossed = tn(pick, nn(image_top, coef))
    pick_t = nn(pick, factor)
    coef_t = nn(coef, factor)
    small_ref[PICK] = pick
    small_ref[COEF] = coef
    small_ref[PICK_T] = pick_t
    small_ref[COEF_T] = coef_t
    small_ref[LOWER] = lower
    small_ref[FACTOR] = factor
    small_ref[INNER] = tn(pick, nn(next_top, pick)) - crossed - crossed.T
    small_ref[WIDE] = nn(next_top, pick_t) - nn(image_top, coef_t)
    sizes = jnp.sum(jnp.where(sub == lane, gram, 0.0), axis=0, keepdims=True)
    fine = jnp.sum(root * root * sizes) < 1.5 * NB
    return pick, coef, pick_t, coef_t, fine


def vectors_of(once, index, start, pick, coef):
    vec = -nn(once, coef)
    top = vec[start : start + NB] + jnp.where(index == 0, pick, 0.0)
    return jnp.concatenate([vec[:start], top, vec[start + NB :]], axis=0)


def half_core(small_ref, inner):
    coef = small_ref[COEF]
    factor = small_ref[FACTOR]
    inner = small_ref[INNER] + tn(coef, nn(inner, coef))
    return 0.5 * tn(factor, nn(inner, factor))


def first_factor_kernel(
    near, chunk, half, row_ref, col_ref, gathered_ref, raw_ref, once_c_ref, once_r_ref,
    small_ref, state_ref, vec_ref, factor_ref, fine_ref,
):
    gram, image_top, top, next_top, _, _ = get_pairs(gathered_ref, half, 3)
    pick, coef, pick_t, coef_t, fine = factor_small(
        near, gram, top, next_top, image_top, small_ref
    )
    fine_ref[0] = jnp.where(fine, 1, 0)
    factor_ref[...] = small_ref[FACTOR]
    vec_ref[...] = vectors_of(once_r_ref[...], row_ref[0], NB, pick, coef)
    following = raw_ref[:, :chunk, :].reshape(-1, 2 * NB)[:, NB:]
    image = unfold(gathered_ref[:, :half, :])
    vec = vectors_of(once_c_ref[...], col_ref[0], NB, pick, coef)
    state_ref[...] = beside(vec, nn(following, pick_t) - nn(image, coef_t))


def second_panel(following, vec, wide, wide_top, lower, index):
    return below(following - nt(vec, wide_top) - nt(wide, lower), index, 2 * NB)


def first_cols(chunk, index, got_ref, small_ref, state_ref, raw_ref, pair_ref, panel_ref, tops_ref):
    half = half_core(small_ref, unpack_symmetric(jnp.sum(got_ref[:, :PACKED, :], axis=0)))
    lower = small_ref[LOWER]
    wide_top = small_ref[WIDE] - nn(lower, half)
    tops_ref[0] = half
    tops_ref[1] = wide_top
    vec = state_ref[:, :NB]
    wide = state_ref[:, NB:] - nn(vec, half)
    pair_ref[...] = beside(wide, vec)
    following = raw_ref[:, :chunk, :].reshape(-1, 2 * NB)[:, NB:]
    panel = second_panel(following, vec, wide, wide_top, lower, index)
    panel_ref[...] = panel
    return panel, vec, wide


def first_cols_kernel(
    chunk, col_ref, got_ref, small_ref, state_ref, raw_ref, pair_ref, panel_ref, tops_ref, out_ref
):
    panel, _, _ = first_cols(
        chunk, col_ref[0], got_ref, small_ref, state_ref, raw_ref, pair_ref, panel_ref, tops_ref
    )
    packed = pack_symmetric(tn(panel, panel))
    out_ref[...] = jnp.broadcast_to(packed[None], out_ref.shape)


def plain_cols_kernel(
    chunk, col_ref, got_ref, small_ref, state_ref, raw_ref, pair_ref, panel_ref, tops_ref, out_ref
):
    panel, vec, wide = first_cols(
        chunk, col_ref[0], got_ref, small_ref, state_ref, raw_ref, pair_ref, panel_ref, tops_ref
    )
    second_pairs(col_ref[0], panel, last_raw(raw_ref, chunk), vec, wide, out_ref)


def first_rows_kernel(
    chunk, row_ref, got_ref, small_ref, vec_ref, raw_ref, tops_ref, pair_ref, panel_ref
):
    image = unfold(got_ref[:, PACKED:, :])
    following = raw_ref[:, :chunk, :].reshape(-1, 2 * NB)[:, NB:]
    vec = vec_ref[...]
    wide = nn(following, small_ref[PICK_T]) - nn(image, small_ref[COEF_T]) - nn(vec, tops_ref[0])
    pair_ref[...] = beside(vec, wide)
    panel_ref[...] = second_panel(following, vec, wide, tops_ref[1], small_ref[LOWER], row_ref[0])


def second_small(near, half, old_half, gathered_ref, old_ref, factor_ref, small_ref, factors_ref):
    gram, image_top, vec_dot, wide_dot, top, vec_top, wide_top, _ = get_pairs(
        gathered_ref, half, 4
    )
    last_top = get_pairs(old_ref, old_half, 3)[4]
    image_top = image_top - nn(vec_top, wide_dot) - nn(wide_top, vec_dot)
    crossed = nt(vec_top, wide_top)
    next_top = last_top - crossed - crossed.T
    pick, coef, pick_t, coef_t, fine = factor_small(
        near, gram, top, next_top, image_top, small_ref
    )
    crossed = tn(nn(vec_dot, coef), nn(wide_dot, coef))
    small_ref[INNER] -= crossed + crossed.T
    factors_ref[0] = factor_ref[...]
    factors_ref[1] = small_ref[FACTOR]
    vec_dots = nn(wide_dot, coef_t) - tn(wide_top, pick_t)
    wide_dots = nn(vec_dot, coef_t) - tn(vec_top, pick_t)
    return pick, coef, pick_t, coef_t, vec_dots, wide_dots, fine


def second_factor_kernel(
    chunk, half, row_ref, col_ref, gathered_ref, old_ref, raw_c_ref, raw_r_ref,
    once_c_ref, once_r_ref, pair_c_ref, pair_r_ref, factor_ref,
    small_ref, right_ref, state_ref, vectors_ref, factors_ref,
):
    pick, coef, pick_t, coef_t, vec_dots, wide_dots, _ = second_small(
        True, half, half, gathered_ref, old_ref, factor_ref, small_ref, factors_ref
    )
    new = vectors_of(once_r_ref[...], row_ref[0], 2 * NB, pick, coef)
    vec = pair_r_ref[:, :NB]
    vectors_ref[0] = vec
    vectors_ref[1] = new
    part = nn(last_raw(raw_r_ref, chunk), pick_t)
    part += nn(vec, vec_dots) + nn(pair_r_ref[:, NB:], wide_dots)
    state_ref[...] = beside(new, part)
    new = vectors_of(once_c_ref[...], col_ref[0], 2 * NB, pick, coef)
    part = nn(last_raw(raw_c_ref, chunk), pick_t) - nn(unfold(gathered_ref[:, :half, :]), coef_t)
    part += nn(pair_c_ref[:, NB:], vec_dots) + nn(pair_c_ref[:, :NB], wide_dots)
    right_ref[...] = beside(part, new)


def plain_second_kernel(
    chunk, half, row_ref, col_ref, gathered_ref, old_ref, raw_c_ref, raw_r_ref,
    panel_c_ref, panel_r_ref, pair_c_ref, pair_r_ref, factor_ref,
    small_ref, state_ref, left_ref, vectors_ref, factors_ref, fine_ref,
):
    pick, coef, pick_t, coef_t, vec_dots, wide_dots, fine = second_small(
        False, half, half, gathered_ref, old_ref, factor_ref, small_ref, factors_ref
    )
    fine_ref[0] = jnp.where(fine, 1, 0)
    new = vectors_of(panel_r_ref[...], row_ref[0], 2 * NB, pick, coef)
    vec = pair_r_ref[:, :NB]
    vectors_ref[0] = vec
    vectors_ref[1] = new
    part = nn(last_raw(raw_r_ref, chunk), pick_t) - nn(unfold(gathered_ref[:, :half, :]), coef_t)
    part += nn(vec, vec_dots) + nn(pair_r_ref[:, NB:], wide_dots)
    left_ref[...] = beside(part, new)
    new = vectors_of(panel_c_ref[...], col_ref[0], 2 * NB, pick, coef)
    part = nn(last_raw(raw_c_ref, chunk), pick_t)
    part += nn(pair_c_ref[:, NB:], vec_dots) + nn(pair_c_ref[:, :NB], wide_dots)
    state_ref[...] = beside(new, part)


def last_kernel(got_ref, small_ref, state_ref, out_ref):
    half = half_core(small_ref, unpack_symmetric(jnp.sum(got_ref[:, :PACKED, :], axis=0)))
    new = state_ref[:, :NB]
    image = unfold(got_ref[:, PACKED:, :])
    wide = state_ref[:, NB:] - nn(image, small_ref[COEF_T]) - nn(new, half + half.T)
    out_ref[...] = beside(new, wide)


def call(kernel, name, outs, *args, statics=(), scalars=0, flag=False):
    in_smem = pl.BlockSpec(memory_space=pltpu.SMEM)
    in_vmem = pl.BlockSpec(memory_space=pltpu.VMEM)
    out_shape = [jax.ShapeDtypeStruct(shape, jnp.float32) for shape in outs]
    out_specs = [in_vmem] * len(outs)
    if flag:
        out_shape.append(jax.ShapeDtypeStruct((1,), jnp.int32))
        out_specs.append(in_smem)
    result = pl.pallas_call(
        functools.partial(kernel, *statics),
        out_shape=out_shape,
        in_specs=[in_smem if k < scalars else in_vmem for k in range(len(args))],
        out_specs=out_specs,
        compiler_params=pltpu.CompilerParams(vmem_limit_bytes=16 << 20),
        cost_estimate=pl.CostEstimate(flops=1 << 24, bytes_accessed=1 << 22, transcendentals=0),
        name=name,
    )(*args)
    return result[0] if len(result) == 1 else result


def swap(x, axis):
    return lax.all_to_all(x, axis, 0, 0)


def solution(mesh):
    nr = mesh.shape["row"]
    nc = mesh.shape["col"]

    def local(matrix):
        rows_here, cols_here = matrix.shape
        chunk = rows_here // nc
        half = chunk // 2
        my_row = lax.axis_index("row").astype(jnp.int32).reshape(1)
        my_col = lax.axis_index("col").astype(jnp.int32).reshape(1)
        col_place = (lax.axis_index("col") * cols_here + jnp.arange(cols_here))[:, None]
        to_rows = []
        for r in range(nr):
            for c in range(nc):
                first = r * rows_here + c * chunk
                source = (first % cols_here // chunk) * nc + first // cols_here
                to_rows.append((source, r * nc + c))
        to_cols = [(b, a) for a, b in to_rows]
        square = (NB, NB)
        tall_r = (rows_here, NB)
        tall_c = (cols_here, NB)
        pair_shape_c = (cols_here, 2 * NB)
        pair_shape_r = (rows_here, 2 * NB)
        raw_rows = chunk + half

        def few(peers):
            return -(-4 * (NB // peers) // 8) * 8

        def image_round(partial_image, smalls, axis, targets, ready):
            mine = jnp.concatenate([fold(partial_image, chunk), smalls], axis=1)
            got, ready = lax.optimization_barrier((swap(mine, axis), ready))
            blocks, image_chunk = call(sum_kernel, "sum_blocks", [got.shape, (half, 2 * NB)], got)
            other = lax.ppermute(image_chunk, ("row", "col"), targets)
            return swap(blocks, axis), other, ready

        def spread_columns(raw_c):
            return swap(jnp.broadcast_to(raw_c[None], (nr, raw_rows, 2 * NB)), "row")

        def first_columns(raw_c):
            first_c = raw_c[:, :chunk].reshape(cols_here, 2 * NB)[:, :NB]
            return jnp.where(col_place >= NB, first_c, 0.0)

        block_r = (nc, PACKED + half, 2 * NB)
        block_c = (nr, PACKED + half, 2 * NB)

        def plain():
            raw = call(
                plain_start_kernel, "plain_start", [(nc, raw_rows, 2 * NB)],
                matrix[:, : 4 * NB], statics=(chunk,),
            )
            raw_chunk = swap(raw, "col")[0]
            raw_chunk_c = lax.ppermute(raw_chunk, ("row", "col"), to_cols)
            raw_r = swap(jnp.broadcast_to(raw_chunk[None], raw.shape), "col")
            raw_c = spread_columns(raw_chunk_c)
            first_r, smalls = call(
                plain_first_kernel, "plain_first", [tall_r, (nr, few(nr), 2 * NB)],
                my_row, raw_r, statics=(chunk,), scalars=1,
            )
            gathered, image_chunk, raw_c = image_round(
                tn(matrix, first_r), smalls, "row", to_rows, raw_c
            )
            first_c = first_columns(raw_c)
            inners = call(inner_kernel, "inner", [block_r], gathered, first_c, image_chunk)
            got = swap(inners, "col")
            small_one, state_c, vec_r, factor_one, fine_one = call(
                first_factor_kernel, "plain_factor", [(8,) + square, pair_shape_c, tall_r, square],
                my_row, my_col, gathered, raw_c, first_c, first_r,
                statics=(False, chunk, half), scalars=2, flag=True,
            )
            pair_c, panel_c, tops, smalls = call(
                plain_cols_kernel, "plain_cols",
                [pair_shape_c, tall_c, (2,) + square, (nc, few(nc), 2 * NB)],
                my_col, got, small_one, state_c, raw_c, statics=(chunk,), scalars=1,
            )
            pair_r, panel_r = call(
                first_rows_kernel, "first_rows", [pair_shape_r, tall_r],
                my_row, got, small_one, vec_r, raw_r, tops, statics=(chunk,), scalars=1,
            )
            old = gathered
            gathered, image_chunk, _ = image_round(
                nn(matrix, panel_c), smalls, "col", to_cols, my_row
            )
            current = matrix - nt(pair_r, pair_c)
            gathered, current = lax.optimization_barrier((gathered, current))
            inners = call(inner_kernel, "inner", [block_c], gathered, panel_r, image_chunk)
            got = swap(inners, "row")
            small_two, state_c, left, vectors, factors, fine_two = call(
                plain_second_kernel, "plain_second",
                [(8,) + square, pair_shape_c, pair_shape_r, (2,) + tall_r, (2,) + square],
                my_row, my_col, gathered, old, raw_c, raw_r, panel_c, panel_r,
                pair_c, pair_r, factor_one, statics=(chunk, half), scalars=2, flag=True,
            )
            right = call(last_kernel, "last", [pair_shape_c], got, small_two, state_c)
            return (current, left, right, vectors, factors), (fine_one + fine_two)[0] == 2

        def careful():
            raw, grams = call(
                start_kernel, "start", [(nc, raw_rows, 2 * NB), (nr, PACKED, 2 * NB)],
                my_row, matrix[:, : 4 * NB], statics=(chunk,), scalars=1,
            )
            raw_chunk = swap(raw, "col")[0]
            raw_chunk_c = lax.ppermute(raw_chunk, ("row", "col"), to_cols)
            raw_r = call(
                relay_kernel, "relay", [(nc, raw_rows + PACKED, 2 * NB)], raw_chunk, swap(grams, "row")
            )
            raw_r = swap(raw_r, "col")
            raw_c = spread_columns(raw_chunk_c)

            root, once_r, smalls = call(
                first_once_kernel, "first_once", [square, tall_r, (nr, few(nr), 2 * NB)],
                my_row, raw_r, statics=(chunk,), scalars=1,
            )

            gathered, image_chunk_r, raw_c = image_round(
                tn(matrix, once_r), smalls, "row", to_rows, raw_c
            )
            once_c = nt(first_columns(raw_c), root)
            inners = call(inner_kernel, "inner", [block_r], gathered, once_c, image_chunk_r)
            got = swap(inners, "col")
            small_one, state_c, vec_r, factor_one, _ = call(
                first_factor_kernel, "first_factor", [(8,) + square, pair_shape_c, tall_r, square],
                my_row, my_col, gathered, raw_c, once_c, once_r,
                statics=(True, chunk, half), scalars=2, flag=True,
            )
            pair_c, panel_c, tops, grams = call(
                first_cols_kernel, "first_cols",
                [pair_shape_c, tall_c, (2,) + square, (nc, PACKED, 2 * NB)],
                my_col, got, small_one, state_c, raw_c, statics=(chunk,), scalars=1,
            )
            grams = swap(grams, "col")
            pair_r, panel_r = call(
                first_rows_kernel, "first_rows", [pair_shape_r, tall_r],
                my_row, got, small_one, vec_r, raw_r, tops, statics=(chunk,), scalars=1,
            )

            root, once_r, smalls = call(
                second_once_kernel, "second_once", [square, tall_r, (nr, few(nr), 2 * NB)],
                my_row, grams, raw_r, panel_r, pair_r, statics=(chunk,), scalars=1,
            )
            old = gathered
            gathered, image_chunk_r, _ = image_round(
                tn(matrix, once_r), smalls, "row", to_rows, my_row
            )
            once_c = nt(panel_c, root)
            current = matrix - nt(pair_r, pair_c)
            inners = call(inner_kernel, "inner", [block_r], gathered, once_c, image_chunk_r)
            got = swap(inners, "col")
            small_two, right, state_r, vectors, factors = call(
                second_factor_kernel, "second_factor",
                [(8,) + square, pair_shape_c, pair_shape_r, (2,) + tall_r, (2,) + square],
                my_row, my_col, gathered, old, raw_c, raw_r, once_c, once_r, pair_c, pair_r, factor_one,
                statics=(chunk, half), scalars=2,
            )
            left = call(last_kernel, "last", [pair_shape_r], got, small_two, state_r)
            return current - nt(left, right), vectors, factors

        ready, fine = plain()

        def finish(current, left, right, vectors, factors):
            return current - nt(left, right), vectors, factors

        return lax.cond(fine, finish, lambda *_: careful(), *ready)

    return jax.shard_map(
        local,
        mesh=mesh,
        in_specs=(P("row", "col"),),
        out_specs=(P("row", "col"), P(None, "row", None), P()),
        check_vma=False,
    )
```

profile of v0, /device:TPU:1, one launch (start us, length us, event | category | flops | bytes accessed | tf_op | source)
XLA Modules:
  0.0 513.6 jit_solution(1187374879210508068)
XLA Ops:
  1.8 26.2 %all_to_all.92 = f32[16,48,128]{2,1,0:T(8,128)S(1)} all-to-all(f32[16,48,128]{2,1,0:T(8,128)S(1)} %plain_start.1), channel_id=1, replica_groups=mesh['row'=32,'col'=16] {'col'}, dimensions={0} | all-to-all | bytes 786432 | tf_op jit(solution)/shard_map/all_to_all | solution.py:444
  28.8 3.5 all-to-all-start.12
  32.2 14.0 %all-to-all-done.12.raw_ref.raw_r_ref = f32[16,48,128]{2,1,0:T(8,128)S(1)} async-done(((f32[16,48,128]{2,1,0:T(8,128)}), f32[16,48,128]{2,1,0:T(8,128)S(1)}, u32[]{:S(2)}, u32[]{:S(2)}) %all-to-all-start.12) | async-done | bytes 393248 | tf_op jit(solution)/shard_map/all_to_all | solution.py:444
  51.0 9.7 %all-to-all-start.13 = ((f32[32,24,128]{2,1,0:T(8,128)}), f32[32,24,128]{2,1,0:T(8,128)S(1)}, u32[]{:S(2)}, u32[]{:S(2)}) async-start(f32[32,24,128]{2,1,0:T(8,128)} %pad_maximum_fusion.2), calls=%async_computation.13 | async-start | bytes 786432 | tf_op jit(solution)/shard_map/all_to_all | solution.py:444
  63.5 9.4 %collective-permute-done.3 = f32[48,128]{1,0:T(8,128)S(1)} collective-permute-done((f32[48,128]{1,0:T(8,128)S(1)}, f32[48,128]{1,0:T(8,128)S(1)}, u32[]{:S(2)}, u32[]{:S(2)}) %collective-permute-start.3) | collective-permute-done | bytes 24608 | tf_op jit(solution)/shard_map/ppermute | solution.py:498
  75.6 24.2 %all_to_all.93.raw_ref.raw_c_ref = f32[32,48,128]{2,1,0:T(8,128)S(1)} all-to-all(f32[32,48,128]{2,1,0:T(8,128)S(1)} %broadcast_in_dim.44), channel_id=1, replica_groups=mesh['row'=32,'col'=16] {'row'}, dimensions={0} | all-to-all | bytes 1572864 | tf_op jit(solution)/shard_map/all_to_all | solution.py:444
  100.7 7.3 %all-to-all-start.15 = ((f32[32,24,128]{2,1,0:T(8,128)}), f32[32,24,128]{2,1,0:T(8,128)S(1)}, u32[]{:S(2)}, u32[]{:S(2)}) async-start(f32[32,24,128]{2,1,0:T(8,128)} %get-tuple-element.91), calls=%async_computation.15 | async-start | bytes 786432 | tf_op jit(solution)/shard_map/all_to_all | solution.py:444
  108.0 7.3 %collective-permute-start.4 = (f32[16,128]{1,0:T(8,128)S(1)}, f32[16,128]{1,0:T(8,128)S(1)}, u32[]{:S(2)}, u32[]{:S(2)}) collective-permute-start(f32[16,128]{1,0:T(8,128)S(1)} %get-tuple-element.94), channel_id=1, source_target_pairs={{0,0},{16,1},{32,2},{48,3},{64,4},{80,5},{96,6},{112,7},{128,8},{1... | collective-permute-start | bytes 24584 | tf_op jit(solution)/shard_map/ppermute | solution.py:479
  119.8 11.9 %all-to-all-start.16 = ((f32[16,40,128]{2,1,0:T(8,128)}), f32[16,40,128]{2,1,0:T(8,128)S(1)}, u32[]{:S(2)}, u32[]{:S(2)}) async-start(f32[16,40,128]{2,1,0:T(8,128)} %inner.6), calls=%async_computation.16 | async-start | bytes 655360 | tf_op jit(solution)/shard_map/all_to_all | solution.py:444
  131.7 14.0 %plain_factor.1 = (f32[8,64,64]{2,1,0:T(8,128)S(1)}, f32[1024,128]{1,0:T(8,128)S(1)}, f32[512,64]{1,0:T(8,128)S(1)}, f32[64,64]{1,0:T(8,128)S(1)}, s32[1]{0:T(128)}) custom-call(s32[1]{0:T(128)} %bitcast.6.index_ref.row_ref, s32[1]{0:T(128)} %bitcast.7.col_ref, f32[32,24,128]{2,1,0:T(8,128)S(1)} %all-to-all-done.15.gathered_ref.old_ref, ...), custom_call_target="tpu_custom_call" | custom-call | flops 16777216 | bytes 4194304 | tf_op jit(solution)/shard_map/plain_factor/pallas_call | solution.py:431
  148.2 4.7 plain_cols.1
  153.5 4.6 convolution_bitcast_fusion.3
  161.9 18.7 %all_to_all.94.got_ref = f32[16,32,128]{2,1,0:T(8,128)S(1)} all-to-all(f32[16,32,128]{2,1,0:T(8,128)S(1)} %pad_maximum_fusion.3), channel_id=1, replica_groups=mesh['row'=32,'col'=16] {'col'}, dimensions={0} | all-to-all | bytes 524288 | tf_op jit(solution)/shard_map/all_to_all | solution.py:444
  181.4 3.8 all-to-all-start.18
  186.6 3.7 collective-permute-start.5
  190.3 4.7 convolution_subtract_fusion.1
  197.6 12.7 %all-to-all-start.19 = ((f32[32,40,128]{2,1,0:T(8,128)}), f32[32,40,128]{2,1,0:T(8,128)S(1)}, u32[]{:S(2)}, u32[]{:S(2)}) async-start(f32[32,40,128]{2,1,0:T(8,128)} %inner.7), calls=%async_computation.19 | async-start | bytes 1310720 | tf_op jit(solution)/shard_map/all_to_all | solution.py:444
  213.4 16.3 %plain_second.1 = (f32[8,64,64]{2,1,0:T(8,128)S(1)}, f32[1024,128]{1,0:T(8,128)S(1)}, f32[512,128]{1,0:T(8,128)}, f32[2,512,64]{2,1,0:T(8,128)}, f32[2,64,64]{2,1,0:T(8,128)}, /*index=5*/s32[1]{0:T(128)}) custom-call(s32[1]{0:T(128)} %bitcast.6.index_ref.row_ref, s32[1]{0:T(128)} %bitcast.7.col_ref, f32[16,32,128]{2,1,0:T(8,128)S(1)} %all-to-all-done.18.gathered_ref, ...), custom_call_target="tpu_custom_call" | custom-call | flops 16777216 | bytes 4194304 | tf_op jit(solution)/shard_map/plain_second/pallas_call | solution.py:431
  237.3 273.8 %conditional.1 = (f32[2,512,64]{2,1,0:T(8,128)}, f32[2,64,64]{2,1,0:T(8,128)}, f32[512,1024]{1,0:T(8,128)S(1)}) conditional(s32[]{:T(128)} %bitcast.14, (f32[512,1024]{1,0:T(8,128)}, s32[1]{0:T(128)}, s32[]{:T(128)}, s32[1]{0:T(128)}, s32[1024,1]{0,1:T(1,128)S(1)}) %tuple.23, (f32[512,128]{1,0:T(8,128)}, f32[1024,128]{1,0:T(8,128)}, ...), branch_computations={%region_0.1_spmd, %region_1.2_spmd} | conditional | flops 2736195584 | bytes 105921392 | solution.py:608
  239.6 22.0 %all_to_all.89 = f32[16,48,128]{2,1,0:T(8,128)S(1)} all-to-all(f32[16,48,128]{2,1,0:T(8,128)S(1)} %get-tuple-element.20), channel_id=1, replica_groups=mesh['row'=32,'col'=16] {'col'}, dimensions={0} | all-to-all | bytes 786432 | tf_op jit(solution)/shard_map/cond/branch_0_fun/all_to_all | solution.py:444
  261.7 9.6 %all-to-all-start.1 = ((f32[32,24,128]{2,1,0:T(8,128)}), f32[32,24,128]{2,1,0:T(8,128)S(1)}, u32[]{:S(2)}, u32[]{:S(2)}) async-start(f32[32,24,128]{2,1,0:T(8,128)} %get-tuple-element.21), calls=%async_computation.1 | async-start | bytes 786432 | tf_op jit(solution)/shard_map/cond/branch_0_fun/all_to_all | solution.py:444
  271.3 14.9 %all-to-all-done.1.got_ref = f32[32,24,128]{2,1,0:T(8,128)S(1)} async-done(((f32[32,24,128]{2,1,0:T(8,128)}), f32[32,24,128]{2,1,0:T(8,128)S(1)}, u32[]{:S(2)}, u32[]{:S(2)}) %all-to-all-start.1) | async-done | bytes 393248 | tf_op jit(solution)/shard_map/cond/branch_0_fun/all_to_all | solution.py:444
  287.1 3.8 all-to-all-start.2
  290.9 3.7 collective-permute-start
  297.4 12.9 %all-to-all-done.2.raw_ref.raw_r_ref = f32[16,72,128]{2,1,0:T(8,128)S(1)} async-done(((f32[16,72,128]{2,1,0:T(8,128)}), f32[16,72,128]{2,1,0:T(8,128)S(1)}, u32[]{:S(2)}, u32[]{:S(2)}) %all-to-all-start.2) | async-done | bytes 589856 | tf_op jit(solution)/shard_map/cond/branch_0_fun/all_to_all | solution.py:444
  311.2 6.0 %all-to-all-start.4 = ((f32[32,48,128]{2,1,0:T(8,128)}), f32[32,48,128]{2,1,0:T(8,128)S(1)}, u32[]{:S(2)}, u32[]{:S(2)}) async-start(f32[32,48,128]{2,1,0:T(8,128)} %broadcast_in_dim.33), calls=%async_computation.4 | async-start | bytes 1572864 | tf_op jit(solution)/shard_map/cond/branch_0_fun/all_to_all | solution.py:444
  317.3 6.7 %first_once.1 = (f32[64,64]{1,0:T(8,128)S(1)}, f32[512,64]{1,0:T(8,128)S(1)}, f32[32,8,128]{2,1,0:T(8,128)S(1)}) custom-call(s32[1]{0:T(128)} %get-tuple-element.19.index_ref.row_ref, f32[16,72,128]{2,1,0:T(8,128)S(1)} %all-to-all-done.2.raw_ref.raw_r_ref), custom_call_target="tpu_custom_call" | custom-call | flops 16777216 | bytes 4194304 | tf_op jit(solution)/shard_map/cond/branch_0_fun/first_once/pallas_call | solution.py:431
  324.0 3.0 convolution_bitcast_fusion.1
  327.4 9.7 %all-to-all-done.4.raw_ref.raw_c_ref = f32[32,48,128]{2,1,0:T(8,128)S(1)} async-done(((f32[32,48,128]{2,1,0:T(8,128)}), f32[32,48,128]{2,1,0:T(8,128)S(1)}, u32[]{:S(2)}, u32[]{:S(2)}) %all-to-all-start.4) | async-done | bytes 786464 | tf_op jit(solution)/shard_map/cond/branch_0_fun/all_to_all | solution.py:444
  337.1 18.2 %all_to_all.90.got_ref = f32[32,24,128]{2,1,0:T(8,128)S(1)} all-to-all(f32[32,24,128]{2,1,0:T(8,128)S(1)} %pad_maximum_fusion), channel_id=1, replica_groups=mesh['row'=32,'col'=16] {'row'}, dimensions={0} | all-to-all | bytes 786432 | tf_op jit(solution)/shard_map/cond/branch_0_fun/all_to_all | solution.py:444
  356.1 7.5 %all-to-all-start.5 = ((f32[32,24,128]{2,1,0:T(8,128)}), f32[32,24,128]{2,1,0:T(8,128)S(1)}, u32[]{:S(2)}, u32[]{:S(2)}) async-start(f32[32,24,128]{2,1,0:T(8,128)} %get-tuple-element.25), calls=%async_computation.5 | async-start | bytes 786432 | tf_op jit(solution)/shard_map/cond/branch_0_fun/all_to_all | solution.py:444
  363.6 6.6 %collective-permute-start.1 = (f32[16,128]{1,0:T(8,128)S(1)}, f32[16,128]{1,0:T(8,128)S(1)}, u32[]{:S(2)}, u32[]{:S(2)}) collective-permute-start(f32[16,128]{1,0:T(8,128)S(1)} %get-tuple-element.29), channel_id=1, source_target_pairs={{0,0},{16,1},{32,2},{48,3},{64,4},{80,5},{96,6},{112,7},{128,8},{1... | collective-permute-start | bytes 24584 | tf_op jit(solution)/shard_map/cond/branch_0_fun/ppermute | solution.py:479
  371.0 3.9 collective-permute-done.1.chunk_ref
  376.2 9.9 %all-to-all-start.6 = ((f32[16,40,128]{2,1,0:T(8,128)}), f32[16,40,128]{2,1,0:T(8,128)S(1)}, u32[]{:S(2)}, u32[]{:S(2)}) async-start(f32[16,40,128]{2,1,0:T(8,128)} %inner.4), calls=%async_computation.6 | async-start | bytes 655360 | tf_op jit(solution)/shard_map/cond/branch_0_fun/all_to_all | solution.py:444
  386.1 9.4 %first_factor.1 = (f32[8,64,64]{2,1,0:T(8,128)S(1)}, f32[1024,128]{1,0:T(8,128)S(1)}, f32[512,64]{1,0:T(8,128)S(1)}, f32[64,64]{1,0:T(8,128)S(1)}, s32[1]{0:T(128)}) custom-call(s32[1]{0:T(128)} %get-tuple-element.19.index_ref.row_ref, s32[1]{0:T(128)} %get-tuple-element.30.col_ref, f32[32,24,128]{2,1,0:T(8,128)S(1)} %all-to-all-done.5.gathered_ref.old_ref, ...), custom_call_target="tpu_custom_call" | custom-call | flops 16777216 | bytes 4194304 | tf_op jit(solution)/shard_map/cond/branch_0_fun/first_factor/pallas_call | solution.py:431
  400.2 3.6 first_cols.1
  405.3 4.8 all-to-all-start.7
  413.2 7.1 %all-to-all-done.7.got_ref = f32[16,24,128]{2,1,0:T(8,128)S(1)} async-done(((f32[16,24,128]{2,1,0:T(8,128)}), f32[16,24,128]{2,1,0:T(8,128)S(1)}, u32[]{:S(2)}, u32[]{:S(2)}) %all-to-all-start.7) | async-done | bytes 196640 | tf_op jit(solution)/shard_map/cond/branch_0_fun/all_to_all | solution.py:444
  421.2 6.9 %second_once.1 = (f32[64,64]{1,0:T(8,128)S(1)}, f32[512,64]{1,0:T(8,128)S(1)}, f32[32,8,128]{2,1,0:T(8,128)S(1)}) custom-call(s32[1]{0:T(128)} %get-tuple-element.19.index_ref.row_ref, f32[16,24,128]{2,1,0:T(8,128)S(1)} %all-to-all-done.7.got_ref, f32[16,72,128]{2,1,0:T(8,128)S(1)} %all-to-all-done.2.raw_ref.raw_r_ref, f32[512,64]{1,0:T(8,128)S(1)} %copy-done.24, ...), custom_call_target="tpu_custom_call" | custom-call | flops 16777216 | bytes 4194304 | tf_op jit(solution)/shard_map/cond/branch_0_fun/second_once/pallas_call | solution.py:431
  428.1 3.0 convolution_bitcast_fusion
  432.2 22.9 %all_to_all.91.got_ref = f32[32,24,128]{2,1,0:T(8,128)S(1)} all-to-all(f32[32,24,128]{2,1,0:T(8,128)S(1)} %pad_maximum_fusion.1), channel_id=1, replica_groups=mesh['row'=32,'col'=16] {'row'}, dimensions={0} | all-to-all | bytes 786432 | tf_op jit(solution)/shard_map/cond/branch_0_fun/all_to_all | solution.py:444
  456.0 6.4 %all-to-all-start.9 = ((f32[32,24,128]{2,1,0:T(8,128)}), f32[32,24,128]{2,1,0:T(8,128)S(1)}, u32[]{:S(2)}, u32[]{:S(2)}) async-start(f32[32,24,128]{2,1,0:T(8,128)} %get-tuple-element.42), calls=%async_computation.9 | async-start | bytes 786432 | tf_op jit(solution)/shard_map/cond/branch_0_fun/all_to_all | solution.py:444
  462.4 5.2 %collective-permute-start.2 = (f32[16,128]{1,0:T(8,128)S(1)}, f32[16,128]{1,0:T(8,128)S(1)}, u32[]{:S(2)}, u32[]{:S(2)}) collective-permute-start(f32[16,128]{1,0:T(8,128)S(1)} %get-tuple-element.45), channel_id=1, source_target_pairs={{0,0},{16,1},{32,2},{48,3},{64,4},{80,5},{96,6},{112,7},{128,8},{1... | collective-permute-start | bytes 24584 | tf_op jit(solution)/shard_map/cond/branch_0_fun/ppermute | solution.py:479
  469.3 4.4 collective-permute-done.2.chunk_ref
  475.2 9.8 %all-to-all-start.10 = ((f32[16,40,128]{2,1,0:T(8,128)}), f32[16,40,128]{2,1,0:T(8,128)}, u32[]{:S(2)}, u32[]{:S(2)}) async-start(f32[16,40,128]{2,1,0:T(8,128)} %copy-done.2), calls=%async_computation.10 | async-start | bytes 655360 | tf_op jit(solution)/shard_map/cond/branch_0_fun/all_to_all | solution.py:444
  484.9 3.1 fusion.9
  488.0 11.9 %second_factor.1 = (f32[8,64,64]{2,1,0:T(8,128)S(1)}, f32[1024,128]{1,0:T(8,128)S(1)}, f32[512,128]{1,0:T(8,128)S(1)}, f32[2,512,64]{2,1,0:T(8,128)}, f32[2,64,64]{2,1,0:T(8,128)}) custom-call(s32[1]{0:T(128)} %get-tuple-element.19.index_ref.row_ref, s32[1]{0:T(128)} %get-tuple-element.30.col_ref, f32[32,24,128]{2,1,0:T(8,128)S(1)} %all-to-all-done.9.gathered_ref, ...), custom_call_target="tpu_custom_call" | custom-call | flops 16777216 | bytes 4194304 | tf_op jit(solution)/shard_map/cond/branch_0_fun/second_factor/pallas_call | solution.py:431
  506.7 4.3 subtract_subtract_fusion
  (122 shorter events, 72.8 us)
Async XLA Ops:
  28.8 17.4 %all-to-all-start.12 = ((f32[16,48,128]{2,1,0:T(8,128)}), f32[16,48,128]{2,1,0:T(8,128)S(1)}, u32[]{:S(2)}, u32[]{:S(2)}) async-start(f32[16,48,128]{2,1,0:T(8,128)} %broadcast_in_dim.43), calls=%async_computation.12 | async-start | bytes 786432 | tf_op jit(solution)/shard_map/all_to_all | solution.py:444
  51.0 24.6 %all-to-all-start.13 = ((f32[32,24,128]{2,1,0:T(8,128)}), f32[32,24,128]{2,1,0:T(8,128)S(1)}, u32[]{:S(2)}, u32[]{:S(2)}) async-start(f32[32,24,128]{2,1,0:T(8,128)} %pad_maximum_fusion.2), calls=%async_computation.13 | async-start | bytes 786432 | tf_op jit(solution)/shard_map/all_to_all | solution.py:444
  60.7 12.2 %collective-permute-start.3 = (f32[48,128]{1,0:T(8,128)S(1)}, f32[48,128]{1,0:T(8,128)S(1)}, u32[]{:S(2)}, u32[]{:S(2)}) collective-permute-start(f32[48,128]{1,0:T(8,128)S(1)} %slice_bitcast_fusion.1), channel_id=1, source_target_pairs={{0,0},{1,16},{2,32},{3,48},{4,64},{5,80},{6,96},{7,112},{8,128},{9... | collective-permute-start | bytes 73736 | tf_op jit(solution)/shard_map/ppermute | solution.py:498
  100.7 17.8 %all-to-all-start.15 = ((f32[32,24,128]{2,1,0:T(8,128)}), f32[32,24,128]{2,1,0:T(8,128)S(1)}, u32[]{:S(2)}, u32[]{:S(2)}) async-start(f32[32,24,128]{2,1,0:T(8,128)} %get-tuple-element.91), calls=%async_computation.15 | async-start | bytes 786432 | tf_op jit(solution)/shard_map/all_to_all | solution.py:444
  108.0 10.4 %collective-permute-start.4 = (f32[16,128]{1,0:T(8,128)S(1)}, f32[16,128]{1,0:T(8,128)S(1)}, u32[]{:S(2)}, u32[]{:S(2)}) collective-permute-start(f32[16,128]{1,0:T(8,128)S(1)} %get-tuple-element.94), channel_id=1, source_target_pairs={{0,0},{16,1},{32,2},{48,3},{64,4},{80,5},{96,6},{112,7},{128,8},{1... | collective-permute-start | bytes 24584 | tf_op jit(solution)/shard_map/ppermute | solution.py:479
  119.8 27.4 %all-to-all-start.16 = ((f32[16,40,128]{2,1,0:T(8,128)}), f32[16,40,128]{2,1,0:T(8,128)S(1)}, u32[]{:S(2)}, u32[]{:S(2)}) async-start(f32[16,40,128]{2,1,0:T(8,128)} %inner.6), calls=%async_computation.16 | async-start | bytes 655360 | tf_op jit(solution)/shard_map/all_to_all | solution.py:444
  145.7 0.8 copy-start.13
  147.1 1.0 copy-start.14
  153.5 8.4 %copy-start = (f32[1024,64]{1,0:T(8,128)}, f32[1024,64]{1,0:T(8,128)S(1)}, u32[]{:S(2)}) copy-start(f32[1024,64]{1,0:T(8,128)S(1)} %get-tuple-element.97.panel_c_ref) | copy-start | bytes 786436
  181.4 14.9 %all-to-all-start.18 = ((f32[16,32,128]{2,1,0:T(8,128)}), f32[16,32,128]{2,1,0:T(8,128)S(1)}, u32[]{:S(2)}, u32[]{:S(2)}) async-start(f32[16,32,128]{2,1,0:T(8,128)} %get-tuple-element.100), calls=%async_computation.18 | async-start | bytes 524288 | tf_op jit(solution)/shard_map/all_to_all | solution.py:444
  186.6 9.7 %copy-start.7 = (f32[512,64]{1,0:T(8,128)}, f32[512,64]{1,0:T(8,128)S(1)}, u32[]{:S(2)}) copy-start(f32[512,64]{1,0:T(8,128)S(1)} %get-tuple-element.106.panel_r_ref.once_ref) | copy-start | bytes 393220
  186.6 9.7 %collective-permute-start.5 = (f32[16,128]{1,0:T(8,128)S(1)}, f32[16,128]{1,0:T(8,128)S(1)}, u32[]{:S(2)}, u32[]{:S(2)}) collective-permute-start(f32[16,128]{1,0:T(8,128)S(1)} %get-tuple-element.110), channel_id=1, source_target_pairs={{0,0},{1,16},{2,32},{3,48},{4,64},{5,80},{6,96},{7,112},{8,128},{9... | collective-permute-start | bytes 24584 | tf_op jit(solution)/shard_map/ppermute | solution.py:479
  195.8 14.6 %copy-start.30 = (f32[64,64]{1,0:T(8,128)S(1)}, f32[64,64]{1,0:T(8,128)}, u32[]{:S(2)}) copy-start(f32[64,64]{1,0:T(8,128)} %copy-done.29) | copy-start | bytes 49156
  197.6 34.9 %all-to-all-start.19 = ((f32[32,40,128]{2,1,0:T(8,128)}), f32[32,40,128]{2,1,0:T(8,128)S(1)}, u32[]{:S(2)}, u32[]{:S(2)}) async-start(f32[32,40,128]{2,1,0:T(8,128)} %inner.7), calls=%async_computation.19 | async-start | bytes 1310720 | tf_op jit(solution)/shard_map/all_to_all | solution.py:444
  210.4 1.0 copy-start.1
  211.5 0.9 copy-start.6
  212.4 0.9 copy-start.8
  229.7 0.8 copy-start.11
  230.5 0.7 copy-start.17
  232.5 1.0 copy-start.12
  233.6 0.9 copy-start.18
  261.7 24.5 %all-to-all-start.1 = ((f32[32,24,128]{2,1,0:T(8,128)}), f32[32,24,128]{2,1,0:T(8,128)S(1)}, u32[]{:S(2)}, u32[]{:S(2)}) async-start(f32[32,24,128]{2,1,0:T(8,128)} %get-tuple-element.21), calls=%async_computation.1 | async-start | bytes 786432 | tf_op jit(solution)/shard_map/cond/branch_0_fun/all_to_all | solution.py:444
  287.1 23.2 %all-to-all-start.2 = ((f32[16,72,128]{2,1,0:T(8,128)}), f32[16,72,128]{2,1,0:T(8,128)S(1)}, u32[]{:S(2)}, u32[]{:S(2)}) async-start(f32[16,72,128]{2,1,0:T(8,128)} %relay.1), calls=%async_computation.2 | async-start | bytes 1179648 | tf_op jit(solution)/shard_map/cond/branch_0_fun/all_to_all | solution.py:444
  290.9 6.6 %collective-permute-start = (f32[48,128]{1,0:T(8,128)S(1)}, f32[48,128]{1,0:T(8,128)S(1)}, u32[]{:S(2)}, u32[]{:S(2)}) collective-permute-start(f32[48,128]{1,0:T(8,128)S(1)} %slice_bitcast_fusion.raw_ref), channel_id=1, source_target_pairs={{0,0},{1,16},{2,32},{3,48},{4,64},{5,80},{6,96},{7,112},{8,128},{9... | collective-permute-start | bytes 73736 | tf_op jit(solution)/shard_map/cond/branch_0_fun/ppermute | solution.py:548
  311.2 25.9 %all-to-all-start.4 = ((f32[32,48,128]{2,1,0:T(8,128)}), f32[32,48,128]{2,1,0:T(8,128)S(1)}, u32[]{:S(2)}, u32[]{:S(2)}) async-start(f32[32,48,128]{2,1,0:T(8,128)} %broadcast_in_dim.33), calls=%async_computation.4 | async-start | bytes 1572864 | tf_op jit(solution)/shard_map/cond/branch_0_fun/all_to_all | solution.py:444
  356.1 18.8 %all-to-all-start.5 = ((f32[32,24,128]{2,1,0:T(8,128)}), f32[32,24,128]{2,1,0:T(8,128)S(1)}, u32[]{:S(2)}, u32[]{:S(2)}) async-start(f32[32,24,128]{2,1,0:T(8,128)} %get-tuple-element.25), calls=%async_computation.5 | async-start | bytes 786432 | tf_op jit(solution)/shard_map/cond/branch_0_fun/all_to_all | solution.py:444
  363.6 11.2 %collective-permute-start.1 = (f32[16,128]{1,0:T(8,128)S(1)}, f32[16,128]{1,0:T(8,128)S(1)}, u32[]{:S(2)}, u32[]{:S(2)}) collective-permute-start(f32[16,128]{1,0:T(8,128)S(1)} %get-tuple-element.29), channel_id=1, source_target_pairs={{0,0},{16,1},{32,2},{48,3},{64,4},{80,5},{96,6},{112,7},{128,8},{1... | collective-permute-start | bytes 24584 | tf_op jit(solution)/shard_map/cond/branch_0_fun/ppermute | solution.py:479
  376.2 23.0 %all-to-all-start.6 = ((f32[16,40,128]{2,1,0:T(8,128)}), f32[16,40,128]{2,1,0:T(8,128)S(1)}, u32[]{:S(2)}, u32[]{:S(2)}) async-start(f32[16,40,128]{2,1,0:T(8,128)} %inner.4), calls=%async_computation.6 | async-start | bytes 655360 | tf_op jit(solution)/shard_map/cond/branch_0_fun/all_to_all | solution.py:444
  395.5 0.8 copy-start.15
  396.3 13.8 %copy-start.25 = (f32[512,64]{1,0:T(8,128)}, f32[512,64]{1,0:T(8,128)S(1)}, u32[]{:S(2)}) copy-start(f32[512,64]{1,0:T(8,128)S(1)} %get-tuple-element.32.vec_ref) | copy-start | bytes 393220 | tf_op jit(solution)/shard_map/cond
  399.2 1.0 copy-start.16
  403.8 0.8 copy-start.10
  405.3 15.0 %all-to-all-start.7 = ((f32[16,24,128]{2,1,0:T(8,128)}), f32[16,24,128]{2,1,0:T(8,128)S(1)}, u32[]{:S(2)}, u32[]{:S(2)}) async-start(f32[16,24,128]{2,1,0:T(8,128)} %copy-done.27), calls=%async_computation.7 | async-start | bytes 393216 | tf_op jit(solution)/shard_map/cond/branch_0_fun/all_to_all | solution.py:444
  410.0 1.0 copy-start.26
  412.4 0.7 copy-start.23
  420.3 1.0 copy-start.24
  431.1 0.7 copy-start.3
  456.0 17.8 %all-to-all-start.9 = ((f32[32,24,128]{2,1,0:T(8,128)}), f32[32,24,128]{2,1,0:T(8,128)S(1)}, u32[]{:S(2)}, u32[]{:S(2)}) async-start(f32[32,24,128]{2,1,0:T(8,128)} %get-tuple-element.42), calls=%async_computation.9 | async-start | bytes 786432 | tf_op jit(solution)/shard_map/cond/branch_0_fun/all_to_all | solution.py:444
  462.4 11.3 %collective-permute-start.2 = (f32[16,128]{1,0:T(8,128)S(1)}, f32[16,128]{1,0:T(8,128)S(1)}, u32[]{:S(2)}, u32[]{:S(2)}) collective-permute-start(f32[16,128]{1,0:T(8,128)S(1)} %get-tuple-element.45), channel_id=1, source_target_pairs={{0,0},{16,1},{32,2},{48,3},{64,4},{80,5},{96,6},{112,7},{128,8},{1... | collective-permute-start | bytes 24584 | tf_op jit(solution)/shard_map/cond/branch_0_fun/ppermute | solution.py:479
  474.4 0.7 copy-start.2
  475.2 27.1 %all-to-all-start.10 = ((f32[16,40,128]{2,1,0:T(8,128)}), f32[16,40,128]{2,1,0:T(8,128)}, u32[]{:S(2)}, u32[]{:S(2)}) async-start(f32[16,40,128]{2,1,0:T(8,128)} %copy-done.2), calls=%async_computation.10 | async-start | bytes 655360 | tf_op jit(solution)/shard_map/cond/branch_0_fun/all_to_all | solution.py:444
  484.9 3.1 copy-start.4
  500.0 0.8 copy-start.9
  500.8 0.7 copy-start.19
  501.5 0.7 copy-start.21
  502.2 1.0 copy-start.20
  503.2 0.9 copy-start.22
  511.1 2.3 copy-start.31
  (4 other events, 2.7 us)
where the time goes:
time: 520 us; the launch traced here: 514 us
  starting transfers between devices  136 us (26%)
  blocking collectives  132 us (25%)
  Pallas kernels  92.4 us (18%)
  waiting for transfers between devices  88.1 us (17%)
  local copies, waits for them, and re-layouts  31.5 us (6%)
  matrix products  27.9 us (5%)
    all_to_all x6, blocking collectives, swap(): return lax.all_to_all(x, axis, 0, 0)  132 us
    all_to_all x14, starting transfers between devices, swap(): return lax.all_to_all(x, axis, 0, 0)  107 us
    pallas_call x24, Pallas kernels, call(): pl.pallas_call(functools.partial(kernel, *statics), out_shape=out_shape,...  92.4 us
    all_to_all x14, waiting for transfers between devices, swap(): return lax.all_to_all(x, axis, 0, 0)  64.9 us
    ppermute x4, starting transfers between devices, image_round(): other = lax.ppermute(image_chunk, ('row', 'col'), targets)  22.9 us
    dot_general x5, matrix products, nt(): lax.dot_general(a, b, (((1,), (1,)), ((), ())), precision=precise, prefer...  14.3 us
    unnamed x33, local copies, waits for them, and re-layouts  12.5 us
    cond x32, local copies, waits for them, and re-layouts  11.5 us
  transfers between devices with their start and end apart: 20, of which 14 were waited for; matrix products, arithmetic and copies ran while one was open for 3% of the time, Pallas kernels for 12%

commit v1 on v0

--- a/solution.py
+++ b/solution.py
@@ -40,14 +40,22 @@
     eye = (sub + NB == lane).astype(jnp.float32)
     work = jnp.concatenate([gram, jnp.zeros_like(gram)], axis=1) + eye
     scales = jnp.zeros((NB, 2 * NB), jnp.float32)
-    for step in range(NB):
-        row = work[step : step + 1, :]
-        pivot = row[:, step : step + 1]
-        scales = jnp.where(sub == step, pivot, scales)
-        if step + 1 < NB:
-            scaled = row * (1.0 / pivot)
-            column = jnp.where(sub > step, work[:, step : step + 1], 0.0)
-            work = work - column * scaled
+    for step in range(0, NB, 2):
+        first = work[step : step + 1]
+        second = work[step + 1 : step + 2]
+        left = jnp.broadcast_to(work[:, step : step + 1], work.shape)
+        right = jnp.broadcast_to(work[:, step + 1 : step + 2], work.shape)
+        a, b = left[step : step + 1], right[step : step + 1]
+        c, d = left[step + 1 : step + 2], right[step + 1 : step + 2]
+        inverse = 1.0 / a
+        det = a * d - b * c
+        last = a * (1.0 / det)
+        second = second - (c * inverse) * first
+        scales = jnp.where(sub == step, a, jnp.where(sub == step + 1, det * inverse, scales))
+        second_scaled = second * last
+        first_scaled = first * inverse - (b * inverse) * second_scaled
+        change = left * first_scaled + right * second_scaled
+        work = jnp.where(sub > step + 1, work - change, jnp.where(sub == step + 1, second, work))
     return (work * lax.rsqrt(scales))[:, NB:]
 
 
@@ -59,21 +67,38 @@
     upper = jnp.zeros((NB, 2 * NB), jnp.float32)
     signs = jnp.zeros((1, 2 * NB), jnp.float32)
     lane_row = lax.broadcasted_iota(jnp.int32, (1, 2 * NB), 1)
-    for step in range(NB):
-        row = work[step : step + 1, :]
-        raw = row[:, step : step + 1]
+    for step in range(0, NB, 2):
+        left = jnp.broadcast_to(work[:, step : step + 1], work.shape)
+        right = jnp.broadcast_to(work[:, step + 1 : step + 2], work.shape)
+        raw, b = left[step : step + 1], right[step : step + 1]
+        c, d = left[step + 1 : step + 2], right[step + 1 : step + 2]
         flip = jnp.where(raw > 0, 1.0, -1.0)
-        signs = jnp.where(lane_row == step, flip, signs)
-        pivot = raw + flip
-        inverse = 1.0 / pivot
-        row = jnp.where(lane_row == step, pivot, row)
-        upper = jnp.where((sub == step) & (lane >= step), row, upper)
-        column = work[:, step : step + 1]
-        lower = jnp.where(
-            lane == step, jnp.where(sub > step, column * inverse, jnp.where(sub == step, 1.0, 0.0)), lower
+        a = raw + flip
+        raw_det = a * d - b * c
+        flip_last = jnp.where(raw_det * flip > 0, 1.0, -1.0)
+        det = raw_det + flip_last * a
+        inverse = 1.0 / a
+        last = a * (1.0 / det)
+        signs = jnp.where(lane_row == step, flip, jnp.where(lane_row == step + 1, flip_last, signs))
+        first = jnp.where(lane_row == step, a, work[step : step + 1])
+        second = work[step + 1 : step + 2] - (c * inverse) * first
+        second = jnp.where(lane_row == step + 1, det * inverse, second)
+        upper = jnp.where(
+            (sub == step) & (lane >= step), first,
+            jnp.where((sub == step + 1) & (lane > step), second, upper),
         )
-        scaled = row * inverse
-        work = jnp.where(sub == step, scaled, work - column * scaled)
+        second_scaled = second * last
+        second_scaled = jnp.where(lane_row == step, 0.0, second_scaled)
+        ratio = b * inverse
+        first_scaled = first * inverse - ratio * second_scaled
+        below_first = jnp.where(sub > step, left * inverse, jnp.where(sub == step, 1.0, 0.0))
+        below_last = (right - left * ratio) * last
+        below_last = jnp.where(sub > step + 1, below_last, jnp.where(sub == step + 1, 1.0, 0.0))
+        lower = jnp.where(lane == step, below_first, jnp.where(lane == step + 1, below_last, lower))
+        change = left * first_scaled + right * second_scaled
+        work = jnp.where(
+            sub == step, first_scaled, jnp.where(sub == step + 1, second_scaled, work - change)
+        )
     return lower[:, :NB], upper[:, :NB], work[:, NB:], signs[:, :NB]
 
 
@@ -117,13 +142,13 @@
 PACKED = 24
 
 
-def put_pairs(out_ref, pairs):
+def put_pairs(out_ref, pairs, first=0):
     peers, rows = out_ref.shape[:2]
     per = NB // peers
     for q, pair in enumerate(pairs):
         for t in range(per):
-            out_ref[:, q * per + t, :] = pair[t * peers : (t + 1) * peers]
-    for k in range(len(pairs) * per, rows):
+            out_ref[:, first + q * per + t, :] = pair[t * peers : (t + 1) * peers]
+    for k in range(first + len(pairs) * per, rows):
         out_ref[:, k, :] = jnp.zeros((peers, 2 * NB), jnp.float32)
 
 
@@ -163,12 +188,16 @@
     out_ref[...] = jnp.broadcast_to(block[None], out_ref.shape)
 
 
-def last_raw(raw_ref, chunk):
-    return unfold(raw_ref[:, chunk : chunk + chunk // 2, :])
+def pair_raw(raw_ref, chunk, at=0):
+    return raw_ref[:, at : at + chunk, :].reshape(-1, 2 * NB)
+
+
+def last_raw(raw_ref, chunk, at=0):
+    return unfold(raw_ref[:, at + chunk : at + chunk + chunk // 2, :])
 
 
 def first_pairs(chunk, index, raw_ref, root, once_ref, small_ref):
-    pair = raw_ref[:, :chunk, :].reshape(-1, 2 * NB)
+    pair = pair_raw(raw_ref, chunk)
     following = pair[:, NB:]
     once = below(pair[:, :NB], index, NB)
     if root is not None:
@@ -201,7 +230,7 @@
     first_pairs(chunk, index_ref[0], raw_ref, root, once_ref, small_ref)
 
 
-def second_pairs(index, once, last, vec, wide, small_ref):
+def second_pairs(index, once, last, vec, wide, small_ref, first=0):
     def top(x):
         return jnp.where(index == 0, x[2 * NB : 3 * NB], 0.0)
 
@@ -213,6 +242,7 @@
             beside(top(once), top(vec)),
             beside(top(wide), jnp.zeros((NB, NB), jnp.float32)),
         ],
+        first,
     )
 
 
@@ -233,9 +263,24 @@
     chunk_ref[...] = summed[: chunk_ref.shape[0]]
 
 
+def sum_with_kernel(got_ref, raw_ref, out_ref, chunk_ref):
+    summed = jnp.sum(got_ref[...], axis=0)
+    block = jnp.concatenate([summed, raw_ref[...]], axis=0)
+    out_ref[...] = jnp.broadcast_to(block[None], out_ref.shape)
+    chunk_ref[...] = summed[: chunk_ref.shape[0]]
+
+
 def inner_kernel(gathered_ref, once_ref, chunk_ref, out_ref):
     half = chunk_ref.shape[0]
     inner = tn(once_ref[...], unfold(gathered_ref[:, :half, :]))
+    block = jnp.concatenate([pack_symmetric(inner), chunk_ref[...]], axis=0)
+    out_ref[...] = jnp.broadcast_to(block[None], out_ref.shape)
+
+
+def plain_inner_kernel(chunk, at, col_ref, gathered_ref, chunk_ref, out_ref):
+    half = chunk_ref.shape[0]
+    panel = below(pair_raw(gathered_ref, chunk, at)[:, :NB], col_ref[0], NB)
+    inner = tn(panel, unfold(gathered_ref[:, :half, :]))
     block = jnp.concatenate([pack_symmetric(inner), chunk_ref[...]], axis=0)
     out_ref[...] = jnp.broadcast_to(block[None], out_ref.shape)
 
@@ -283,28 +328,44 @@
     return 0.5 * tn(factor, nn(inner, factor))
 
 
-def first_factor_kernel(
-    near, chunk, half, row_ref, col_ref, gathered_ref, raw_ref, once_c_ref, once_r_ref,
-    small_ref, state_ref, vec_ref, factor_ref, fine_ref,
-):
+def first_factor(near, chunk, half, at, row, col, gathered_ref, once_c, once_r, outs):
+    small_ref, state_ref, vec_ref, factor_ref, fine_ref = outs
     gram, image_top, top, next_top, _, _ = get_pairs(gathered_ref, half, 3)
     pick, coef, pick_t, coef_t, fine = factor_small(
         near, gram, top, next_top, image_top, small_ref
     )
     fine_ref[0] = jnp.where(fine, 1, 0)
     factor_ref[...] = small_ref[FACTOR]
-    vec_ref[...] = vectors_of(once_r_ref[...], row_ref[0], NB, pick, coef)
-    following = raw_ref[:, :chunk, :].reshape(-1, 2 * NB)[:, NB:]
+    vec_ref[...] = vectors_of(once_r, row, NB, pick, coef)
+    following = pair_raw(gathered_ref, chunk, at)[:, NB:]
     image = unfold(gathered_ref[:, :half, :])
-    vec = vectors_of(once_c_ref[...], col_ref[0], NB, pick, coef)
+    vec = vectors_of(once_c, col, NB, pick, coef)
     state_ref[...] = beside(vec, nn(following, pick_t) - nn(image, coef_t))
+
+
+def first_factor_kernel(
+    chunk, half, at, row_ref, col_ref, gathered_ref, once_c_ref, once_r_ref, *outs
+):
+    first_factor(
+        True, chunk, half, at, row_ref[0], col_ref[0], gathered_ref,
+        once_c_ref[...], once_r_ref[...], outs,
+    )
+
+
+def plain_factor_kernel(chunk, half, at, row_ref, col_ref, gathered_ref, panel_r_ref, *outs):
+    panel = below(pair_raw(gathered_ref, chunk, at)[:, :NB], col_ref[0], NB)
+    first_factor(
+        False, chunk, half, at, row_ref[0], col_ref[0], gathered_ref, panel, panel_r_ref[...], outs
+    )
 
 
 def second_panel(following, vec, wide, wide_top, lower, index):
     return below(following - nt(vec, wide_top) - nt(wide, lower), index, 2 * NB)
 
 
-def first_cols(chunk, index, got_ref, small_ref, state_ref, raw_ref, pair_ref, panel_ref, tops_ref):
+def first_cols(
+    chunk, at, index, got_ref, small_ref, state_ref, raw_ref, pair_ref, panel_ref, tops_ref
+):
     half = half_core(small_ref, unpack_symmetric(jnp.sum(got_ref[:, :PACKED, :], axis=0)))
     lower = small_ref[LOWER]
     wide_top = small_ref[WIDE] - nn(lower, half)
@@ -313,36 +374,43 @@
     vec = state_ref[:, :NB]
     wide = state_ref[:, NB:] - nn(vec, half)
     pair_ref[...] = beside(wide, vec)
-    following = raw_ref[:, :chunk, :].reshape(-1, 2 * NB)[:, NB:]
+    following = pair_raw(raw_ref, chunk, at)[:, NB:]
     panel = second_panel(following, vec, wide, wide_top, lower, index)
     panel_ref[...] = panel
     return panel, vec, wide
 
 
 def first_cols_kernel(
-    chunk, col_ref, got_ref, small_ref, state_ref, raw_ref, pair_ref, panel_ref, tops_ref, out_ref
+    chunk, at, col_ref, got_ref, small_ref, state_ref, raw_ref,
+    pair_ref, panel_ref, tops_ref, out_ref,
 ):
     panel, _, _ = first_cols(
-        chunk, col_ref[0], got_ref, small_ref, state_ref, raw_ref, pair_ref, panel_ref, tops_ref
+        chunk, at, col_ref[0], got_ref, small_ref, state_ref, raw_ref,
+        pair_ref, panel_ref, tops_ref,
     )
     packed = pack_symmetric(tn(panel, panel))
     out_ref[...] = jnp.broadcast_to(packed[None], out_ref.shape)
 
 
 def plain_cols_kernel(
-    chunk, col_ref, got_ref, small_ref, state_ref, raw_ref, pair_ref, panel_ref, tops_ref, out_ref
+    chunk, at, col_ref, got_ref, small_ref, state_ref, raw_ref, matrix_ref,
+    pair_ref, panel_ref, tops_ref, out_ref,
 ):
     panel, vec, wide = first_cols(
-        chunk, col_ref[0], got_ref, small_ref, state_ref, raw_ref, pair_ref, panel_ref, tops_ref
-    )
-    second_pairs(col_ref[0], panel, last_raw(raw_ref, chunk), vec, wide, out_ref)
+        chunk, at, col_ref[0], got_ref, small_ref, state_ref, raw_ref,
+        pair_ref, panel_ref, tops_ref,
+    )
+    half = chunk // 2
+    out_ref[:, :half, :] = fold(nn(matrix_ref[...], panel), chunk)
+    last = last_raw(raw_ref, chunk, at)
+    second_pairs(col_ref[0], panel, last, vec, wide, out_ref, half)
 
 
 def first_rows_kernel(
     chunk, row_ref, got_ref, small_ref, vec_ref, raw_ref, tops_ref, pair_ref, panel_ref
 ):
     image = unfold(got_ref[:, PACKED:, :])
-    following = raw_ref[:, :chunk, :].reshape(-1, 2 * NB)[:, NB:]
+    following = pair_raw(raw_ref, chunk)[:, NB:]
     vec = vec_ref[...]
     wide = nn(following, small_ref[PICK_T]) - nn(image, small_ref[COEF_T]) - nn(vec, tops_ref[0])
     pair_ref[...] = beside(vec, wide)
@@ -370,7 +438,7 @@
 
 
 def second_factor_kernel(
-    chunk, half, row_ref, col_ref, gathered_ref, old_ref, raw_c_ref, raw_r_ref,
+    chunk, half, at, row_ref, col_ref, gathered_ref, old_ref, raw_r_ref,
     once_c_ref, once_r_ref, pair_c_ref, pair_r_ref, factor_ref,
     small_ref, right_ref, state_ref, vectors_ref, factors_ref,
 ):
@@ -379,19 +447,19 @@
     )
     new = vectors_of(once_r_ref[...], row_ref[0], 2 * NB, pick, coef)
     vec = pair_r_ref[:, :NB]
-    vectors_ref[0] = vec
-    vectors_ref[1] = new
+    vectors_ref[0] = vec.T
+    vectors_ref[1] = new.T
     part = nn(last_raw(raw_r_ref, chunk), pick_t)
     part += nn(vec, vec_dots) + nn(pair_r_ref[:, NB:], wide_dots)
     state_ref[...] = beside(new, part)
     new = vectors_of(once_c_ref[...], col_ref[0], 2 * NB, pick, coef)
-    part = nn(last_raw(raw_c_ref, chunk), pick_t) - nn(unfold(gathered_ref[:, :half, :]), coef_t)
+    part = nn(last_raw(old_ref, chunk, at), pick_t) - nn(unfold(gathered_ref[:, :half, :]), coef_t)
     part += nn(pair_c_ref[:, NB:], vec_dots) + nn(pair_c_ref[:, :NB], wide_dots)
     right_ref[...] = beside(part, new)
 
 
 def plain_second_kernel(
-    chunk, half, row_ref, col_ref, gathered_ref, old_ref, raw_c_ref, raw_r_ref,
+    chunk, half, at, row_ref, col_ref, gathered_ref, old_ref, raw_r_ref,
     panel_c_ref, panel_r_ref, pair_c_ref, pair_r_ref, factor_ref,
     small_ref, state_ref, left_ref, vectors_ref, factors_ref, fine_ref,
 ):
@@ -401,13 +469,13 @@
     fine_ref[0] = jnp.where(fine, 1, 0)
     new = vectors_of(panel_r_ref[...], row_ref[0], 2 * NB, pick, coef)
     vec = pair_r_ref[:, :NB]
-    vectors_ref[0] = vec
-    vectors_ref[1] = new
+    vectors_ref[0] = vec.T
+    vectors_ref[1] = new.T
     part = nn(last_raw(raw_r_ref, chunk), pick_t) - nn(unfold(gathered_ref[:, :half, :]), coef_t)
     part += nn(vec, vec_dots) + nn(pair_r_ref[:, NB:], wide_dots)
     left_ref[...] = beside(part, new)
     new = vectors_of(panel_c_ref[...], col_ref[0], 2 * NB, pick, coef)
-    part = nn(last_raw(raw_c_ref, chunk), pick_t)
+    part = nn(last_raw(old_ref, chunk, at), pick_t)
     part += nn(pair_c_ref[:, NB:], vec_dots) + nn(pair_c_ref[:, :NB], wide_dots)
     state_ref[...] = beside(new, part)
 
@@ -472,19 +540,19 @@
         def few(peers):
             return -(-4 * (NB // peers) // 8) * 8
 
-        def image_round(partial_image, smalls, axis, targets, ready):
-            mine = jnp.concatenate([fold(partial_image, chunk), smalls], axis=1)
-            got, ready = lax.optimization_barrier((swap(mine, axis), ready))
-            blocks, image_chunk = call(sum_kernel, "sum_blocks", [got.shape, (half, 2 * NB)], got)
-            other = lax.ppermute(image_chunk, ("row", "col"), targets)
-            return swap(blocks, axis), other, ready
-
-        def spread_columns(raw_c):
-            return swap(jnp.broadcast_to(raw_c[None], (nr, raw_rows, 2 * NB)), "row")
-
-        def first_columns(raw_c):
-            first_c = raw_c[:, :chunk].reshape(cols_here, 2 * NB)[:, :NB]
-            return jnp.where(col_place >= NB, first_c, 0.0)
+        def image_round(mine, axis, targets, extra=()):
+            got = swap(mine, axis)
+            rows = got.shape[1] + sum(x.shape[0] for x in extra)
+            blocks, image_chunk = call(
+                sum_with_kernel if extra else sum_kernel, "sum_blocks",
+                [(got.shape[0], rows, 2 * NB), (half, 2 * NB)], got, *extra,
+            )
+            return swap(blocks, axis), lax.ppermute(image_chunk, ("row", "col"), targets)
+
+        def image_blocks(once_r, smalls):
+            return jnp.concatenate([fold(tn(matrix, once_r), chunk), smalls], axis=1)
+
+        at = half + few(nr)
 
         block_r = (nc, PACKED + half, 2 * NB)
         block_c = (nr, PACKED + half, 2 * NB)
@@ -497,44 +565,42 @@
             raw_chunk = swap(raw, "col")[0]
             raw_chunk_c = lax.ppermute(raw_chunk, ("row", "col"), to_cols)
             raw_r = swap(jnp.broadcast_to(raw_chunk[None], raw.shape), "col")
-            raw_c = spread_columns(raw_chunk_c)
             first_r, smalls = call(
                 plain_first_kernel, "plain_first", [tall_r, (nr, few(nr), 2 * NB)],
                 my_row, raw_r, statics=(chunk,), scalars=1,
             )
-            gathered, image_chunk, raw_c = image_round(
-                tn(matrix, first_r), smalls, "row", to_rows, raw_c
-            )
-            first_c = first_columns(raw_c)
-            inners = call(inner_kernel, "inner", [block_r], gathered, first_c, image_chunk)
+            gathered, image_chunk = image_round(
+                image_blocks(first_r, smalls), "row", to_rows, (raw_chunk_c,)
+            )
+            inners = call(
+                plain_inner_kernel, "plain_inner", [block_r],
+                my_col, gathered, image_chunk, statics=(chunk, at), scalars=1,
+            )
             got = swap(inners, "col")
             small_one, state_c, vec_r, factor_one, fine_one = call(
-                first_factor_kernel, "plain_factor", [(8,) + square, pair_shape_c, tall_r, square],
-                my_row, my_col, gathered, raw_c, first_c, first_r,
-                statics=(False, chunk, half), scalars=2, flag=True,
-            )
-            pair_c, panel_c, tops, smalls = call(
+                plain_factor_kernel, "plain_factor", [(8,) + square, pair_shape_c, tall_r, square],
+                my_row, my_col, gathered, first_r, statics=(chunk, half, at), scalars=2, flag=True,
+            )
+            pair_c, panel_c, tops, blocks = call(
                 plain_cols_kernel, "plain_cols",
-                [pair_shape_c, tall_c, (2,) + square, (nc, few(nc), 2 * NB)],
-                my_col, got, small_one, state_c, raw_c, statics=(chunk,), scalars=1,
+                [pair_shape_c, tall_c, (2,) + square, (nc, half + few(nc), 2 * NB)],
+                my_col, got, small_one, state_c, gathered, matrix, statics=(chunk, at), scalars=1,
             )
             pair_r, panel_r = call(
                 first_rows_kernel, "first_rows", [pair_shape_r, tall_r],
                 my_row, got, small_one, vec_r, raw_r, tops, statics=(chunk,), scalars=1,
             )
             old = gathered
-            gathered, image_chunk, _ = image_round(
-                nn(matrix, panel_c), smalls, "col", to_cols, my_row
-            )
+            gathered, image_chunk = image_round(blocks, "col", to_cols)
             current = matrix - nt(pair_r, pair_c)
             gathered, current = lax.optimization_barrier((gathered, current))
             inners = call(inner_kernel, "inner", [block_c], gathered, panel_r, image_chunk)
             got = swap(inners, "row")
             small_two, state_c, left, vectors, factors, fine_two = call(
                 plain_second_kernel, "plain_second",
-                [(8,) + square, pair_shape_c, pair_shape_r, (2,) + tall_r, (2,) + square],
-                my_row, my_col, gathered, old, raw_c, raw_r, panel_c, panel_r,
-                pair_c, pair_r, factor_one, statics=(chunk, half), scalars=2, flag=True,
+                [(8,) + square, pair_shape_c, pair_shape_r, (2, NB, rows_here), (2,) + square],
+                my_row, my_col, gathered, old, raw_r, panel_c, panel_r,
+                pair_c, pair_r, factor_one, statics=(chunk, half, at), scalars=2, flag=True,
             )
             right = call(last_kernel, "last", [pair_shape_c], got, small_two, state_c)
             return (current, left, right, vectors, factors), (fine_one + fine_two)[0] == 2
@@ -550,28 +616,28 @@
                 relay_kernel, "relay", [(nc, raw_rows + PACKED, 2 * NB)], raw_chunk, swap(grams, "row")
             )
             raw_r = swap(raw_r, "col")
-            raw_c = spread_columns(raw_chunk_c)
 
             root, once_r, smalls = call(
                 first_once_kernel, "first_once", [square, tall_r, (nr, few(nr), 2 * NB)],
                 my_row, raw_r, statics=(chunk,), scalars=1,
             )
 
-            gathered, image_chunk_r, raw_c = image_round(
-                tn(matrix, once_r), smalls, "row", to_rows, raw_c
-            )
-            once_c = nt(first_columns(raw_c), root)
+            gathered, image_chunk_r = image_round(
+                image_blocks(once_r, smalls), "row", to_rows, (raw_chunk_c,)
+            )
+            first_c = gathered[:, at : at + chunk, :NB].reshape(tall_c)
+            once_c = nt(jnp.where(col_place >= NB, first_c, 0.0), root)
             inners = call(inner_kernel, "inner", [block_r], gathered, once_c, image_chunk_r)
             got = swap(inners, "col")
             small_one, state_c, vec_r, factor_one, _ = call(
                 first_factor_kernel, "first_factor", [(8,) + square, pair_shape_c, tall_r, square],
-                my_row, my_col, gathered, raw_c, once_c, once_r,
-                statics=(True, chunk, half), scalars=2, flag=True,
+                my_row, my_col, gathered, once_c, once_r,
+                statics=(chunk, half, at), scalars=2, flag=True,
             )
             pair_c, panel_c, tops, grams = call(
                 first_cols_kernel, "first_cols",
                 [pair_shape_c, tall_c, (2,) + square, (nc, PACKED, 2 * NB)],
-                my_col, got, small_one, state_c, raw_c, statics=(chunk,), scalars=1,
+                my_col, got, small_one, state_c, gathered, statics=(chunk, at), scalars=1,
             )
             grams = swap(grams, "col")
             pair_r, panel_r = call(
@@ -584,18 +650,16 @@
                 my_row, grams, raw_r, panel_r, pair_r, statics=(chunk,), scalars=1,
             )
             old = gathered
-            gathered, image_chunk_r, _ = image_round(
-                tn(matrix, once_r), smalls, "row", to_rows, my_row
-            )
+            gathered, image_chunk_r = image_round(image_blocks(once_r, smalls), "row", to_rows)
             once_c = nt(panel_c, root)
             current = matrix - nt(pair_r, pair_c)
             inners = call(inner_kernel, "inner", [block_r], gathered, once_c, image_chunk_r)
             got = swap(inners, "col")
             small_two, right, state_r, vectors, factors = call(
                 second_factor_kernel, "second_factor",
-                [(8,) + square, pair_shape_c, pair_shape_r, (2,) + tall_r, (2,) + square],
-                my_row, my_col, gathered, old, raw_c, raw_r, once_c, once_r, pair_c, pair_r, factor_one,
-                statics=(chunk, half), scalars=2,
+                [(8,) + square, pair_shape_c, pair_shape_r, (2, NB, rows_here), (2,) + square],
+                my_row, my_col, gathered, old, raw_r, once_c, once_r, pair_c, pair_r, factor_one,
+                statics=(chunk, half, at), scalars=2,
             )
             left = call(last_kernel, "last", [pair_shape_r], got, small_two, state_r)
             return current - nt(left, right), vectors, factors
@@ -605,7 +669,8 @@
         def finish(current, left, right, vectors, factors):
             return current - nt(left, right), vectors, factors
 
-        return lax.cond(fine, finish, lambda *_: careful(), *ready)
+        banded, vectors, factors = lax.cond(fine, finish, lambda *_: careful(), *ready)
+        return banded, vectors.transpose(0, 2, 1), factors
 
     return jax.shard_map(
         local,

time: 520 us -> 476 us (0.915)
  blocking collectives: 132 us -> 104 us
  waiting for transfers between devices: 88.1 us -> 111 us
  Pallas kernels: 92.4 us -> 78 us
  starting transfers between devices: 136 us -> 124 us
  local copies, waits for them, and re-layouts: 31.5 us -> 25.2 us
    all_to_all x6 -> x5, blocking collectives: 132 us -> 104 us  [swap(): return lax.all_to_all(x, axis, 0, 0)]
    ppermute x4, waiting for transfers between devices: 11.1 us -> 27.5 us  [image_round(): lax.ppermute(image_chunk, ('row', 'col'), targets)]
    pallas_call x24, Pallas kernels: 92.4 us -> 78 us  [call(): pl.pallas_call(functools.partial(kernel, *statics), out_shape=out_shape,...]
    all_to_all x14 -> x13, starting transfers between devices: 107 us -> 95.3 us  [swap(): return lax.all_to_all(x, axis, 0, 0)]
    ppermute x1, waiting for transfers between devices: 2.81 us -> 8.62 us  [careful(): raw_chunk_c = lax.ppermute(raw_chunk, ('row', 'col'), to_cols)]
    unnamed x33 -> x26, local copies, waits for them, and re-layouts: 12.5 us -> 10 us
    all_to_all x14 -> x13, waiting for transfers between devices: 64.9 us -> 65.6 us  [swap(): return lax.all_to_all(x, axis, 0, 0)]
    cond x32 -> x30, local copies, waits for them, and re-layouts: 11.5 us -> 11.5 us
  transfers between devices with their start and end apart: 20 -> 19, of which waited for: 14 -> 15; matrix products, arithmetic and copies ran while one was open for 3% -> 2% of each run, Pallas kernels for 12% -> 9%
where the time goes in v1:
time: 476 us; the launch traced here: 470 us
  starting transfers between devices  124 us (26%)
  waiting for transfers between devices  111 us (23%)
  blocking collectives  104 us (22%)
  Pallas kernels  78 us (16%)
  local copies, waits for them, and re-layouts  25.2 us (5%)
  matrix products  23.2 us (5%)
    all_to_all x5, blocking collectives, swap(): return lax.all_to_all(x, axis, 0, 0)  104 us
    all_to_all x13, starting transfers between devices, swap(): return lax.all_to_all(x, axis, 0, 0)  95.3 us
    pallas_call x24, Pallas kernels, call(): pl.pallas_call(functools.partial(kernel, *statics), out_shape=out_shape,...  78 us
    all_to_all x13, waiting for transfers between devices, swap(): return lax.all_to_all(x, axis, 0, 0)  65.6 us
    ppermute x4, waiting for transfers between devices, image_round(): lax.ppermute(image_chunk, ('row', 'col'), targets)  27.5 us
    ppermute x4, starting transfers between devices, image_round(): lax.ppermute(image_chunk, ('row', 'col'), targets)  22.4 us
    dot_general x5, matrix products, nt(): lax.dot_general(a, b, (((1,), (1,)), ((), ())), precision=precise, prefer...  14.3 us
    cond x30, local copies, waits for them, and re-layouts  11.5 us
  transfers between devices with their start and end apart: 19, of which 15 were waited for; matrix products, arithmetic and copies ran while one was open for 2% of the time, Pallas kernels for 9%

profile of v1, /device:TPU:1, one launch (start us, length us, event | category | flops | bytes accessed | tf_op | source)
XLA Modules:
  0.0 470.2 jit_solution(17220026601681401351)
XLA Ops:
  1.8 26.2 %all_to_all.83 = f32[16,48,128]{2,1,0:T(8,128)S(1)} all-to-all(f32[16,48,128]{2,1,0:T(8,128)S(1)} %plain_start.1), channel_id=1, replica_groups=mesh['row'=32,'col'=16] {'col'}, dimensions={0} | all-to-all | bytes 786432 | tf_op jit(solution)/shard_map/all_to_all | solution.py:512
  28.8 3.5 all-to-all-start.11
  32.2 14.0 %all-to-all-done.11.raw_ref.raw_r_ref = f32[16,48,128]{2,1,0:T(8,128)S(1)} async-done(((f32[16,48,128]{2,1,0:T(8,128)}), f32[16,48,128]{2,1,0:T(8,128)S(1)}, u32[]{:S(2)}, u32[]{:S(2)}) %all-to-all-start.11) | async-done | bytes 393248 | tf_op jit(solution)/shard_map/all_to_all | solution.py:512
  46.8 3.0 convolution_bitcast_fusion.2
  51.0 9.7 %all-to-all-start.12 = ((f32[32,24,128]{2,1,0:T(8,128)}), f32[32,24,128]{2,1,0:T(8,128)S(1)}, u32[]{:S(2)}, u32[]{:S(2)}) async-start(f32[32,24,128]{2,1,0:T(8,128)} %pad_maximum_fusion.2), calls=%async_computation.12 | async-start | bytes 786432 | tf_op jit(solution)/shard_map/all_to_all | solution.py:512
  60.6 2.9 collective-permute-start.3
  63.5 9.4 %collective-permute-done.3.raw_ref = f32[48,128]{1,0:T(8,128)S(1)} collective-permute-done((f32[48,128]{1,0:T(8,128)S(1)}, f32[48,128]{1,0:T(8,128)S(1)}, u32[]{:S(2)}, u32[]{:S(2)}) %collective-permute-start.3) | collective-permute-done | bytes 24608 | tf_op jit(solution)/shard_map/ppermute | solution.py:566
  76.7 5.8 %all-to-all-start.13 = ((f32[32,72,128]{2,1,0:T(8,128)}), f32[32,72,128]{2,1,0:T(8,128)S(1)}, u32[]{:S(2)}, u32[]{:S(2)}) async-start(f32[32,72,128]{2,1,0:T(8,128)} %get-tuple-element.87), calls=%async_computation.13 | async-start | bytes 2359296 | tf_op jit(solution)/shard_map/all_to_all | solution.py:512
  82.5 6.4 %collective-permute-start.4 = (f32[16,128]{1,0:T(8,128)S(1)}, f32[16,128]{1,0:T(8,128)S(1)}, u32[]{:S(2)}, u32[]{:S(2)}) collective-permute-start(f32[16,128]{1,0:T(8,128)S(1)} %get-tuple-element.89), channel_id=1, source_target_pairs={{0,0},{16,1},{32,2},{48,3},{64,4},{80,5},{96,6},{112,7},{128,8},{1... | collective-permute-start | bytes 24584 | tf_op jit(solution)/shard_map/ppermute | solution.py:550
  88.9 21.7 %collective-permute-done.4.chunk_ref = f32[16,128]{1,0:T(8,128)S(1)} collective-permute-done((f32[16,128]{1,0:T(8,128)S(1)}, f32[16,128]{1,0:T(8,128)S(1)}, u32[]{:S(2)}, u32[]{:S(2)}) %collective-permute-start.4) | collective-permute-done | bytes 8224 | tf_op jit(solution)/shard_map/ppermute | solution.py:550
  112.0 10.2 %all-to-all-start.14 = ((f32[16,40,128]{2,1,0:T(8,128)}), f32[16,40,128]{2,1,0:T(8,128)S(1)}, u32[]{:S(2)}, u32[]{:S(2)}) async-start(f32[16,40,128]{2,1,0:T(8,128)} %plain_inner.1), calls=%async_computation.14 | async-start | bytes 655360 | tf_op jit(solution)/shard_map/all_to_all | solution.py:512
  122.2 9.6 %plain_factor.1 = (f32[8,64,64]{2,1,0:T(8,128)S(1)}, f32[1024,128]{1,0:T(8,128)S(1)}, f32[512,64]{1,0:T(8,128)S(1)}, f32[64,64]{1,0:T(8,128)S(1)}, s32[1]{0:T(128)}) custom-call(s32[1]{0:T(128)} %bitcast.6.index_ref.row_ref, s32[1]{0:T(128)} %bitcast.7.col_ref, f32[32,72,128]{2,1,0:T(8,128)S(1)} %all-to-all-done.13.gathered_ref.raw_ref.old_ref, ...), custom_call_target="tpu_custom_call" | custom-call | flops 16777216 | bytes 4194304 | tf_op jit(solution)/shard_map/plain_factor/pallas_call | solution.py:499
  136.2 8.2 %plain_cols.1 = (f32[1024,128]{1,0:T(8,128)S(1)}, f32[1024,64]{1,0:T(8,128)S(1)}, f32[2,64,64]{2,1,0:T(8,128)S(1)}, f32[16,32,128]{2,1,0:T(8,128)S(1)}) custom-call(s32[1]{0:T(128)} %bitcast.7.col_ref, f32[16,40,128]{2,1,0:T(8,128)S(1)} %all-to-all-done.14.got_ref, f32[8,64,64]{2,1,0:T(8,128)S(1)} %get-tuple-element.90.small_ref, ...), custom_call_target="tpu_custom_call" | custom-call | flops 16777216 | bytes 4194304 | tf_op jit(solution)/shard_map/plain_cols/pallas_call | solution.py:499
  144.4 17.4 %all_to_all.84.got_ref = f32[16,32,128]{2,1,0:T(8,128)S(1)} all-to-all(f32[16,32,128]{2,1,0:T(8,128)S(1)} %get-tuple-element.92), channel_id=1, replica_groups=mesh['row'=32,'col'=16] {'col'}, dimensions={0} | all-to-all | bytes 524288 | tf_op jit(solution)/shard_map/all_to_all | solution.py:512
  162.6 3.4 all-to-all-start.16
  168.5 3.5 collective-permute-start.5
  172.0 4.7 %convolution_subtract_fusion.1 = f32[512,1024]{1,0:T(8,128)} fusion(f32[512,1024]{1,0:T(8,128)} %matrix_ref.1, f32[512,128]{1,0:T(8,128)S(1)} %get-tuple-element.96.pair_r_ref, f32[1024,128]{1,0:T(8,128)S(1)} %get-tuple-element.97.pair_c_ref), kind=kOutput, calls=%fused_computation.9 | convolution fusion | flops 805830656 | bytes 4980736 | tf_op jit(solution)/shard_map/dot_general | solution.py:27
  178.5 12.0 %all-to-all-start.17 = ((f32[32,40,128]{2,1,0:T(8,128)}), f32[32,40,128]{2,1,0:T(8,128)S(1)}, u32[]{:S(2)}, u32[]{:S(2)}) async-start(f32[32,40,128]{2,1,0:T(8,128)} %inner.5), calls=%async_computation.17 | async-start | bytes 1310720 | tf_op jit(solution)/shard_map/all_to_all | solution.py:512
  193.3 11.9 %plain_second.1 = (f32[8,64,64]{2,1,0:T(8,128)S(1)}, f32[1024,128]{1,0:T(8,128)S(1)}, f32[512,128]{1,0:T(8,128)}, f32[2,64,512]{2,1,0:T(8,128)}, f32[2,64,64]{2,1,0:T(8,128)}, /*index=5*/s32[1]{0:T(128)}) custom-call(s32[1]{0:T(128)} %bitcast.6.index_ref.row_ref, s32[1]{0:T(128)} %bitcast.7.col_ref, f32[16,32,128]{2,1,0:T(8,128)S(1)} %all-to-all-done.16.gathered_ref, ...), custom_call_target="tpu_custom_call" | custom-call | flops 16777216 | bytes 4194304 | tf_op jit(solution)/shard_map/plain_second/pallas_call | solution.py:499
  213.5 255.1 %conditional.1 = (f32[512,1024]{1,0:T(8,128)S(1)}, f32[2,64,512]{2,1,0:T(8,128)}, f32[2,64,64]{2,1,0:T(8,128)}) conditional(s32[]{:T(128)} %bitcast.11, (f32[512,1024]{1,0:T(8,128)}, s32[1]{0:T(128)}, s32[]{:T(128)}, s32[1]{0:T(128)}, s32[1024,1]{0,1:T(1,128)S(1)}, /*index=5*/()) %tuple.18, (f32[512,128]{1,0:T(8,128)}, f32[1024,128]{1,0:T(8,128)}, ...), branch_computations={%region_0.1_spmd, %region_1.2_spmd} | conditional | flops 2736195584 | bytes 103865152 | solution.py:672
  215.8 20.0 %all_to_all.80 = f32[16,48,128]{2,1,0:T(8,128)S(1)} all-to-all(f32[16,48,128]{2,1,0:T(8,128)S(1)} %get-tuple-element.20), channel_id=1, replica_groups=mesh['row'=32,'col'=16] {'col'}, dimensions={0} | all-to-all | bytes 786432 | tf_op jit(solution)/shard_map/cond/branch_0_fun/all_to_all | solution.py:512
  235.8 6.3 %all-to-all-start.1 = ((f32[32,24,128]{2,1,0:T(8,128)}), f32[32,24,128]{2,1,0:T(8,128)S(1)}, u32[]{:S(2)}, u32[]{:S(2)}) async-start(f32[32,24,128]{2,1,0:T(8,128)} %get-tuple-element.21), calls=%async_computation.1 | async-start | bytes 786432 | tf_op jit(solution)/shard_map/cond/branch_0_fun/all_to_all | solution.py:512
  242.1 14.9 %all-to-all-done.1.got_ref = f32[32,24,128]{2,1,0:T(8,128)S(1)} async-done(((f32[32,24,128]{2,1,0:T(8,128)}), f32[32,24,128]{2,1,0:T(8,128)S(1)}, u32[]{:S(2)}, u32[]{:S(2)}) %all-to-all-start.1) | async-done | bytes 393248 | tf_op jit(solution)/shard_map/cond/branch_0_fun/all_to_all | solution.py:512
  257.0 22.3 %all_to_all.81.raw_ref.raw_r_ref = f32[16,72,128]{2,1,0:T(8,128)S(1)} all-to-all(f32[16,72,128]{2,1,0:T(8,128)S(1)} %relay.1), channel_id=1, replica_groups=mesh['row'=32,'col'=16] {'col'}, dimensions={0} | all-to-all | bytes 1179648 | tf_op jit(solution)/shard_map/cond/branch_0_fun/all_to_all | solution.py:512
  279.3 4.5 first_once.1
  283.9 3.0 convolution_bitcast_fusion.1
  288.0 5.0 %all-to-all-start.3 = ((f32[32,24,128]{2,1,0:T(8,128)}), f32[32,24,128]{2,1,0:T(8,128)S(1)}, u32[]{:S(2)}, u32[]{:S(2)}) async-start(f32[32,24,128]{2,1,0:T(8,128)} %pad_maximum_fusion), calls=%async_computation.3 | async-start | bytes 786432 | tf_op jit(solution)/shard_map/cond/branch_0_fun/all_to_all | solution.py:512
  293.1 3.7 collective-permute-start
  296.7 8.6 %collective-permute-done.raw_ref = f32[48,128]{1,0:T(8,128)S(1)} collective-permute-done((f32[48,128]{1,0:T(8,128)S(1)}, f32[48,128]{1,0:T(8,128)S(1)}, u32[]{:S(2)}, u32[]{:S(2)}) %collective-permute-start) | collective-permute-done | bytes 24608 | tf_op jit(solution)/shard_map/cond/branch_0_fun/ppermute | solution.py:614
  306.5 8.4 %all-to-all-start.4 = ((f32[32,72,128]{2,1,0:T(8,128)}), f32[32,72,128]{2,1,0:T(8,128)S(1)}, u32[]{:S(2)}, u32[]{:S(2)}) async-start(f32[32,72,128]{2,1,0:T(8,128)} %get-tuple-element.24), calls=%async_computation.4 | async-start | bytes 2359296 | tf_op jit(solution)/shard_map/cond/branch_0_fun/all_to_all | solution.py:512
  314.9 7.3 %collective-permute-start.1 = (f32[16,128]{1,0:T(8,128)S(1)}, f32[16,128]{1,0:T(8,128)S(1)}, u32[]{:S(2)}, u32[]{:S(2)}) collective-permute-start(f32[16,128]{1,0:T(8,128)S(1)} %get-tuple-element.27), channel_id=1, source_target_pairs={{0,0},{16,1},{32,2},{48,3},{64,4},{80,5},{96,6},{112,7},{128,8},{1... | collective-permute-start | bytes 24584 | tf_op jit(solution)/shard_map/cond/branch_0_fun/ppermute | solution.py:550
  322.2 18.6 %all-to-all-done.4.gathered_ref.raw_ref.old_ref = f32[32,72,128]{2,1,0:T(8,128)S(1)} async-done(((f32[32,72,128]{2,1,0:T(8,128)}), f32[32,72,128]{2,1,0:T(8,128)S(1)}, u32[]{:S(2)}, u32[]{:S(2)}) %all-to-all-start.4) | async-done | bytes 1179680 | tf_op jit(solution)/shard_map/cond/branch_0_fun/all_to_all | solution.py:512
  344.4 10.4 %all-to-all-start.5 = ((f32[16,40,128]{2,1,0:T(8,128)}), f32[16,40,128]{2,1,0:T(8,128)S(1)}, u32[]{:S(2)}, u32[]{:S(2)}) async-start(f32[16,40,128]{2,1,0:T(8,128)} %inner.3), calls=%async_computation.5 | async-start | bytes 655360 | tf_op jit(solution)/shard_map/cond/branch_0_fun/all_to_all | solution.py:512
  354.8 7.0 %first_factor.1 = (f32[8,64,64]{2,1,0:T(8,128)S(1)}, f32[1024,128]{1,0:T(8,128)S(1)}, f32[512,64]{1,0:T(8,128)S(1)}, f32[64,64]{1,0:T(8,128)S(1)}, s32[1]{0:T(128)}) custom-call(s32[1]{0:T(128)} %get-tuple-element.19.index_ref.row_ref, s32[1]{0:T(128)} %get-tuple-element.28.col_ref, f32[32,72,128]{2,1,0:T(8,128)S(1)} %all-to-all-done.4.gathered_ref.raw_ref.old_ref, ...), custom_call_target="tpu_custom_call" | custom-call | flops 16777216 | bytes 4194304 | tf_op jit(solution)/shard_map/cond/branch_0_fun/first_factor/pallas_call | solution.py:499
  363.3 4.5 all-to-all-done.5.got_ref
  368.9 4.2 first_cols.1
  374.0 3.4 all-to-all-start.6
  380.5 6.7 %all-to-all-done.6.got_ref = f32[16,24,128]{2,1,0:T(8,128)S(1)} async-done(((f32[16,24,128]{2,1,0:T(8,128)}), f32[16,24,128]{2,1,0:T(8,128)S(1)}, u32[]{:S(2)}, u32[]{:S(2)}) %all-to-all-start.6) | async-done | bytes 196640 | tf_op jit(solution)/shard_map/cond/branch_0_fun/all_to_all | solution.py:512
  388.1 4.8 %second_once.1 = (f32[64,64]{1,0:T(8,128)S(1)}, f32[512,64]{1,0:T(8,128)S(1)}, f32[32,8,128]{2,1,0:T(8,128)S(1)}) custom-call(s32[1]{0:T(128)} %get-tuple-element.19.index_ref.row_ref, f32[16,24,128]{2,1,0:T(8,128)S(1)} %all-to-all-done.6.got_ref, f32[16,72,128]{2,1,0:T(8,128)S(1)} %all_to_all.81.raw_ref.raw_r_ref, f32[512,64]{1,0:T(8,128)S(1)} %copy-done.22, ...), custom_call_target="tpu_custom_call" | custom-call | flops 16777216 | bytes 4194304 | tf_op jit(solution)/shard_map/cond/branch_0_fun/second_once/pallas_call | solution.py:499
  392.9 3.0 convolution_bitcast_fusion
  397.0 17.6 %all_to_all.82.got_ref = f32[32,24,128]{2,1,0:T(8,128)S(1)} all-to-all(f32[32,24,128]{2,1,0:T(8,128)S(1)} %pad_maximum_fusion.1), channel_id=1, replica_groups=mesh['row'=32,'col'=16] {'row'}, dimensions={0} | all-to-all | bytes 786432 | tf_op jit(solution)/shard_map/cond/branch_0_fun/all_to_all | solution.py:512
  415.4 7.3 %all-to-all-start.8 = ((f32[32,24,128]{2,1,0:T(8,128)}), f32[32,24,128]{2,1,0:T(8,128)S(1)}, u32[]{:S(2)}, u32[]{:S(2)}) async-start(f32[32,24,128]{2,1,0:T(8,128)} %get-tuple-element.39), calls=%async_computation.8 | async-start | bytes 786432 | tf_op jit(solution)/shard_map/cond/branch_0_fun/all_to_all | solution.py:512
  422.7 5.2 %collective-permute-start.2 = (f32[16,128]{1,0:T(8,128)S(1)}, f32[16,128]{1,0:T(8,128)S(1)}, u32[]{:S(2)}, u32[]{:S(2)}) collective-permute-start(f32[16,128]{1,0:T(8,128)S(1)} %get-tuple-element.42), channel_id=1, source_target_pairs={{0,0},{16,1},{32,2},{48,3},{64,4},{80,5},{96,6},{112,7},{128,8},{1... | collective-permute-start | bytes 24584 | tf_op jit(solution)/shard_map/cond/branch_0_fun/ppermute | solution.py:550
  429.6 4.4 collective-permute-done.2.chunk_ref
  435.4 9.8 %all-to-all-start.9 = ((f32[16,40,128]{2,1,0:T(8,128)}), f32[16,40,128]{2,1,0:T(8,128)}, u32[]{:S(2)}, u32[]{:S(2)}) async-start(f32[16,40,128]{2,1,0:T(8,128)} %copy-done), calls=%async_computation.9 | async-start | bytes 655360 | tf_op jit(solution)/shard_map/cond/branch_0_fun/all_to_all | solution.py:512
  445.2 3.1 fusion.4
  448.4 9.1 %second_factor.1 = (f32[8,64,64]{2,1,0:T(8,128)S(1)}, f32[1024,128]{1,0:T(8,128)S(1)}, f32[512,128]{1,0:T(8,128)S(1)}, f32[2,64,512]{2,1,0:T(8,128)}, f32[2,64,64]{2,1,0:T(8,128)}) custom-call(s32[1]{0:T(128)} %get-tuple-element.19.index_ref.row_ref, s32[1]{0:T(128)} %get-tuple-element.28.col_ref, f32[32,24,128]{2,1,0:T(8,128)S(1)} %all-to-all-done.8.gathered_ref, ...), custom_call_target="tpu_custom_call" | custom-call | flops 16777216 | bytes 4194304 | tf_op jit(solution)/shard_map/cond/branch_0_fun/second_factor/pallas_call | solution.py:499
  464.1 4.3 subtract_subtract_fusion
  (102 shorter events, 56.5 us)
Async XLA Ops:
  28.8 17.4 %all-to-all-start.11 = ((f32[16,48,128]{2,1,0:T(8,128)}), f32[16,48,128]{2,1,0:T(8,128)S(1)}, u32[]{:S(2)}, u32[]{:S(2)}) async-start(f32[16,48,128]{2,1,0:T(8,128)} %broadcast_in_dim.23), calls=%async_computation.11 | async-start | bytes 786432 | tf_op jit(solution)/shard_map/all_to_all | solution.py:512
  51.0 24.6 %all-to-all-start.12 = ((f32[32,24,128]{2,1,0:T(8,128)}), f32[32,24,128]{2,1,0:T(8,128)S(1)}, u32[]{:S(2)}, u32[]{:S(2)}) async-start(f32[32,24,128]{2,1,0:T(8,128)} %pad_maximum_fusion.2), calls=%async_computation.12 | async-start | bytes 786432 | tf_op jit(solution)/shard_map/all_to_all | solution.py:512
  60.6 12.2 %collective-permute-start.3 = (f32[48,128]{1,0:T(8,128)S(1)}, f32[48,128]{1,0:T(8,128)S(1)}, u32[]{:S(2)}, u32[]{:S(2)}) collective-permute-start(f32[48,128]{1,0:T(8,128)S(1)} %slice_bitcast_fusion.1), channel_id=1, source_target_pairs={{0,0},{1,16},{2,32},{3,48},{4,64},{5,80},{6,96},{7,112},{8,128},{9... | collective-permute-start | bytes 73736 | tf_op jit(solution)/shard_map/ppermute | solution.py:566
  76.7 34.0 %all-to-all-start.13 = ((f32[32,72,128]{2,1,0:T(8,128)}), f32[32,72,128]{2,1,0:T(8,128)S(1)}, u32[]{:S(2)}, u32[]{:S(2)}) async-start(f32[32,72,128]{2,1,0:T(8,128)} %get-tuple-element.87), calls=%async_computation.13 | async-start | bytes 2359296 | tf_op jit(solution)/shard_map/all_to_all | solution.py:512
  82.5 28.1 %collective-permute-start.4 = (f32[16,128]{1,0:T(8,128)S(1)}, f32[16,128]{1,0:T(8,128)S(1)}, u32[]{:S(2)}, u32[]{:S(2)}) collective-permute-start(f32[16,128]{1,0:T(8,128)S(1)} %get-tuple-element.89), channel_id=1, source_target_pairs={{0,0},{16,1},{32,2},{48,3},{64,4},{80,5},{96,6},{112,7},{128,8},{1... | collective-permute-start | bytes 24584 | tf_op jit(solution)/shard_map/ppermute | solution.py:550
  112.0 23.1 %all-to-all-start.14 = ((f32[16,40,128]{2,1,0:T(8,128)}), f32[16,40,128]{2,1,0:T(8,128)S(1)}, u32[]{:S(2)}, u32[]{:S(2)}) async-start(f32[16,40,128]{2,1,0:T(8,128)} %plain_inner.1), calls=%async_computation.14 | async-start | bytes 655360 | tf_op jit(solution)/shard_map/all_to_all | solution.py:512
  131.8 0.8 copy-start.10
  132.6 0.7 copy-start.15
  133.3 0.6 copy-start.25
  135.2 1.0 copy-start.11
  144.4 18.2 %copy-start.5 = (f32[1024,64]{1,0:T(8,128)}, f32[1024,64]{1,0:T(8,128)S(1)}, u32[]{:S(2)}) copy-start(f32[1024,64]{1,0:T(8,128)S(1)} %get-tuple-element.99.panel_c_ref) | copy-start | bytes 786436
  162.6 14.6 %all-to-all-start.16 = ((f32[16,32,128]{2,1,0:T(8,128)}), f32[16,32,128]{2,1,0:T(8,128)S(1)}, u32[]{:S(2)}, u32[]{:S(2)}) async-start(f32[16,32,128]{2,1,0:T(8,128)} %get-tuple-element.93), calls=%async_computation.16 | async-start | bytes 524288 | tf_op jit(solution)/shard_map/all_to_all | solution.py:512
  166.1 1.0 copy-start.16
  168.5 8.7 %copy-start.3 = (f32[512,64]{1,0:T(8,128)}, f32[512,64]{1,0:T(8,128)S(1)}, u32[]{:S(2)}) copy-start(f32[512,64]{1,0:T(8,128)S(1)} %get-tuple-element.100.panel_r_ref.once_ref) | copy-start | bytes 393220
  168.5 8.7 %collective-permute-start.5 = (f32[16,128]{1,0:T(8,128)S(1)}, f32[16,128]{1,0:T(8,128)S(1)}, u32[]{:S(2)}, u32[]{:S(2)}) collective-permute-start(f32[16,128]{1,0:T(8,128)S(1)} %get-tuple-element.104), channel_id=1, source_target_pairs={{0,0},{1,16},{2,32},{3,48},{4,64},{5,80},{6,96},{7,112},{8,128},{9... | collective-permute-start | bytes 24584 | tf_op jit(solution)/shard_map/ppermute | solution.py:550
  178.5 31.1 %all-to-all-start.17 = ((f32[32,40,128]{2,1,0:T(8,128)}), f32[32,40,128]{2,1,0:T(8,128)S(1)}, u32[]{:S(2)}, u32[]{:S(2)}) async-start(f32[32,40,128]{2,1,0:T(8,128)} %inner.5), calls=%async_computation.17 | async-start | bytes 1310720 | tf_op jit(solution)/shard_map/all_to_all | solution.py:512
  190.6 1.0 copy-start.4
  191.5 1.0 copy-start.6
  192.6 0.8 copy-start.26
  205.2 0.8 copy-start.13
  209.6 1.0 copy-start.14
  235.8 21.2 %all-to-all-start.1 = ((f32[32,24,128]{2,1,0:T(8,128)}), f32[32,24,128]{2,1,0:T(8,128)S(1)}, u32[]{:S(2)}, u32[]{:S(2)}) async-start(f32[32,24,128]{2,1,0:T(8,128)} %get-tuple-element.21), calls=%async_computation.1 | async-start | bytes 786432 | tf_op jit(solution)/shard_map/cond/branch_0_fun/all_to_all | solution.py:512
  288.0 17.3 %all-to-all-start.3 = ((f32[32,24,128]{2,1,0:T(8,128)}), f32[32,24,128]{2,1,0:T(8,128)S(1)}, u32[]{:S(2)}, u32[]{:S(2)}) async-start(f32[32,24,128]{2,1,0:T(8,128)} %pad_maximum_fusion), calls=%async_computation.3 | async-start | bytes 786432 | tf_op jit(solution)/shard_map/cond/branch_0_fun/all_to_all | solution.py:512
  293.1 12.3 %collective-permute-start = (f32[48,128]{1,0:T(8,128)S(1)}, f32[48,128]{1,0:T(8,128)S(1)}, u32[]{:S(2)}, u32[]{:S(2)}) collective-permute-start(f32[48,128]{1,0:T(8,128)S(1)} %slice_bitcast_fusion.raw_ref), channel_id=1, source_target_pairs={{0,0},{1,16},{2,32},{3,48},{4,64},{5,80},{6,96},{7,112},{8,128},{9... | collective-permute-start | bytes 73736 | tf_op jit(solution)/shard_map/cond/branch_0_fun/ppermute | solution.py:614
  306.5 34.3 %all-to-all-start.4 = ((f32[32,72,128]{2,1,0:T(8,128)}), f32[32,72,128]{2,1,0:T(8,128)S(1)}, u32[]{:S(2)}, u32[]{:S(2)}) async-start(f32[32,72,128]{2,1,0:T(8,128)} %get-tuple-element.24), calls=%async_computation.4 | async-start | bytes 2359296 | tf_op jit(solution)/shard_map/cond/branch_0_fun/all_to_all | solution.py:512
  314.9 28.1 %collective-permute-start.1 = (f32[16,128]{1,0:T(8,128)S(1)}, f32[16,128]{1,0:T(8,128)S(1)}, u32[]{:S(2)}, u32[]{:S(2)}) collective-permute-start(f32[16,128]{1,0:T(8,128)S(1)} %get-tuple-element.27), channel_id=1, source_target_pairs={{0,0},{16,1},{32,2},{48,3},{64,4},{80,5},{96,6},{112,7},{128,8},{1... | collective-permute-start | bytes 24584 | tf_op jit(solution)/shard_map/cond/branch_0_fun/ppermute | solution.py:550
  344.4 23.4 %all-to-all-start.5 = ((f32[16,40,128]{2,1,0:T(8,128)}), f32[16,40,128]{2,1,0:T(8,128)S(1)}, u32[]{:S(2)}, u32[]{:S(2)}) async-start(f32[16,40,128]{2,1,0:T(8,128)} %inner.3), calls=%async_computation.5 | async-start | bytes 655360 | tf_op jit(solution)/shard_map/cond/branch_0_fun/all_to_all | solution.py:512
  361.8 0.8 copy-start.8
  362.6 0.7 copy-start.23
  367.8 1.0 copy-start.9
  373.1 0.8 copy-start.12
  374.0 13.2 %all-to-all-start.6 = ((f32[16,24,128]{2,1,0:T(8,128)}), f32[16,24,128]{2,1,0:T(8,128)S(1)}, u32[]{:S(2)}, u32[]{:S(2)}) async-start(f32[16,24,128]{2,1,0:T(8,128)} %get-tuple-element.35), calls=%async_computation.6 | async-start | bytes 393216 | tf_op jit(solution)/shard_map/cond/branch_0_fun/all_to_all | solution.py:512
  377.4 1.0 copy-start.24
  379.8 0.7 copy-start.21
  387.1 1.0 copy-start.22
  395.9 0.7 copy-start.1
  415.4 18.7 %all-to-all-start.8 = ((f32[32,24,128]{2,1,0:T(8,128)}), f32[32,24,128]{2,1,0:T(8,128)S(1)}, u32[]{:S(2)}, u32[]{:S(2)}) async-start(f32[32,24,128]{2,1,0:T(8,128)} %get-tuple-element.39), calls=%async_computation.8 | async-start | bytes 786432 | tf_op jit(solution)/shard_map/cond/branch_0_fun/all_to_all | solution.py:512
  422.7 11.3 %collective-permute-start.2 = (f32[16,128]{1,0:T(8,128)S(1)}, f32[16,128]{1,0:T(8,128)S(1)}, u32[]{:S(2)}, u32[]{:S(2)}) collective-permute-start(f32[16,128]{1,0:T(8,128)S(1)} %get-tuple-element.42), channel_id=1, source_target_pairs={{0,0},{16,1},{32,2},{48,3},{64,4},{80,5},{96,6},{112,7},{128,8},{1... | collective-permute-start | bytes 24584 | tf_op jit(solution)/shard_map/cond/branch_0_fun/ppermute | solution.py:550
  434.7 0.7 copy-start
  435.4 24.3 %all-to-all-start.9 = ((f32[16,40,128]{2,1,0:T(8,128)}), f32[16,40,128]{2,1,0:T(8,128)}, u32[]{:S(2)}, u32[]{:S(2)}) async-start(f32[16,40,128]{2,1,0:T(8,128)} %copy-done), calls=%async_computation.9 | async-start | bytes 655360 | tf_op jit(solution)/shard_map/cond/branch_0_fun/all_to_all | solution.py:512
  445.2 3.1 copy-start.2
  457.5 0.8 copy-start.7
  458.3 0.7 copy-start.17
  459.0 0.7 copy-start.19
  459.7 1.0 copy-start.18
  460.6 0.9 copy-start.20
  468.6 1.3 copy-start.27

commit v2 on v1

--- a/solution.py
+++ b/solution.py
@@ -488,19 +488,69 @@
     out_ref[...] = beside(new, wide)
 
 
-def call(kernel, name, outs, *args, statics=(), scalars=0, flag=False):
+class FarIn:
+    def __init__(self, ref, buffer, semaphore):
+        self.buffer = buffer
+        self.copy = pltpu.make_async_copy(ref, buffer, semaphore)
+        self.copy.start()
+        self.here = False
+
+    def __getitem__(self, index):
+        if not self.here:
+            self.copy.wait()
+            self.here = True
+        return self.buffer[index]
+
+
+class FarOut:
+    def __init__(self, ref, buffer, semaphore):
+        self.buffer = buffer
+        self.copy = pltpu.make_async_copy(buffer, ref, semaphore)
+
+    def __setitem__(self, index, value):
+        self.buffer[index] = value
+        self.copy.start()
+
+
+def call(kernel, name, outs, *args, statics=(), scalars=0, flag=False, far_in=(), far_out=()):
     in_smem = pl.BlockSpec(memory_space=pltpu.SMEM)
     in_vmem = pl.BlockSpec(memory_space=pltpu.VMEM)
+    in_hbm = pl.BlockSpec(memory_space=pltpu.HBM)
+    in_specs = [in_smem if k < scalars else in_vmem for k in range(len(args))]
     out_shape = [jax.ShapeDtypeStruct(shape, jnp.float32) for shape in outs]
     out_specs = [in_vmem] * len(outs)
     if flag:
         out_shape.append(jax.ShapeDtypeStruct((1,), jnp.int32))
         out_specs.append(in_smem)
+    buffers = []
+    for k in far_in:
+        in_specs[k] = in_hbm
+        buffers.append(pltpu.VMEM(args[k].shape, jnp.float32))
+    for k in far_out:
+        out_specs[k] = in_hbm
+        buffers.append(pltpu.VMEM(outs[k], jnp.float32))
+    far = [*far_in, *[len(args) + k for k in far_out]]
+
+    def body(*refs):
+        refs = list(refs)
+        if far:
+            *refs, semaphores = refs
+            held = refs[len(refs) - len(far) :]
+            refs = refs[: len(refs) - len(far)]
+            for slot, k in enumerate(far):
+                kind = FarIn if k < len(args) else FarOut
+                refs[k] = kind(refs[k], held[slot], semaphores.at[slot])
+        kernel(*statics, *refs)
+        for k in far:
+            if k >= len(args):
+                refs[k].copy.wait()
+
     result = pl.pallas_call(
-        functools.partial(kernel, *statics),
+        body,
         out_shape=out_shape,
-        in_specs=[in_smem if k < scalars else in_vmem for k in range(len(args))],
+        in_specs=in_specs,
         out_specs=out_specs,
+        scratch_shapes=[*buffers, pltpu.SemaphoreType.DMA((len(far),))] if far else [],
         compiler_params=pltpu.CompilerParams(vmem_limit_bytes=16 << 20),
         cost_estimate=pl.CostEstimate(flops=1 << 24, bytes_accessed=1 << 22, transcendentals=0),
         name=name,
@@ -540,14 +590,14 @@
         def few(peers):
             return -(-4 * (NB // peers) // 8) * 8
 
-        def image_round(mine, axis, targets, extra=()):
-            got = swap(mine, axis)
+        def image_round(mine, axis, targets, extra=(), beside=()):
+            got, *beside = lax.optimization_barrier((swap(mine, axis), *beside))
             rows = got.shape[1] + sum(x.shape[0] for x in extra)
             blocks, image_chunk = call(
                 sum_with_kernel if extra else sum_kernel, "sum_blocks",
                 [(got.shape[0], rows, 2 * NB), (half, 2 * NB)], got, *extra,
             )
-            return swap(blocks, axis), lax.ppermute(image_chunk, ("row", "col"), targets)
+            return swap(blocks, axis), lax.ppermute(image_chunk, ("row", "col"), targets), *beside
 
         def image_blocks(once_r, smalls):
             return jnp.concatenate([fold(tn(matrix, once_r), chunk), smalls], axis=1)
@@ -558,10 +608,14 @@
         block_c = (nr, PACKED + half, 2 * NB)
 
         def plain():
-            raw = call(
-                plain_start_kernel, "plain_start", [(nc, raw_rows, 2 * NB)],
-                matrix[:, : 4 * NB], statics=(chunk,),
-            )
+            raw = pl.pallas_call(
+                functools.partial(plain_start_kernel, chunk),
+                grid=(1,),
+                in_specs=[pl.BlockSpec((rows_here, 4 * NB), lambda _: (0, 0))],
+                out_specs=pl.BlockSpec((nc, raw_rows, 2 * NB), lambda _: (0, 0, 0)),
+                out_shape=jax.ShapeDtypeStruct((nc, raw_rows, 2 * NB), jnp.float32),
+                name="plain_start",
+            )(matrix)
             raw_chunk = swap(raw, "col")[0]
             raw_chunk_c = lax.ppermute(raw_chunk, ("row", "col"), to_cols)
             raw_r = swap(jnp.broadcast_to(raw_chunk[None], raw.shape), "col")
@@ -580,29 +634,38 @@
             small_one, state_c, vec_r, factor_one, fine_one = call(
                 plain_factor_kernel, "plain_factor", [(8,) + square, pair_shape_c, tall_r, square],
                 my_row, my_col, gathered, first_r, statics=(chunk, half, at), scalars=2, flag=True,
+                far_out=(1, 2, 3),
             )
             pair_c, panel_c, tops, blocks = call(
                 plain_cols_kernel, "plain_cols",
                 [pair_shape_c, tall_c, (2,) + square, (nc, half + few(nc), 2 * NB)],
                 my_col, got, small_one, state_c, gathered, matrix, statics=(chunk, at), scalars=1,
+                far_in=(3,), far_out=(1,),
             )
             pair_r, panel_r = call(
                 first_rows_kernel, "first_rows", [pair_shape_r, tall_r],
                 my_row, got, small_one, vec_r, raw_r, tops, statics=(chunk,), scalars=1,
-            )
+                far_in=(3,), far_out=(1,),
+            )
+            current = matrix - nt(pair_r, pair_c)
             old = gathered
-            gathered, image_chunk = image_round(blocks, "col", to_cols)
-            current = matrix - nt(pair_r, pair_c)
-            gathered, current = lax.optimization_barrier((gathered, current))
-            inners = call(inner_kernel, "inner", [block_c], gathered, panel_r, image_chunk)
+            gathered, image_chunk, current, pair_r, panel_r = image_round(
+                blocks, "col", to_cols, beside=(current, pair_r, panel_r)
+            )
+            inners = call(
+                inner_kernel, "inner", [block_c], gathered, panel_r, image_chunk, far_in=(1,)
+            )
             got = swap(inners, "row")
             small_two, state_c, left, vectors, factors, fine_two = call(
                 plain_second_kernel, "plain_second",
                 [(8,) + square, pair_shape_c, pair_shape_r, (2, NB, rows_here), (2,) + square],
                 my_row, my_col, gathered, old, raw_r, panel_c, panel_r,
                 pair_c, pair_r, factor_one, statics=(chunk, half, at), scalars=2, flag=True,
-            )
-            right = call(last_kernel, "last", [pair_shape_c], got, small_two, state_c)
+                far_in=(5, 6, 9), far_out=(1,),
+            )
+            right = call(
+                last_kernel, "last", [pair_shape_c], got, small_two, state_c, far_in=(2,)
+            )
             return (current, left, right, vectors, factors), (fine_one + fine_two)[0] == 2
 
         def careful():

time: 476 us -> 480 us (level)
  blocking collectives: 104 us -> 87.7 us
  waiting for transfers between devices: 111 us -> 121 us
  Pallas kernels: 78 us -> 83.1 us
  starting transfers between devices: 124 us -> 129 us
    all_to_all x13 -> x14, waiting for transfers between devices: 65.6 us -> 90.7 us  [swap(): return lax.all_to_all(x, axis, 0, 0)]
    all_to_all x5 -> x4, blocking collectives: 104 us -> 87.7 us  [swap(): return lax.all_to_all(x, axis, 0, 0)]
    ppermute x1, waiting for transfers between devices: 9.38 us -> 0.01 us  [plain(): raw_chunk_c = lax.ppermute(raw_chunk, ('row', 'col'), to_cols)]
    ppermute x1, waiting for transfers between devices: 8.62 us -> 0.02 us  [careful(): raw_chunk_c = lax.ppermute(raw_chunk, ('row', 'col'), to_cols)]
    pallas_call x24, Pallas kernels: 78 us -> 83.1 us  [the longest x23 81.2 us: call(): pl.pallas_call(body, out_shape=out_shape, in_specs=in_specs, out_specs=ou...]
    all_to_all x13 -> x14, starting transfers between devices: 95.3 us -> 99.8 us  [swap(): return lax.all_to_all(x, axis, 0, 0)]
    unnamed x26 -> x24, local copies, waits for them, and re-layouts: 10 us -> 10.4 us
  transfers between devices with their start and end apart: 19 -> 20, of which waited for: 15 -> 16; matrix products, arithmetic and copies ran while one was open for 2% -> 2% of each run, Pallas kernels for 9% -> 9%
where the time goes in v2:
time: 480 us; the launch traced here: 474 us
  starting transfers between devices  129 us (27%)
  waiting for transfers between devices  121 us (25%)
  blocking collectives  87.7 us (18%)
  Pallas kernels  83.1 us (17%)
  local copies, waits for them, and re-layouts  24.5 us (5%)
  matrix products  23.2 us (5%)
    all_to_all x14, starting transfers between devices, swap(): return lax.all_to_all(x, axis, 0, 0)  99.8 us
    all_to_all x14, waiting for transfers between devices, swap(): return lax.all_to_all(x, axis, 0, 0)  90.7 us
    all_to_all x4, blocking collectives, swap(): return lax.all_to_all(x, axis, 0, 0)  87.7 us
    pallas_call x23, Pallas kernels, call(): pl.pallas_call(body, out_shape=out_shape, in_specs=in_specs, out_specs=ou...  81.2 us
    ppermute x4, waiting for transfers between devices, image_round(): lax.ppermute(image_chunk, ('row', 'col'), targets)  30.2 us
    ppermute x4, starting transfers between devices, image_round(): lax.ppermute(image_chunk, ('row', 'col'), targets)  22.4 us
    dot_general x5, matrix products, nt(): lax.dot_general(a, b, (((1,), (1,)), ((), ())), precision=precise, prefer...  14.3 us
    cond x30, local copies, waits for them, and re-layouts  11.6 us
  transfers between devices with their start and end apart: 20, of which 16 were waited for; matrix products, arithmetic and copies ran while one was open for 2% of the time, Pallas kernels for 9%

profile of v2, /device:TPU:1, one launch (start us, length us, event | category | flops | bytes accessed | tf_op | source)
XLA Modules:
  0.0 473.5 jit_solution(3091909907530127066)
XLA Ops:
  2.5 26.4 %all_to_all.83 = f32[16,48,128]{2,1,0:T(8,128)S(1)} all-to-all(f32[16,48,128]{2,1,0:T(8,128)} %plain_start.1), channel_id=1, replica_groups=mesh['row'=32,'col'=16] {'col'}, dimensions={0} | all-to-all | bytes 786432 | tf_op jit(solution)/shard_map/all_to_all | solution.py:562
  29.7 3.5 all-to-all-start.11
  33.1 14.0 %all-to-all-done.11.refs_1_.refs_4_ = f32[16,48,128]{2,1,0:T(8,128)S(1)} async-done(((f32[16,48,128]{2,1,0:T(8,128)}), f32[16,48,128]{2,1,0:T(8,128)S(1)}, u32[]{:S(2)}, u32[]{:S(2)}) %all-to-all-start.11) | async-done | bytes 393248 | tf_op jit(solution)/shard_map/all_to_all | solution.py:562
  47.7 3.0 convolution_bitcast_fusion.2
  51.9 9.7 %all-to-all-start.12 = ((f32[32,24,128]{2,1,0:T(8,128)}), f32[32,24,128]{2,1,0:T(8,128)S(1)}, u32[]{:S(2)}, u32[]{:S(2)}) async-start(f32[32,24,128]{2,1,0:T(8,128)} %pad_maximum_fusion.2), calls=%async_computation.12 | async-start | bytes 786432 | tf_op jit(solution)/shard_map/all_to_all | solution.py:562
  64.4 12.1 %all-to-all-done.12.refs_0_ = f32[32,24,128]{2,1,0:T(8,128)S(1)} async-done(((f32[32,24,128]{2,1,0:T(8,128)}), f32[32,24,128]{2,1,0:T(8,128)S(1)}, u32[]{:S(2)}, u32[]{:S(2)}) %all-to-all-start.12) | async-done | bytes 393248 | tf_op jit(solution)/shard_map/all_to_all | solution.py:562
  77.6 5.8 %all-to-all-start.13 = ((f32[32,72,128]{2,1,0:T(8,128)}), f32[32,72,128]{2,1,0:T(8,128)S(1)}, u32[]{:S(2)}, u32[]{:S(2)}) async-start(f32[32,72,128]{2,1,0:T(8,128)} %get-tuple-element.89), calls=%async_computation.13 | async-start | bytes 2359296 | tf_op jit(solution)/shard_map/all_to_all | solution.py:562
  83.4 6.4 %collective-permute-start.4 = (f32[16,128]{1,0:T(8,128)S(1)}, f32[16,128]{1,0:T(8,128)S(1)}, u32[]{:S(2)}, u32[]{:S(2)}) collective-permute-start(f32[16,128]{1,0:T(8,128)S(1)} %get-tuple-element.91), channel_id=1, source_target_pairs={{0,0},{16,1},{32,2},{48,3},{64,4},{80,5},{96,6},{112,7},{128,8},{1... | collective-permute-start | bytes 24584 | tf_op jit(solution)/shard_map/ppermute | solution.py:600
  89.8 21.7 %collective-permute-done.4.refs_2_ = f32[16,128]{1,0:T(8,128)S(1)} collective-permute-done((f32[16,128]{1,0:T(8,128)S(1)}, f32[16,128]{1,0:T(8,128)S(1)}, u32[]{:S(2)}, u32[]{:S(2)}) %collective-permute-start.4) | collective-permute-done | bytes 8224 | tf_op jit(solution)/shard_map/ppermute | solution.py:600
  112.9 10.2 %all-to-all-start.14 = ((f32[16,40,128]{2,1,0:T(8,128)}), f32[16,40,128]{2,1,0:T(8,128)S(1)}, u32[]{:S(2)}, u32[]{:S(2)}) async-start(f32[16,40,128]{2,1,0:T(8,128)} %plain_inner.1), calls=%async_computation.14 | async-start | bytes 655360 | tf_op jit(solution)/shard_map/all_to_all | solution.py:562
  123.1 10.9 %plain_factor.1 = (f32[8,64,64]{2,1,0:T(8,128)S(1)}, f32[1024,128]{1,0:T(8,128)S(1)}, f32[512,64]{1,0:T(8,128)S(1)}, f32[64,64]{1,0:T(8,128)S(1)}, s32[1]{0:T(128)}) custom-call(s32[1]{0:T(128)} %bitcast.6.refs_0_, s32[1]{0:T(128)} %bitcast.7.refs_1_.refs_0_, f32[32,72,128]{2,1,0:T(8,128)S(1)} %all-to-all-done.13.refs_2_.refs_1_.refs_4_.refs_3_, ...), custom_call_target="tpu_custom_call" | custom-call | flops 16777216 | bytes 4194304 | tf_op jit(solution)/shard_map/plain_factor/pallas_call | solution.py:548
  136.1 8.7 %plain_cols.1 = (f32[1024,128]{1,0:T(8,128)S(1)}, f32[1024,64]{1,0:T(8,128)S(1)}, f32[2,64,64]{2,1,0:T(8,128)S(1)}, f32[16,32,128]{2,1,0:T(8,128)S(1)}) custom-call(s32[1]{0:T(128)} %bitcast.7.refs_1_.refs_0_, f32[16,40,128]{2,1,0:T(8,128)S(1)} %all-to-all-done.14.refs_1_, f32[8,64,64]{2,1,0:T(8,128)S(1)} %get-tuple-element.92.refs_2_, ...), custom_call_target="tpu_custom_call" | custom-call | flops 16777216 | bytes 4194304 | tf_op jit(solution)/shard_map/plain_cols/pallas_call | solution.py:548
  146.3 6.8 %all-to-all-start.15 = ((f32[16,32,128]{2,1,0:T(8,128)}), f32[16,32,128]{2,1,0:T(8,128)S(1)}, u32[]{:S(2)}, u32[]{:S(2)}) async-start(f32[16,32,128]{2,1,0:T(8,128)} %copy-done.21), calls=%async_computation.15 | async-start | bytes 524288 | tf_op jit(solution)/shard_map/all_to_all | solution.py:562
  155.7 4.7 convolution_subtract_fusion.1
  160.4 4.3 all-to-all-done.15.refs_0_
  165.4 3.4 all-to-all-start.16
  168.9 3.5 collective-permute-start.5
  175.0 4.9 %all-to-all-done.16.refs_2_.refs_0_ = f32[16,32,128]{2,1,0:T(8,128)S(1)} async-done(((f32[16,32,128]{2,1,0:T(8,128)}), f32[16,32,128]{2,1,0:T(8,128)S(1)}, u32[]{:S(2)}, u32[]{:S(2)}) %all-to-all-start.16) | async-done | bytes 262176 | tf_op jit(solution)/shard_map/all_to_all | solution.py:562
  181.4 8.0 %all-to-all-start.17 = ((f32[32,40,128]{2,1,0:T(8,128)}), f32[32,40,128]{2,1,0:T(8,128)S(1)}, u32[]{:S(2)}, u32[]{:S(2)}) async-start(f32[32,40,128]{2,1,0:T(8,128)} %inner.5), calls=%async_computation.17 | async-start | bytes 1310720 | tf_op jit(solution)/shard_map/all_to_all | solution.py:562
  191.1 13.1 %plain_second.1 = (f32[8,64,64]{2,1,0:T(8,128)S(1)}, f32[1024,128]{1,0:T(8,128)S(1)}, f32[512,128]{1,0:T(8,128)}, f32[2,64,512]{2,1,0:T(8,128)}, f32[2,64,64]{2,1,0:T(8,128)}, /*index=5*/s32[1]{0:T(128)}) custom-call(s32[1]{0:T(128)} %bitcast.6.refs_0_, s32[1]{0:T(128)} %bitcast.7.refs_1_.refs_0_, f32[16,32,128]{2,1,0:T(8,128)S(1)} %all-to-all-done.16.refs_2_.refs_0_, ...), custom_call_target="tpu_custom_call" | custom-call | flops 16777216 | bytes 4194304 | tf_op jit(solution)/shard_map/plain_second/pallas_call | solution.py:548
  213.3 258.4 %conditional.1 = (f32[512,1024]{1,0:T(8,128)S(1)}, f32[2,64,512]{2,1,0:T(8,128)}, f32[2,64,64]{2,1,0:T(8,128)}) conditional(s32[]{:T(128)} %bitcast.11, (f32[512,1024]{1,0:T(8,128)}, s32[1]{0:T(128)}, s32[]{:T(128)}, s32[1]{0:T(128)}, s32[1024,1]{0,1:T(1,128)S(1)}, /*index=5*/()) %tuple.18, (f32[512,128]{1,0:T(8,128)}, f32[1024,128]{1,0:T(8,128)}, ...), branch_computations={%region_0.1_spmd, %region_1.2_spmd} | conditional | flops 2736195584 | bytes 103865152 | solution.py:735
  215.6 21.6 %all_to_all.80 = f32[16,48,128]{2,1,0:T(8,128)S(1)} all-to-all(f32[16,48,128]{2,1,0:T(8,128)S(1)} %get-tuple-element.20), channel_id=1, replica_groups=mesh['row'=32,'col'=16] {'col'}, dimensions={0} | all-to-all | bytes 786432 | tf_op jit(solution)/shard_map/cond/branch_0_fun/all_to_all | solution.py:562
  237.2 8.0 %all-to-all-start.1 = ((f32[32,24,128]{2,1,0:T(8,128)}), f32[32,24,128]{2,1,0:T(8,128)S(1)}, u32[]{:S(2)}, u32[]{:S(2)}) async-start(f32[32,24,128]{2,1,0:T(8,128)} %get-tuple-element.21), calls=%async_computation.1 | async-start | bytes 786432 | tf_op jit(solution)/shard_map/cond/branch_0_fun/all_to_all | solution.py:562
  245.2 14.9 %all-to-all-done.1.refs_1_ = f32[32,24,128]{2,1,0:T(8,128)S(1)} async-done(((f32[32,24,128]{2,1,0:T(8,128)}), f32[32,24,128]{2,1,0:T(8,128)S(1)}, u32[]{:S(2)}, u32[]{:S(2)}) %all-to-all-start.1) | async-done | bytes 393248 | tf_op jit(solution)/shard_map/cond/branch_0_fun/all_to_all | solution.py:562
  260.1 22.0 %all_to_all.81.refs_1_.refs_4_.refs_2_ = f32[16,72,128]{2,1,0:T(8,128)S(1)} all-to-all(f32[16,72,128]{2,1,0:T(8,128)S(1)} %relay.1), channel_id=1, replica_groups=mesh['row'=32,'col'=16] {'col'}, dimensions={0} | all-to-all | bytes 1179648 | tf_op jit(solution)/shard_map/cond/branch_0_fun/all_to_all | solution.py:562
  282.2 4.5 first_once.1
  286.7 3.0 convolution_bitcast_fusion.1
  290.9 5.0 %all-to-all-start.3 = ((f32[32,24,128]{2,1,0:T(8,128)}), f32[32,24,128]{2,1,0:T(8,128)S(1)}, u32[]{:S(2)}, u32[]{:S(2)}) async-start(f32[32,24,128]{2,1,0:T(8,128)} %pad_maximum_fusion), calls=%async_computation.3 | async-start | bytes 786432 | tf_op jit(solution)/shard_map/cond/branch_0_fun/all_to_all | solution.py:562
  295.9 3.7 collective-permute-start
  299.6 8.6 %all-to-all-done.3.refs_0_ = f32[32,24,128]{2,1,0:T(8,128)S(1)} async-done(((f32[32,24,128]{2,1,0:T(8,128)}), f32[32,24,128]{2,1,0:T(8,128)S(1)}, u32[]{:S(2)}, u32[]{:S(2)}) %all-to-all-start.3) | async-done | bytes 393248 | tf_op jit(solution)/shard_map/cond/branch_0_fun/all_to_all | solution.py:562
  309.3 8.4 %all-to-all-start.4 = ((f32[32,72,128]{2,1,0:T(8,128)}), f32[32,72,128]{2,1,0:T(8,128)S(1)}, u32[]{:S(2)}, u32[]{:S(2)}) async-start(f32[32,72,128]{2,1,0:T(8,128)} %get-tuple-element.24), calls=%async_computation.4 | async-start | bytes 2359296 | tf_op jit(solution)/shard_map/cond/branch_0_fun/all_to_all | solution.py:562
  317.8 7.3 %collective-permute-start.1 = (f32[16,128]{1,0:T(8,128)S(1)}, f32[16,128]{1,0:T(8,128)S(1)}, u32[]{:S(2)}, u32[]{:S(2)}) collective-permute-start(f32[16,128]{1,0:T(8,128)S(1)} %get-tuple-element.27), channel_id=1, source_target_pairs={{0,0},{16,1},{32,2},{48,3},{64,4},{80,5},{96,6},{112,7},{128,8},{1... | collective-permute-start | bytes 24584 | tf_op jit(solution)/shard_map/cond/branch_0_fun/ppermute | solution.py:600
  325.1 18.6 %all-to-all-done.4.refs_0_.refs_2_.refs_4_.refs_3_ = f32[32,72,128]{2,1,0:T(8,128)S(1)} async-done(((f32[32,72,128]{2,1,0:T(8,128)}), f32[32,72,128]{2,1,0:T(8,128)S(1)}, u32[]{:S(2)}, u32[]{:S(2)}) %all-to-all-start.4) | async-done | bytes 1179680 | tf_op jit(solution)/shard_map/cond/branch_0_fun/all_to_all | solution.py:562
  347.2 10.4 %all-to-all-start.5 = ((f32[16,40,128]{2,1,0:T(8,128)}), f32[16,40,128]{2,1,0:T(8,128)S(1)}, u32[]{:S(2)}, u32[]{:S(2)}) async-start(f32[16,40,128]{2,1,0:T(8,128)} %inner.3), calls=%async_computation.5 | async-start | bytes 655360 | tf_op jit(solution)/shard_map/cond/branch_0_fun/all_to_all | solution.py:562
  357.7 7.1 %first_factor.1 = (f32[8,64,64]{2,1,0:T(8,128)S(1)}, f32[1024,128]{1,0:T(8,128)S(1)}, f32[512,64]{1,0:T(8,128)S(1)}, f32[64,64]{1,0:T(8,128)S(1)}, s32[1]{0:T(128)}) custom-call(s32[1]{0:T(128)} %get-tuple-element.19.refs_0_, s32[1]{0:T(128)} %get-tuple-element.28.refs_1_.refs_0_, f32[32,72,128]{2,1,0:T(8,128)S(1)} %all-to-all-done.4.refs_0_.refs_2_.refs_4_.refs_3_, ...), custom_call_target="tpu_custom_call" | custom-call | flops 16777216 | bytes 4194304 | tf_op jit(solution)/shard_map/cond/branch_0_fun/first_factor/pallas_call | solution.py:548
  366.3 4.5 all-to-all-done.5.refs_1_
  371.8 4.2 first_cols.1
  376.8 3.4 all-to-all-start.6
  383.4 6.7 %all-to-all-done.6.refs_1_ = f32[16,24,128]{2,1,0:T(8,128)S(1)} async-done(((f32[16,24,128]{2,1,0:T(8,128)}), f32[16,24,128]{2,1,0:T(8,128)S(1)}, u32[]{:S(2)}, u32[]{:S(2)}) %all-to-all-start.6) | async-done | bytes 196640 | tf_op jit(solution)/shard_map/cond/branch_0_fun/all_to_all | solution.py:562
  391.0 4.8 %second_once.1 = (f32[64,64]{1,0:T(8,128)S(1)}, f32[512,64]{1,0:T(8,128)S(1)}, f32[32,8,128]{2,1,0:T(8,128)S(1)}) custom-call(s32[1]{0:T(128)} %get-tuple-element.19.refs_0_, f32[16,24,128]{2,1,0:T(8,128)S(1)} %all-to-all-done.6.refs_1_, f32[16,72,128]{2,1,0:T(8,128)S(1)} %all_to_all.81.refs_1_.refs_4_.refs_2_, f32[512,64]{1,0:T(8,128)S(1)} %copy-done.20, ...), custom_call_target="tpu_custom_call" | custom-call | flops 16777216 | bytes 4194304 | tf_op jit(solution)/shard_map/cond/branch_0_fun/second_once/pallas_call | solution.py:548
  399.9 17.7 %all_to_all.82.refs_0_ = f32[32,24,128]{2,1,0:T(8,128)S(1)} all-to-all(f32[32,24,128]{2,1,0:T(8,128)S(1)} %pad_maximum_fusion.1), channel_id=1, replica_groups=mesh['row'=32,'col'=16] {'row'}, dimensions={0} | all-to-all | bytes 786432 | tf_op jit(solution)/shard_map/cond/branch_0_fun/all_to_all | solution.py:562
  418.4 7.3 %all-to-all-start.8 = ((f32[32,24,128]{2,1,0:T(8,128)}), f32[32,24,128]{2,1,0:T(8,128)S(1)}, u32[]{:S(2)}, u32[]{:S(2)}) async-start(f32[32,24,128]{2,1,0:T(8,128)} %get-tuple-element.39), calls=%async_computation.8 | async-start | bytes 786432 | tf_op jit(solution)/shard_map/cond/branch_0_fun/all_to_all | solution.py:562
  425.7 5.2 %collective-permute-start.2 = (f32[16,128]{1,0:T(8,128)S(1)}, f32[16,128]{1,0:T(8,128)S(1)}, u32[]{:S(2)}, u32[]{:S(2)}) collective-permute-start(f32[16,128]{1,0:T(8,128)S(1)} %get-tuple-element.42), channel_id=1, source_target_pairs={{0,0},{16,1},{32,2},{48,3},{64,4},{80,5},{96,6},{112,7},{128,8},{1... | collective-permute-start | bytes 24584 | tf_op jit(solution)/shard_map/cond/branch_0_fun/ppermute | solution.py:600
  432.6 4.4 collective-permute-done.2.refs_2_
  438.4 9.8 %all-to-all-start.9 = ((f32[16,40,128]{2,1,0:T(8,128)}), f32[16,40,128]{2,1,0:T(8,128)}, u32[]{:S(2)}, u32[]{:S(2)}) async-start(f32[16,40,128]{2,1,0:T(8,128)} %copy-done), calls=%async_computation.9 | async-start | bytes 655360 | tf_op jit(solution)/shard_map/cond/branch_0_fun/all_to_all | solution.py:562
  448.2 3.1 fusion.4
  451.4 9.1 %second_factor.1 = (f32[8,64,64]{2,1,0:T(8,128)S(1)}, f32[1024,128]{1,0:T(8,128)S(1)}, f32[512,128]{1,0:T(8,128)S(1)}, f32[2,64,512]{2,1,0:T(8,128)}, f32[2,64,64]{2,1,0:T(8,128)}) custom-call(s32[1]{0:T(128)} %get-tuple-element.19.refs_0_, s32[1]{0:T(128)} %get-tuple-element.28.refs_1_.refs_0_, f32[32,24,128]{2,1,0:T(8,128)S(1)} %all-to-all-done.8.refs_0_.refs_2_, ...), custom_call_target="tpu_custom_call" | custom-call | flops 16777216 | bytes 4194304 | tf_op jit(solution)/shard_map/cond/branch_0_fun/second_factor/pallas_call | solution.py:548
  467.2 4.3 subtract_subtract_fusion
  (100 shorter events, 61.6 us)
Async XLA Ops:
  29.7 17.4 %all-to-all-start.11 = ((f32[16,48,128]{2,1,0:T(8,128)}), f32[16,48,128]{2,1,0:T(8,128)S(1)}, u32[]{:S(2)}, u32[]{:S(2)}) async-start(f32[16,48,128]{2,1,0:T(8,128)} %broadcast_in_dim.23), calls=%async_computation.11 | async-start | bytes 786432 | tf_op jit(solution)/shard_map/all_to_all | solution.py:562
  51.9 24.6 %all-to-all-start.12 = ((f32[32,24,128]{2,1,0:T(8,128)}), f32[32,24,128]{2,1,0:T(8,128)S(1)}, u32[]{:S(2)}, u32[]{:S(2)}) async-start(f32[32,24,128]{2,1,0:T(8,128)} %pad_maximum_fusion.2), calls=%async_computation.12 | async-start | bytes 786432 | tf_op jit(solution)/shard_map/all_to_all | solution.py:562
  61.5 14.9 %collective-permute-start.3 = (f32[48,128]{1,0:T(8,128)S(1)}, f32[48,128]{1,0:T(8,128)S(1)}, u32[]{:S(2)}, u32[]{:S(2)}) collective-permute-start(f32[48,128]{1,0:T(8,128)S(1)} %slice_bitcast_fusion.1), channel_id=1, source_target_pairs={{0,0},{1,16},{2,32},{3,48},{4,64},{5,80},{6,96},{7,112},{8,128},{9... | collective-permute-start | bytes 73736 | tf_op jit(solution)/shard_map/ppermute | solution.py:620
  77.6 34.0 %all-to-all-start.13 = ((f32[32,72,128]{2,1,0:T(8,128)}), f32[32,72,128]{2,1,0:T(8,128)S(1)}, u32[]{:S(2)}, u32[]{:S(2)}) async-start(f32[32,72,128]{2,1,0:T(8,128)} %get-tuple-element.89), calls=%async_computation.13 | async-start | bytes 2359296 | tf_op jit(solution)/shard_map/all_to_all | solution.py:562
  83.4 28.1 %collective-permute-start.4 = (f32[16,128]{1,0:T(8,128)S(1)}, f32[16,128]{1,0:T(8,128)S(1)}, u32[]{:S(2)}, u32[]{:S(2)}) collective-permute-start(f32[16,128]{1,0:T(8,128)S(1)} %get-tuple-element.91), channel_id=1, source_target_pairs={{0,0},{16,1},{32,2},{48,3},{64,4},{80,5},{96,6},{112,7},{128,8},{1... | collective-permute-start | bytes 24584 | tf_op jit(solution)/shard_map/ppermute | solution.py:600
  112.9 23.2 %all-to-all-start.14 = ((f32[16,40,128]{2,1,0:T(8,128)}), f32[16,40,128]{2,1,0:T(8,128)S(1)}, u32[]{:S(2)}, u32[]{:S(2)}) async-start(f32[16,40,128]{2,1,0:T(8,128)} %plain_inner.1), calls=%async_computation.14 | async-start | bytes 655360 | tf_op jit(solution)/shard_map/all_to_all | solution.py:562
  134.0 0.7 copy-start.13
  134.7 0.6 copy-start.24
  144.8 0.8 copy-start.3
  145.6 0.7 copy-start.21
  146.3 18.4 %all-to-all-start.15 = ((f32[16,32,128]{2,1,0:T(8,128)}), f32[16,32,128]{2,1,0:T(8,128)S(1)}, u32[]{:S(2)}, u32[]{:S(2)}) async-start(f32[16,32,128]{2,1,0:T(8,128)} %copy-done.21), calls=%async_computation.15 | async-start | bytes 524288 | tf_op jit(solution)/shard_map/all_to_all | solution.py:562
  153.1 1.0 copy-start.14
  165.4 14.5 %all-to-all-start.16 = ((f32[16,32,128]{2,1,0:T(8,128)}), f32[16,32,128]{2,1,0:T(8,128)S(1)}, u32[]{:S(2)}, u32[]{:S(2)}) async-start(f32[16,32,128]{2,1,0:T(8,128)} %get-tuple-element.101), calls=%async_computation.16 | async-start | bytes 524288 | tf_op jit(solution)/shard_map/all_to_all | solution.py:562
  168.9 6.2 %collective-permute-start.5 = (f32[16,128]{1,0:T(8,128)S(1)}, f32[16,128]{1,0:T(8,128)S(1)}, u32[]{:S(2)}, u32[]{:S(2)}) collective-permute-start(f32[16,128]{1,0:T(8,128)S(1)} %get-tuple-element.108), channel_id=1, source_target_pairs={{0,0},{1,16},{2,32},{3,48},{4,64},{5,80},{6,96},{7,112},{8,128},{9... | collective-permute-start | bytes 24584 | tf_op jit(solution)/shard_map/ppermute | solution.py:600
  181.4 27.0 %all-to-all-start.17 = ((f32[32,40,128]{2,1,0:T(8,128)}), f32[32,40,128]{2,1,0:T(8,128)S(1)}, u32[]{:S(2)}, u32[]{:S(2)}) async-start(f32[32,40,128]{2,1,0:T(8,128)} %inner.5), calls=%async_computation.17 | async-start | bytes 1310720 | tf_op jit(solution)/shard_map/all_to_all | solution.py:562
  189.3 1.0 copy-start.4
  190.4 0.8 copy-start.25
  204.3 0.8 copy-start.9
  205.1 0.7 copy-start.11
  208.4 1.0 copy-start.10
  209.4 0.9 copy-start.12
  237.2 22.9 %all-to-all-start.1 = ((f32[32,24,128]{2,1,0:T(8,128)}), f32[32,24,128]{2,1,0:T(8,128)S(1)}, u32[]{:S(2)}, u32[]{:S(2)}) async-start(f32[32,24,128]{2,1,0:T(8,128)} %get-tuple-element.21), calls=%async_computation.1 | async-start | bytes 786432 | tf_op jit(solution)/shard_map/cond/branch_0_fun/all_to_all | solution.py:562
  290.9 17.3 %all-to-all-start.3 = ((f32[32,24,128]{2,1,0:T(8,128)}), f32[32,24,128]{2,1,0:T(8,128)S(1)}, u32[]{:S(2)}, u32[]{:S(2)}) async-start(f32[32,24,128]{2,1,0:T(8,128)} %pad_maximum_fusion), calls=%async_computation.3 | async-start | bytes 786432 | tf_op jit(solution)/shard_map/cond/branch_0_fun/all_to_all | solution.py:562
  295.9 12.3 %collective-permute-start = (f32[48,128]{1,0:T(8,128)S(1)}, f32[48,128]{1,0:T(8,128)S(1)}, u32[]{:S(2)}, u32[]{:S(2)}) collective-permute-start(f32[48,128]{1,0:T(8,128)S(1)} %slice_bitcast_fusion.refs_0_), channel_id=1, source_target_pairs={{0,0},{1,16},{2,32},{3,48},{4,64},{5,80},{6,96},{7,112},{8,128},{9... | collective-permute-start | bytes 73736 | tf_op jit(solution)/shard_map/cond/branch_0_fun/ppermute | solution.py:677
  309.3 34.3 %all-to-all-start.4 = ((f32[32,72,128]{2,1,0:T(8,128)}), f32[32,72,128]{2,1,0:T(8,128)S(1)}, u32[]{:S(2)}, u32[]{:S(2)}) async-start(f32[32,72,128]{2,1,0:T(8,128)} %get-tuple-element.24), calls=%async_computation.4 | async-start | bytes 2359296 | tf_op jit(solution)/shard_map/cond/branch_0_fun/all_to_all | solution.py:562
  317.8 28.1 %collective-permute-start.1 = (f32[16,128]{1,0:T(8,128)S(1)}, f32[16,128]{1,0:T(8,128)S(1)}, u32[]{:S(2)}, u32[]{:S(2)}) collective-permute-start(f32[16,128]{1,0:T(8,128)S(1)} %get-tuple-element.27), channel_id=1, source_target_pairs={{0,0},{16,1},{32,2},{48,3},{64,4},{80,5},{96,6},{112,7},{128,8},{1... | collective-permute-start | bytes 24584 | tf_op jit(solution)/shard_map/cond/branch_0_fun/ppermute | solution.py:600
  347.2 23.5 %all-to-all-start.5 = ((f32[16,40,128]{2,1,0:T(8,128)}), f32[16,40,128]{2,1,0:T(8,128)S(1)}, u32[]{:S(2)}, u32[]{:S(2)}) async-start(f32[16,40,128]{2,1,0:T(8,128)} %inner.3), calls=%async_computation.5 | async-start | bytes 655360 | tf_op jit(solution)/shard_map/cond/branch_0_fun/all_to_all | solution.py:562
  364.7 0.8 copy-start.6
  365.6 0.7 copy-start.22
  370.7 1.0 copy-start.7
  376.0 0.8 copy-start.8
  376.8 13.2 %all-to-all-start.6 = ((f32[16,24,128]{2,1,0:T(8,128)}), f32[16,24,128]{2,1,0:T(8,128)S(1)}, u32[]{:S(2)}, u32[]{:S(2)}) async-start(f32[16,24,128]{2,1,0:T(8,128)} %get-tuple-element.35), calls=%async_computation.6 | async-start | bytes 393216 | tf_op jit(solution)/shard_map/cond/branch_0_fun/all_to_all | solution.py:562
  380.3 1.0 copy-start.23
  382.7 0.7 copy-start.19
  390.0 1.0 copy-start.20
  398.8 0.7 copy-start.1
  418.4 18.7 %all-to-all-start.8 = ((f32[32,24,128]{2,1,0:T(8,128)}), f32[32,24,128]{2,1,0:T(8,128)S(1)}, u32[]{:S(2)}, u32[]{:S(2)}) async-start(f32[32,24,128]{2,1,0:T(8,128)} %get-tuple-element.39), calls=%async_computation.8 | async-start | bytes 786432 | tf_op jit(solution)/shard_map/cond/branch_0_fun/all_to_all | solution.py:562
  425.7 11.3 %collective-permute-start.2 = (f32[16,128]{1,0:T(8,128)S(1)}, f32[16,128]{1,0:T(8,128)S(1)}, u32[]{:S(2)}, u32[]{:S(2)}) collective-permute-start(f32[16,128]{1,0:T(8,128)S(1)} %get-tuple-element.42), channel_id=1, source_target_pairs={{0,0},{16,1},{32,2},{48,3},{64,4},{80,5},{96,6},{112,7},{128,8},{1... | collective-permute-start | bytes 24584 | tf_op jit(solution)/shard_map/cond/branch_0_fun/ppermute | solution.py:600
  437.6 0.7 copy-start
  438.4 24.3 %all-to-all-start.9 = ((f32[16,40,128]{2,1,0:T(8,128)}), f32[16,40,128]{2,1,0:T(8,128)}, u32[]{:S(2)}, u32[]{:S(2)}) async-start(f32[16,40,128]{2,1,0:T(8,128)} %copy-done), calls=%async_computation.9 | async-start | bytes 655360 | tf_op jit(solution)/shard_map/cond/branch_0_fun/all_to_all | solution.py:562
  448.2 3.1 copy-start.2
  460.5 0.8 copy-start.5
  461.3 0.7 copy-start.15
  462.0 0.7 copy-start.17
  462.7 1.0 copy-start.16
  463.7 0.9 copy-start.18
  471.7 1.3 copy-start.26

commit v3 on v1

--- a/solution.py
+++ b/solution.py
@@ -321,42 +321,31 @@
     return jnp.concatenate([vec[:start], top, vec[start + NB :]], axis=0)
 
 
-def half_core(small_ref, inner):
-    coef = small_ref[COEF]
-    factor = small_ref[FACTOR]
-    inner = small_ref[INNER] + tn(coef, nn(inner, coef))
+def half_core(coef, factor, known, got):
+    inner = known + tn(coef, nn(got, coef))
     return 0.5 * tn(factor, nn(inner, factor))
 
 
-def first_factor(near, chunk, half, at, row, col, gathered_ref, once_c, once_r, outs):
-    small_ref, state_ref, vec_ref, factor_ref, fine_ref = outs
+def first_factor(near, chunk, half, at, col, gathered_ref, once_c, outs):
+    small_ref, state_ref, fine_ref = outs
     gram, image_top, top, next_top, _, _ = get_pairs(gathered_ref, half, 3)
     pick, coef, pick_t, coef_t, fine = factor_small(
         near, gram, top, next_top, image_top, small_ref
     )
     fine_ref[0] = jnp.where(fine, 1, 0)
-    factor_ref[...] = small_ref[FACTOR]
-    vec_ref[...] = vectors_of(once_r, row, NB, pick, coef)
     following = pair_raw(gathered_ref, chunk, at)[:, NB:]
     image = unfold(gathered_ref[:, :half, :])
     vec = vectors_of(once_c, col, NB, pick, coef)
     state_ref[...] = beside(vec, nn(following, pick_t) - nn(image, coef_t))
 
 
-def first_factor_kernel(
-    chunk, half, at, row_ref, col_ref, gathered_ref, once_c_ref, once_r_ref, *outs
-):
-    first_factor(
-        True, chunk, half, at, row_ref[0], col_ref[0], gathered_ref,
-        once_c_ref[...], once_r_ref[...], outs,
-    )
-
-
-def plain_factor_kernel(chunk, half, at, row_ref, col_ref, gathered_ref, panel_r_ref, *outs):
+def first_factor_kernel(chunk, half, at, col_ref, gathered_ref, once_c_ref, *outs):
+    first_factor(True, chunk, half, at, col_ref[0], gathered_ref, once_c_ref[...], outs)
+
+
+def plain_factor_kernel(chunk, half, at, col_ref, gathered_ref, *outs):
     panel = below(pair_raw(gathered_ref, chunk, at)[:, :NB], col_ref[0], NB)
-    first_factor(
-        False, chunk, half, at, row_ref[0], col_ref[0], gathered_ref, panel, panel_r_ref[...], outs
-    )
+    first_factor(False, chunk, half, at, col_ref[0], gathered_ref, panel, outs)
 
 
 def second_panel(following, vec, wide, wide_top, lower, index):
@@ -366,7 +355,8 @@
 def first_cols(
     chunk, at, index, got_ref, small_ref, state_ref, raw_ref, pair_ref, panel_ref, tops_ref
 ):
-    half = half_core(small_ref, unpack_symmetric(jnp.sum(got_ref[:, :PACKED, :], axis=0)))
+    got = unpack_symmetric(jnp.sum(got_ref[:, :PACKED, :], axis=0))
+    half = half_core(small_ref[COEF], small_ref[FACTOR], small_ref[INNER], got)
     lower = small_ref[LOWER]
     wide_top = small_ref[WIDE] - nn(lower, half)
     tops_ref[0] = half
@@ -376,7 +366,8 @@
     pair_ref[...] = beside(wide, vec)
     following = pair_raw(raw_ref, chunk, at)[:, NB:]
     panel = second_panel(following, vec, wide, wide_top, lower, index)
-    panel_ref[...] = panel
+    spare = jnp.zeros((panel.shape[0] - NB, NB), jnp.float32)
+    panel_ref[...] = beside(panel, jnp.concatenate([small_ref[FACTOR], spare], axis=0))
     return panel, vec, wide
 
 
@@ -407,21 +398,21 @@
 
 
 def first_rows_kernel(
-    chunk, row_ref, got_ref, small_ref, vec_ref, raw_ref, tops_ref, pair_ref, panel_ref
+    chunk, row_ref, got_ref, small_ref, once_ref, raw_ref, tops_ref, pair_ref, panel_ref
 ):
     image = unfold(got_ref[:, PACKED:, :])
     following = pair_raw(raw_ref, chunk)[:, NB:]
-    vec = vec_ref[...]
+    vec = vectors_of(once_ref[...], row_ref[0], NB, small_ref[PICK], small_ref[COEF])
     wide = nn(following, small_ref[PICK_T]) - nn(image, small_ref[COEF_T]) - nn(vec, tops_ref[0])
     pair_ref[...] = beside(vec, wide)
     panel_ref[...] = second_panel(following, vec, wide, tops_ref[1], small_ref[LOWER], row_ref[0])
 
 
-def second_small(near, half, old_half, gathered_ref, old_ref, factor_ref, small_ref, factors_ref):
+def second_small(near, half, gathered_ref, old_ref, panel_ref, small_ref, factors_ref):
     gram, image_top, vec_dot, wide_dot, top, vec_top, wide_top, _ = get_pairs(
         gathered_ref, half, 4
     )
-    last_top = get_pairs(old_ref, old_half, 3)[4]
+    last_top = get_pairs(old_ref, half, 3)[4]
     image_top = image_top - nn(vec_top, wide_dot) - nn(wide_top, vec_dot)
     crossed = nt(vec_top, wide_top)
     next_top = last_top - crossed - crossed.T
@@ -430,7 +421,7 @@
     )
     crossed = tn(nn(vec_dot, coef), nn(wide_dot, coef))
     small_ref[INNER] -= crossed + crossed.T
-    factors_ref[0] = factor_ref[...]
+    factors_ref[0] = panel_ref[:NB, NB:]
     factors_ref[1] = small_ref[FACTOR]
     vec_dots = nn(wide_dot, coef_t) - tn(wide_top, pick_t)
     wide_dots = nn(vec_dot, coef_t) - tn(vec_top, pick_t)
@@ -439,11 +430,11 @@
 
 def second_factor_kernel(
     chunk, half, at, row_ref, col_ref, gathered_ref, old_ref, raw_r_ref,
-    once_c_ref, once_r_ref, pair_c_ref, pair_r_ref, factor_ref,
-    small_ref, right_ref, state_ref, vectors_ref, factors_ref,
+    panel_c_ref, once_c_ref, once_r_ref, pair_c_ref, pair_r_ref,
+    right_ref, state_ref, vectors_ref, factors_ref, small_ref,
 ):
     pick, coef, pick_t, coef_t, vec_dots, wide_dots, _ = second_small(
-        True, half, half, gathered_ref, old_ref, factor_ref, small_ref, factors_ref
+        True, half, gathered_ref, old_ref, panel_c_ref, small_ref, factors_ref
     )
     new = vectors_of(once_r_ref[...], row_ref[0], 2 * NB, pick, coef)
     vec = pair_r_ref[:, :NB]
@@ -451,7 +442,7 @@
     vectors_ref[1] = new.T
     part = nn(last_raw(raw_r_ref, chunk), pick_t)
     part += nn(vec, vec_dots) + nn(pair_r_ref[:, NB:], wide_dots)
-    state_ref[...] = beside(new, part)
+    state_ref[...] = with_smalls(beside(new, part), small_ref)
     new = vectors_of(once_c_ref[...], col_ref[0], 2 * NB, pick, coef)
     part = nn(last_raw(old_ref, chunk, at), pick_t) - nn(unfold(gathered_ref[:, :half, :]), coef_t)
     part += nn(pair_c_ref[:, NB:], vec_dots) + nn(pair_c_ref[:, :NB], wide_dots)
@@ -460,11 +451,11 @@
 
 def plain_second_kernel(
     chunk, half, at, row_ref, col_ref, gathered_ref, old_ref, raw_r_ref,
-    panel_c_ref, panel_r_ref, pair_c_ref, pair_r_ref, factor_ref,
-    small_ref, state_ref, left_ref, vectors_ref, factors_ref, fine_ref,
+    panel_c_ref, panel_r_ref, pair_c_ref, pair_r_ref,
+    state_ref, left_ref, vectors_ref, factors_ref, fine_ref, small_ref,
 ):
     pick, coef, pick_t, coef_t, vec_dots, wide_dots, fine = second_small(
-        False, half, half, gathered_ref, old_ref, factor_ref, small_ref, factors_ref
+        False, half, gathered_ref, old_ref, panel_c_ref, small_ref, factors_ref
     )
     fine_ref[0] = jnp.where(fine, 1, 0)
     new = vectors_of(panel_r_ref[...], row_ref[0], 2 * NB, pick, coef)
@@ -474,21 +465,31 @@
     part = nn(last_raw(raw_r_ref, chunk), pick_t) - nn(unfold(gathered_ref[:, :half, :]), coef_t)
     part += nn(vec, vec_dots) + nn(pair_r_ref[:, NB:], wide_dots)
     left_ref[...] = beside(part, new)
-    new = vectors_of(panel_c_ref[...], col_ref[0], 2 * NB, pick, coef)
+    new = vectors_of(panel_c_ref[:, :NB], col_ref[0], 2 * NB, pick, coef)
     part = nn(last_raw(old_ref, chunk, at), pick_t)
     part += nn(pair_c_ref[:, NB:], vec_dots) + nn(pair_c_ref[:, :NB], wide_dots)
-    state_ref[...] = beside(new, part)
-
-
-def last_kernel(got_ref, small_ref, state_ref, out_ref):
-    half = half_core(small_ref, unpack_symmetric(jnp.sum(got_ref[:, :PACKED, :], axis=0)))
-    new = state_ref[:, :NB]
+    state_ref[...] = with_smalls(beside(new, part), small_ref)
+
+
+def with_smalls(state, small_ref):
+    upper = beside(small_ref[COEF], small_ref[FACTOR])
+    lower = beside(small_ref[INNER], small_ref[COEF_T])
+    return jnp.concatenate([state, upper, lower], axis=0)
+
+
+def last_kernel(got_ref, state_ref, out_ref):
+    tall = out_ref.shape[0]
+    coef, factor = state_ref[tall : tall + NB, :NB], state_ref[tall : tall + NB, NB:]
+    inner, coef_t = state_ref[tall + NB :, :NB], state_ref[tall + NB :, NB:]
+    got = unpack_symmetric(jnp.sum(got_ref[:, :PACKED, :], axis=0))
+    half = half_core(coef, factor, inner, got)
+    new = state_ref[:tall, :NB]
     image = unfold(got_ref[:, PACKED:, :])
-    wide = state_ref[:, NB:] - nn(image, small_ref[COEF_T]) - nn(new, half + half.T)
+    wide = state_ref[:tall, NB:] - nn(image, coef_t) - nn(new, half + half.T)
     out_ref[...] = beside(new, wide)
 
 
-def call(kernel, name, outs, *args, statics=(), scalars=0, flag=False):
+def call(kernel, name, outs, *args, statics=(), scalars=0, flag=False, small=False):
     in_smem = pl.BlockSpec(memory_space=pltpu.SMEM)
     in_vmem = pl.BlockSpec(memory_space=pltpu.VMEM)
     out_shape = [jax.ShapeDtypeStruct(shape, jnp.float32) for shape in outs]
@@ -502,6 +503,7 @@
         in_specs=[in_smem if k < scalars else in_vmem for k in range(len(args))],
         out_specs=out_specs,
         compiler_params=pltpu.CompilerParams(vmem_limit_bytes=16 << 20),
+        scratch_shapes=[pltpu.VMEM((8, NB, NB), jnp.float32)] if small else [],
         cost_estimate=pl.CostEstimate(flops=1 << 24, bytes_accessed=1 << 22, transcendentals=0),
         name=name,
     )(*args)
@@ -540,14 +542,14 @@
         def few(peers):
             return -(-4 * (NB // peers) // 8) * 8
 
-        def image_round(mine, axis, targets, extra=()):
-            got = swap(mine, axis)
+        def image_round(mine, axis, targets, extra=(), beside=()):
+            got, *beside = lax.optimization_barrier((swap(mine, axis), *beside))
             rows = got.shape[1] + sum(x.shape[0] for x in extra)
             blocks, image_chunk = call(
                 sum_with_kernel if extra else sum_kernel, "sum_blocks",
                 [(got.shape[0], rows, 2 * NB), (half, 2 * NB)], got, *extra,
             )
-            return swap(blocks, axis), lax.ppermute(image_chunk, ("row", "col"), targets)
+            return swap(blocks, axis), lax.ppermute(image_chunk, ("row", "col"), targets), *beside
 
         def image_blocks(once_r, smalls):
             return jnp.concatenate([fold(tn(matrix, once_r), chunk), smalls], axis=1)
@@ -558,10 +560,14 @@
         block_c = (nr, PACKED + half, 2 * NB)
 
         def plain():
-            raw = call(
-                plain_start_kernel, "plain_start", [(nc, raw_rows, 2 * NB)],
-                matrix[:, : 4 * NB], statics=(chunk,),
-            )
+            raw = pl.pallas_call(
+                functools.partial(plain_start_kernel, chunk),
+                grid=(1,),
+                in_specs=[pl.BlockSpec((rows_here, 4 * NB), lambda _: (0, 0))],
+                out_specs=pl.BlockSpec((nc, raw_rows, 2 * NB), lambda _: (0, 0, 0)),
+                out_shape=jax.ShapeDtypeStruct((nc, raw_rows, 2 * NB), jnp.float32),
+                name="plain_start",
+            )(matrix)
             raw_chunk = swap(raw, "col")[0]
             raw_chunk_c = lax.ppermute(raw_chunk, ("row", "col"), to_cols)
             raw_r = swap(jnp.broadcast_to(raw_chunk[None], raw.shape), "col")
@@ -577,32 +583,40 @@
                 my_col, gathered, image_chunk, statics=(chunk, at), scalars=1,
             )
             got = swap(inners, "col")
-            small_one, state_c, vec_r, factor_one, fine_one = call(
-                plain_factor_kernel, "plain_factor", [(8,) + square, pair_shape_c, tall_r, square],
-                my_row, my_col, gathered, first_r, statics=(chunk, half, at), scalars=2, flag=True,
+            small_one, state_c, fine_one = call(
+                plain_factor_kernel, "plain_factor", [(8,) + square, pair_shape_c],
+                my_col, gathered, statics=(chunk, half, at), scalars=1, flag=True,
             )
             pair_c, panel_c, tops, blocks = call(
                 plain_cols_kernel, "plain_cols",
-                [pair_shape_c, tall_c, (2,) + square, (nc, half + few(nc), 2 * NB)],
+                [pair_shape_c, pair_shape_c, (2,) + square, (nc, half + few(nc), 2 * NB)],
                 my_col, got, small_one, state_c, gathered, matrix, statics=(chunk, at), scalars=1,
             )
             pair_r, panel_r = call(
                 first_rows_kernel, "first_rows", [pair_shape_r, tall_r],
-                my_row, got, small_one, vec_r, raw_r, tops, statics=(chunk,), scalars=1,
-            )
+                my_row, got, small_one, first_r, raw_r, tops, statics=(chunk,), scalars=1,
+            )
+            current = matrix - nt(pair_r, pair_c)
             old = gathered
-            gathered, image_chunk = image_round(blocks, "col", to_cols)
-            current = matrix - nt(pair_r, pair_c)
-            gathered, current = lax.optimization_barrier((gathered, current))
-            inners = call(inner_kernel, "inner", [block_c], gathered, panel_r, image_chunk)
+            gathered, image_chunk, current, pair_r, panel_r = image_round(
+                blocks, "col", to_cols, beside=(current, pair_r, panel_r)
+            )
+            inners = call(
+                inner_kernel, "inner", [block_c], gathered, panel_r, image_chunk
+            )
             got = swap(inners, "row")
-            small_two, state_c, left, vectors, factors, fine_two = call(
+            state_c, left, vectors, factors, fine_two = call(
                 plain_second_kernel, "plain_second",
-                [(8,) + square, pair_shape_c, pair_shape_r, (2, NB, rows_here), (2,) + square],
+                [
+                    (cols_here + 2 * NB, 2 * NB), pair_shape_r, (2, NB, rows_here), (2,) + square
+                ],
                 my_row, my_col, gathered, old, raw_r, panel_c, panel_r,
-                pair_c, pair_r, factor_one, statics=(chunk, half, at), scalars=2, flag=True,
-            )
-            right = call(last_kernel, "last", [pair_shape_c], got, small_two, state_c)
+                pair_c, pair_r, statics=(chunk, half, at), scalars=2, flag=True,
+                small=True,
+            )
+            right = call(
+                last_kernel, "last", [pair_shape_c], got, state_c
+            )
             return (current, left, right, vectors, factors), (fine_one + fine_two)[0] == 2
 
         def careful():
@@ -629,20 +643,19 @@
             once_c = nt(jnp.where(col_place >= NB, first_c, 0.0), root)
             inners = call(inner_kernel, "inner", [block_r], gathered, once_c, image_chunk_r)
             got = swap(inners, "col")
-            small_one, state_c, vec_r, factor_one, _ = call(
-                first_factor_kernel, "first_factor", [(8,) + square, pair_shape_c, tall_r, square],
-                my_row, my_col, gathered, once_c, once_r,
-                statics=(chunk, half, at), scalars=2, flag=True,
+            small_one, state_c, _ = call(
+                first_factor_kernel, "first_factor", [(8,) + square, pair_shape_c],
+                my_col, gathered, once_c, statics=(chunk, half, at), scalars=1, flag=True,
             )
             pair_c, panel_c, tops, grams = call(
                 first_cols_kernel, "first_cols",
-                [pair_shape_c, tall_c, (2,) + square, (nc, PACKED, 2 * NB)],
+                [pair_shape_c, pair_shape_c, (2,) + square, (nc, PACKED, 2 * NB)],
                 my_col, got, small_one, state_c, gathered, statics=(chunk, at), scalars=1,
             )
             grams = swap(grams, "col")
             pair_r, panel_r = call(
                 first_rows_kernel, "first_rows", [pair_shape_r, tall_r],
-                my_row, got, small_one, vec_r, raw_r, tops, statics=(chunk,), scalars=1,
+                my_row, got, small_one, once_r, raw_r, tops, statics=(chunk,), scalars=1,
             )
 
             root, once_r, smalls = call(
@@ -651,17 +664,19 @@
             )
             old = gathered
             gathered, image_chunk_r = image_round(image_blocks(once_r, smalls), "row", to_rows)
-            once_c = nt(panel_c, root)
+            once_c = nt(panel_c[:, :NB], root)
             current = matrix - nt(pair_r, pair_c)
             inners = call(inner_kernel, "inner", [block_r], gathered, once_c, image_chunk_r)
             got = swap(inners, "col")
-            small_two, right, state_r, vectors, factors = call(
+            right, state_r, vectors, factors = call(
                 second_factor_kernel, "second_factor",
-                [(8,) + square, pair_shape_c, pair_shape_r, (2, NB, rows_here), (2,) + square],
-                my_row, my_col, gathered, old, raw_r, once_c, once_r, pair_c, pair_r, factor_one,
-                statics=(chunk, half, at), scalars=2,
-            )
-            left = call(last_kernel, "last", [pair_shape_r], got, small_two, state_r)
+                [
+                    pair_shape_c, (rows_here + 2 * NB, 2 * NB), (2, NB, rows_here), (2,) + square
+                ],
+                my_row, my_col, gathered, old, raw_r, panel_c, once_c, once_r, pair_c, pair_r,
+                statics=(chunk, half, at), scalars=2, small=True,
+            )
+            left = call(last_kernel, "last", [pair_shape_r], got, state_r)
             return current - nt(left, right), vectors, factors
 
         ready, fine = plain()

time: 476 us -> 475 us (level)
  waiting for transfers between devices: 111 us -> 129 us
  blocking collectives: 104 us -> 89.4 us
  local copies, waits for them, and re-layouts: 25.2 us -> 18 us
    all_to_all x13 -> x14, waiting for transfers between devices: 65.6 us -> 98 us  [swap(): return lax.all_to_all(x, axis, 0, 0)]
    all_to_all x5 -> x4, blocking collectives: 104 us -> 89.4 us  [swap(): return lax.all_to_all(x, axis, 0, 0)]
    ppermute x1, waiting for transfers between devices: 9.38 us -> 0.01 us  [plain(): raw_chunk_c = lax.ppermute(raw_chunk, ('row', 'col'), to_cols)]
    ppermute x1, waiting for transfers between devices: 8.62 us -> 0.02 us  [careful(): raw_chunk_c = lax.ppermute(raw_chunk, ('row', 'col'), to_cols)]
    cond x30 -> x24, local copies, waits for them, and re-layouts: 11.5 us -> 8.2 us
    unnamed x26 -> x16, local copies, waits for them, and re-layouts: 10 us -> 7.23 us
    all_to_all x13 -> x14, starting transfers between devices: 95.3 us -> 93.5 us  [swap(): return lax.all_to_all(x, axis, 0, 0)]
    pallas_call x24 -> x23, Pallas kernels: 78 us -> 79.2 us  [call(): pl.pallas_call(functools.partial(kernel, *statics), out_shape=out_shape,...]
  transfers between devices with their start and end apart: 19 -> 20, of which waited for: 15 -> 16; matrix products, arithmetic and copies ran while one was open for 2% -> 2% of each run, Pallas kernels for 9% -> 8%
where the time goes in v3:
time: 475 us; the launch traced here: 469 us
  waiting for transfers between devices  129 us (27%)
  starting transfers between devices  123 us (26%)
  blocking collectives  89.4 us (19%)
  Pallas kernels  81 us (17%)
  matrix products  23.3 us (5%)
  local copies, waits for them, and re-layouts  18 us (4%)
    all_to_all x14, waiting for transfers between devices, swap(): return lax.all_to_all(x, axis, 0, 0)  98 us
    all_to_all x14, starting transfers between devices, swap(): return lax.all_to_all(x, axis, 0, 0)  93.5 us
    all_to_all x4, blocking collectives, swap(): return lax.all_to_all(x, axis, 0, 0)  89.4 us
    pallas_call x23, Pallas kernels, call(): pl.pallas_call(functools.partial(kernel, *statics), out_shape=out_shape,...  79.2 us
    ppermute x4, waiting for transfers between devices, image_round(): lax.ppermute(image_chunk, ('row', 'col'), targets)  31 us
    ppermute x4, starting transfers between devices, image_round(): lax.ppermute(image_chunk, ('row', 'col'), targets)  22.6 us
    dot_general x5, matrix products, nt(): lax.dot_general(a, b, (((1,), (1,)), ((), ())), precision=precise, prefer...  14.3 us
  transfers between devices with their start and end apart: 20, of which 16 were waited for; matrix products, arithmetic and copies ran while one was open for 2% of the time, Pallas kernels for 8%

profile of v3, /device:TPU:1, one launch (start us, length us, event | category | flops | bytes accessed | tf_op | source)
XLA Modules:
  0.0 468.5 jit_solution(15091230785633190336)
XLA Ops:
  2.5 26.4 %all_to_all.83 = f32[16,48,128]{2,1,0:T(8,128)S(1)} all-to-all(f32[16,48,128]{2,1,0:T(8,128)} %plain_start.1), channel_id=1, replica_groups=mesh['row'=32,'col'=16] {'col'}, dimensions={0} | all-to-all | bytes 786432 | tf_op jit(solution)/shard_map/all_to_all | solution.py:514
  29.7 3.5 all-to-all-start.11
  33.1 14.0 %all-to-all-done.11.raw_ref.raw_r_ref = f32[16,48,128]{2,1,0:T(8,128)S(1)} async-done(((f32[16,48,128]{2,1,0:T(8,128)}), f32[16,48,128]{2,1,0:T(8,128)S(1)}, u32[]{:S(2)}, u32[]{:S(2)}) %all-to-all-start.11) | async-done | bytes 393248 | tf_op jit(solution)/shard_map/all_to_all | solution.py:514
  51.9 9.7 %all-to-all-start.12 = ((f32[32,24,128]{2,1,0:T(8,128)}), f32[32,24,128]{2,1,0:T(8,128)S(1)}, u32[]{:S(2)}, u32[]{:S(2)}) async-start(f32[32,24,128]{2,1,0:T(8,128)} %pad_maximum_fusion.2), calls=%async_computation.12 | async-start | bytes 786432 | tf_op jit(solution)/shard_map/all_to_all | solution.py:514
  64.4 12.1 %all-to-all-done.12.got_ref = f32[32,24,128]{2,1,0:T(8,128)S(1)} async-done(((f32[32,24,128]{2,1,0:T(8,128)}), f32[32,24,128]{2,1,0:T(8,128)S(1)}, u32[]{:S(2)}, u32[]{:S(2)}) %all-to-all-start.12) | async-done | bytes 393248 | tf_op jit(solution)/shard_map/all_to_all | solution.py:514
  77.6 5.8 %all-to-all-start.13 = ((f32[32,72,128]{2,1,0:T(8,128)}), f32[32,72,128]{2,1,0:T(8,128)S(1)}, u32[]{:S(2)}, u32[]{:S(2)}) async-start(f32[32,72,128]{2,1,0:T(8,128)} %get-tuple-element.83), calls=%async_computation.13 | async-start | bytes 2359296 | tf_op jit(solution)/shard_map/all_to_all | solution.py:514
  83.4 6.4 %collective-permute-start.4 = (f32[16,128]{1,0:T(8,128)S(1)}, f32[16,128]{1,0:T(8,128)S(1)}, u32[]{:S(2)}, u32[]{:S(2)}) collective-permute-start(f32[16,128]{1,0:T(8,128)S(1)} %get-tuple-element.85), channel_id=1, source_target_pairs={{0,0},{16,1},{32,2},{48,3},{64,4},{80,5},{96,6},{112,7},{128,8},{1... | collective-permute-start | bytes 24584 | tf_op jit(solution)/shard_map/ppermute | solution.py:552
  89.8 21.7 %collective-permute-done.4.chunk_ref = f32[16,128]{1,0:T(8,128)S(1)} collective-permute-done((f32[16,128]{1,0:T(8,128)S(1)}, f32[16,128]{1,0:T(8,128)S(1)}, u32[]{:S(2)}, u32[]{:S(2)}) %collective-permute-start.4) | collective-permute-done | bytes 8224 | tf_op jit(solution)/shard_map/ppermute | solution.py:552
  112.9 10.2 %all-to-all-start.14 = ((f32[16,40,128]{2,1,0:T(8,128)}), f32[16,40,128]{2,1,0:T(8,128)S(1)}, u32[]{:S(2)}, u32[]{:S(2)}) async-start(f32[16,40,128]{2,1,0:T(8,128)} %plain_inner.1), calls=%async_computation.14 | async-start | bytes 655360 | tf_op jit(solution)/shard_map/all_to_all | solution.py:514
  123.1 9.3 %plain_factor.1 = (f32[8,64,64]{2,1,0:T(8,128)S(1)}, f32[1024,128]{1,0:T(8,128)S(1)}, s32[1]{0:T(128)}) custom-call(s32[1]{0:T(128)} %bitcast.6.col_ref, f32[32,72,128]{2,1,0:T(8,128)S(1)} %all-to-all-done.13.gathered_ref.raw_ref.old_ref), custom_call_target="tpu_custom_call" | custom-call | flops 16777216 | bytes 4194304 | tf_op jit(solution)/shard_map/plain_factor/pallas_call | solution.py:500
  132.5 3.6 all-to-all-done.14.got_ref
  136.1 8.2 %plain_cols.1 = (f32[1024,128]{1,0:T(8,128)S(1)}, f32[1024,128]{1,0:T(8,128)S(1)}, f32[2,64,64]{2,1,0:T(8,128)S(1)}, f32[16,32,128]{2,1,0:T(8,128)S(1)}) custom-call(s32[1]{0:T(128)} %bitcast.6.col_ref, f32[16,40,128]{2,1,0:T(8,128)S(1)} %all-to-all-done.14.got_ref, f32[8,64,64]{2,1,0:T(8,128)S(1)} %get-tuple-element.86.small_ref, ...), custom_call_target="tpu_custom_call" | custom-call | flops 16777216 | bytes 4194304 | tf_op jit(solution)/shard_map/plain_cols/pallas_call | solution.py:500
  146.5 4.3 all-to-all-start.15
  153.3 4.7 %convolution_subtract_fusion.1 = f32[512,1024]{1,0:T(8,128)} fusion(f32[512,1024]{1,0:T(8,128)} %matrix_ref.3, f32[512,128]{1,0:T(8,128)S(1)} %get-tuple-element.97.pair_r_ref, f32[1024,128]{1,0:T(8,128)S(1)} %get-tuple-element.91.pair_c_ref), kind=kOutput, calls=%fused_computation.11 | convolution fusion | flops 805830656 | bytes 4980736 | tf_op jit(solution)/shard_map/dot_general | solution.py:27
  158.0 4.1 all-to-all-done.15.got_ref
  163.8 3.4 all-to-all-start.16
  167.2 3.7 collective-permute-start.5
  173.4 5.5 %all-to-all-done.16.gathered_ref = f32[16,32,128]{2,1,0:T(8,128)S(1)} async-done(((f32[16,32,128]{2,1,0:T(8,128)}), f32[16,32,128]{2,1,0:T(8,128)S(1)}, u32[]{:S(2)}, u32[]{:S(2)}) %all-to-all-start.16) | async-done | bytes 262176 | tf_op jit(solution)/shard_map/all_to_all | solution.py:514
  180.2 7.2 %all-to-all-start.17 = ((f32[32,40,128]{2,1,0:T(8,128)}), f32[32,40,128]{2,1,0:T(8,128)S(1)}, u32[]{:S(2)}, u32[]{:S(2)}) async-start(f32[32,40,128]{2,1,0:T(8,128)} %inner.5), calls=%async_computation.17 | async-start | bytes 1310720 | tf_op jit(solution)/shard_map/all_to_all | solution.py:514
  188.4 11.8 %plain_second.1 = (f32[1152,128]{1,0:T(8,128)S(1)}, f32[512,128]{1,0:T(8,128)}, f32[2,64,512]{2,1,0:T(8,128)}, f32[2,64,64]{2,1,0:T(8,128)}, s32[1]{0:T(128)}) custom-call(s32[1]{0:T(128)} %bitcast.7.index_ref.row_ref, s32[1]{0:T(128)} %bitcast.6.col_ref, f32[16,32,128]{2,1,0:T(8,128)S(1)} %all-to-all-done.16.gathered_ref, ...), custom_call_target="tpu_custom_call" | custom-call | flops 16777216 | bytes 4194304 | tf_op jit(solution)/shard_map/plain_second/pallas_call | solution.py:500
  202.3 3.7 all-to-all-done.17.got_ref
  210.0 256.9 %conditional.1 = (f32[512,1024]{1,0:T(8,128)S(1)}, f32[2,64,512]{2,1,0:T(8,128)}, f32[2,64,64]{2,1,0:T(8,128)}) conditional(s32[]{:T(128)} %bitcast.11, (f32[512,1024]{1,0:T(8,128)}, s32[1]{0:T(128)}, s32[]{:T(128)}, s32[1]{0:T(128)}, s32[1024,1]{0,1:T(1,128)S(1)}, /*index=5*/()) %tuple.18, (f32[512,128]{1,0:T(8,128)}, f32[1024,128]{1,0:T(8,128)}, ...), branch_computations={%region_0.1_spmd, %region_1.2_spmd} | conditional | flops 2736195584 | bytes 105700080 | solution.py:687
  212.3 22.2 %all_to_all.80 = f32[16,48,128]{2,1,0:T(8,128)S(1)} all-to-all(f32[16,48,128]{2,1,0:T(8,128)S(1)} %get-tuple-element.20), channel_id=1, replica_groups=mesh['row'=32,'col'=16] {'col'}, dimensions={0} | all-to-all | bytes 786432 | tf_op jit(solution)/shard_map/cond/branch_0_fun/all_to_all | solution.py:514
  234.5 5.2 %all-to-all-start.1 = ((f32[32,24,128]{2,1,0:T(8,128)}), f32[32,24,128]{2,1,0:T(8,128)S(1)}, u32[]{:S(2)}, u32[]{:S(2)}) async-start(f32[32,24,128]{2,1,0:T(8,128)} %get-tuple-element.21), calls=%async_computation.1 | async-start | bytes 786432 | tf_op jit(solution)/shard_map/cond/branch_0_fun/all_to_all | solution.py:514
  239.7 14.9 %all-to-all-done.1.got_ref = f32[32,24,128]{2,1,0:T(8,128)S(1)} async-done(((f32[32,24,128]{2,1,0:T(8,128)}), f32[32,24,128]{2,1,0:T(8,128)S(1)}, u32[]{:S(2)}, u32[]{:S(2)}) %all-to-all-start.1) | async-done | bytes 393248 | tf_op jit(solution)/shard_map/cond/branch_0_fun/all_to_all | solution.py:514
  254.6 22.3 %all_to_all.81.raw_ref.raw_r_ref = f32[16,72,128]{2,1,0:T(8,128)S(1)} all-to-all(f32[16,72,128]{2,1,0:T(8,128)S(1)} %relay.1), channel_id=1, replica_groups=mesh['row'=32,'col'=16] {'col'}, dimensions={0} | all-to-all | bytes 1179648 | tf_op jit(solution)/shard_map/cond/branch_0_fun/all_to_all | solution.py:514
  277.0 4.5 first_once.1
  285.7 5.0 %all-to-all-start.3 = ((f32[32,24,128]{2,1,0:T(8,128)}), f32[32,24,128]{2,1,0:T(8,128)S(1)}, u32[]{:S(2)}, u32[]{:S(2)}) async-start(f32[32,24,128]{2,1,0:T(8,128)} %pad_maximum_fusion), calls=%async_computation.3 | async-start | bytes 786432 | tf_op jit(solution)/shard_map/cond/branch_0_fun/all_to_all | solution.py:514
  290.7 3.7 collective-permute-start
  294.4 8.6 %all-to-all-done.3.got_ref = f32[32,24,128]{2,1,0:T(8,128)S(1)} async-done(((f32[32,24,128]{2,1,0:T(8,128)}), f32[32,24,128]{2,1,0:T(8,128)S(1)}, u32[]{:S(2)}, u32[]{:S(2)}) %all-to-all-start.3) | async-done | bytes 393248 | tf_op jit(solution)/shard_map/cond/branch_0_fun/all_to_all | solution.py:514
  304.2 8.4 %all-to-all-start.4 = ((f32[32,72,128]{2,1,0:T(8,128)}), f32[32,72,128]{2,1,0:T(8,128)S(1)}, u32[]{:S(2)}, u32[]{:S(2)}) async-start(f32[32,72,128]{2,1,0:T(8,128)} %get-tuple-element.24), calls=%async_computation.4 | async-start | bytes 2359296 | tf_op jit(solution)/shard_map/cond/branch_0_fun/all_to_all | solution.py:514
  312.6 7.3 %collective-permute-start.1 = (f32[16,128]{1,0:T(8,128)S(1)}, f32[16,128]{1,0:T(8,128)S(1)}, u32[]{:S(2)}, u32[]{:S(2)}) collective-permute-start(f32[16,128]{1,0:T(8,128)S(1)} %get-tuple-element.27), channel_id=1, source_target_pairs={{0,0},{16,1},{32,2},{48,3},{64,4},{80,5},{96,6},{112,7},{128,8},{1... | collective-permute-start | bytes 24584 | tf_op jit(solution)/shard_map/cond/branch_0_fun/ppermute | solution.py:552
  319.9 18.6 %all-to-all-done.4.gathered_ref.raw_ref.old_ref = f32[32,72,128]{2,1,0:T(8,128)S(1)} async-done(((f32[32,72,128]{2,1,0:T(8,128)}), f32[32,72,128]{2,1,0:T(8,128)S(1)}, u32[]{:S(2)}, u32[]{:S(2)}) %all-to-all-start.4) | async-done | bytes 1179680 | tf_op jit(solution)/shard_map/cond/branch_0_fun/all_to_all | solution.py:514
  342.1 10.4 %all-to-all-start.5 = ((f32[16,40,128]{2,1,0:T(8,128)}), f32[16,40,128]{2,1,0:T(8,128)S(1)}, u32[]{:S(2)}, u32[]{:S(2)}) async-start(f32[16,40,128]{2,1,0:T(8,128)} %inner.3), calls=%async_computation.5 | async-start | bytes 655360 | tf_op jit(solution)/shard_map/cond/branch_0_fun/all_to_all | solution.py:514
  352.5 6.8 %first_factor.1 = (f32[8,64,64]{2,1,0:T(8,128)S(1)}, f32[1024,128]{1,0:T(8,128)S(1)}, s32[1]{0:T(128)}) custom-call(s32[1]{0:T(128)} %get-tuple-element.28.col_ref, f32[32,72,128]{2,1,0:T(8,128)S(1)} %all-to-all-done.4.gathered_ref.raw_ref.old_ref, f32[1024,64]{1,0:T(8,128)S(1)} %fusion.5.once_ref.once_c_ref), custom_call_target="tpu_custom_call" | custom-call | flops 16777216 | bytes 4194304 | tf_op jit(solution)/shard_map/cond/branch_0_fun/first_factor/pallas_call | solution.py:500
  360.1 5.4 %all-to-all-done.5.got_ref = f32[16,40,128]{2,1,0:T(8,128)S(1)} async-done(((f32[16,40,128]{2,1,0:T(8,128)}), f32[16,40,128]{2,1,0:T(8,128)S(1)}, u32[]{:S(2)}, u32[]{:S(2)}) %all-to-all-start.5) | async-done | bytes 327712 | tf_op jit(solution)/shard_map/cond/branch_0_fun/all_to_all | solution.py:514
  366.6 4.3 first_cols.1
  371.6 4.1 all-to-all-start.6
  378.1 7.3 %all-to-all-done.6.got_ref = f32[16,24,128]{2,1,0:T(8,128)} async-done(((f32[16,24,128]{2,1,0:T(8,128)}), f32[16,24,128]{2,1,0:T(8,128)}, u32[]{:S(2)}, u32[]{:S(2)}) %all-to-all-start.6) | async-done | bytes 196640 | tf_op jit(solution)/shard_map/cond/branch_0_fun/all_to_all | solution.py:514
  386.4 5.7 %second_once.1 = (f32[64,64]{1,0:T(8,128)S(1)}, f32[512,64]{1,0:T(8,128)S(1)}, f32[32,8,128]{2,1,0:T(8,128)S(1)}) custom-call(s32[1]{0:T(128)} %get-tuple-element.19.index_ref.row_ref, f32[16,24,128]{2,1,0:T(8,128)} %all-to-all-done.6.got_ref, f32[16,72,128]{2,1,0:T(8,128)S(1)} %all_to_all.81.raw_ref.raw_r_ref, f32[512,64]{1,0:T(8,128)S(1)} %copy-done.15, ...), custom_call_target="tpu_custom_call" | custom-call | flops 16777216 | bytes 4194304 | tf_op jit(solution)/shard_map/cond/branch_0_fun/second_once/pallas_call | solution.py:500
  396.2 18.5 %all_to_all.82.got_ref = f32[32,24,128]{2,1,0:T(8,128)S(1)} all-to-all(f32[32,24,128]{2,1,0:T(8,128)S(1)} %pad_maximum_fusion.1), channel_id=1, replica_groups=mesh['row'=32,'col'=16] {'row'}, dimensions={0} | all-to-all | bytes 786432 | tf_op jit(solution)/shard_map/cond/branch_0_fun/all_to_all | solution.py:514
  415.5 6.5 %all-to-all-start.8 = ((f32[32,24,128]{2,1,0:T(8,128)}), f32[32,24,128]{2,1,0:T(8,128)S(1)}, u32[]{:S(2)}, u32[]{:S(2)}) async-start(f32[32,24,128]{2,1,0:T(8,128)} %get-tuple-element.38), calls=%async_computation.8 | async-start | bytes 786432 | tf_op jit(solution)/shard_map/cond/branch_0_fun/all_to_all | solution.py:514
  422.1 5.2 %collective-permute-start.2 = (f32[16,128]{1,0:T(8,128)S(1)}, f32[16,128]{1,0:T(8,128)S(1)}, u32[]{:S(2)}, u32[]{:S(2)}) collective-permute-start(f32[16,128]{1,0:T(8,128)S(1)} %get-tuple-element.41), channel_id=1, source_target_pairs={{0,0},{16,1},{32,2},{48,3},{64,4},{80,5},{96,6},{112,7},{128,8},{1... | collective-permute-start | bytes 24584 | tf_op jit(solution)/shard_map/cond/branch_0_fun/ppermute | solution.py:552
  427.9 5.5 %collective-permute-done.2.chunk_ref = f32[16,128]{1,0:T(8,128)S(1)} collective-permute-done((f32[16,128]{1,0:T(8,128)S(1)}, f32[16,128]{1,0:T(8,128)S(1)}, u32[]{:S(2)}, u32[]{:S(2)}) %collective-permute-start.2) | collective-permute-done | bytes 8224 | tf_op jit(solution)/shard_map/cond/branch_0_fun/ppermute | solution.py:552
  434.8 9.8 %all-to-all-start.9 = ((f32[16,40,128]{2,1,0:T(8,128)}), f32[16,40,128]{2,1,0:T(8,128)}, u32[]{:S(2)}, u32[]{:S(2)}) async-start(f32[16,40,128]{2,1,0:T(8,128)} %copy-done.2), calls=%async_computation.9 | async-start | bytes 655360 | tf_op jit(solution)/shard_map/cond/branch_0_fun/all_to_all | solution.py:514
  444.6 4.2 fusion.6
  448.8 8.5 %second_factor.1 = (f32[1024,128]{1,0:T(8,128)S(1)}, f32[640,128]{1,0:T(8,128)S(1)}, f32[2,64,512]{2,1,0:T(8,128)}, f32[2,64,64]{2,1,0:T(8,128)}) custom-call(s32[1]{0:T(128)} %get-tuple-element.19.index_ref.row_ref, s32[1]{0:T(128)} %get-tuple-element.28.col_ref, f32[32,24,128]{2,1,0:T(8,128)S(1)} %all-to-all-done.8.gathered_ref, ...), custom_call_target="tpu_custom_call" | custom-call | flops 16777216 | bytes 4194304 | tf_op jit(solution)/shard_map/cond/branch_0_fun/second_factor/pallas_call | solution.py:500
  462.4 4.3 subtract_subtract_fusion
  (86 shorter events, 59.0 us)
Async XLA Ops:
  29.7 17.4 %all-to-all-start.11 = ((f32[16,48,128]{2,1,0:T(8,128)}), f32[16,48,128]{2,1,0:T(8,128)S(1)}, u32[]{:S(2)}, u32[]{:S(2)}) async-start(f32[16,48,128]{2,1,0:T(8,128)} %broadcast_in_dim.23), calls=%async_computation.11 | async-start | bytes 786432 | tf_op jit(solution)/shard_map/all_to_all | solution.py:514
  51.9 24.6 %all-to-all-start.12 = ((f32[32,24,128]{2,1,0:T(8,128)}), f32[32,24,128]{2,1,0:T(8,128)S(1)}, u32[]{:S(2)}, u32[]{:S(2)}) async-start(f32[32,24,128]{2,1,0:T(8,128)} %pad_maximum_fusion.2), calls=%async_computation.12 | async-start | bytes 786432 | tf_op jit(solution)/shard_map/all_to_all | solution.py:514
  61.5 14.9 %collective-permute-start.3 = (f32[48,128]{1,0:T(8,128)S(1)}, f32[48,128]{1,0:T(8,128)S(1)}, u32[]{:S(2)}, u32[]{:S(2)}) collective-permute-start(f32[48,128]{1,0:T(8,128)S(1)} %slice_bitcast_fusion.1), channel_id=1, source_target_pairs={{0,0},{1,16},{2,32},{3,48},{4,64},{5,80},{6,96},{7,112},{8,128},{9... | collective-permute-start | bytes 73736 | tf_op jit(solution)/shard_map/ppermute | solution.py:572
  77.6 34.0 %all-to-all-start.13 = ((f32[32,72,128]{2,1,0:T(8,128)}), f32[32,72,128]{2,1,0:T(8,128)S(1)}, u32[]{:S(2)}, u32[]{:S(2)}) async-start(f32[32,72,128]{2,1,0:T(8,128)} %get-tuple-element.83), calls=%async_computation.13 | async-start | bytes 2359296 | tf_op jit(solution)/shard_map/all_to_all | solution.py:514
  83.4 28.1 %collective-permute-start.4 = (f32[16,128]{1,0:T(8,128)S(1)}, f32[16,128]{1,0:T(8,128)S(1)}, u32[]{:S(2)}, u32[]{:S(2)}) collective-permute-start(f32[16,128]{1,0:T(8,128)S(1)} %get-tuple-element.85), channel_id=1, source_target_pairs={{0,0},{16,1},{32,2},{48,3},{64,4},{80,5},{96,6},{112,7},{128,8},{1... | collective-permute-start | bytes 24584 | tf_op jit(solution)/shard_map/ppermute | solution.py:552
  112.9 23.1 %all-to-all-start.14 = ((f32[16,40,128]{2,1,0:T(8,128)}), f32[16,40,128]{2,1,0:T(8,128)S(1)}, u32[]{:S(2)}, u32[]{:S(2)}) async-start(f32[16,40,128]{2,1,0:T(8,128)} %plain_inner.1), calls=%async_computation.14 | async-start | bytes 655360 | tf_op jit(solution)/shard_map/all_to_all | solution.py:514
  144.3 0.8 copy-start.7
  145.1 0.7 copy-start.16
  145.8 0.6 copy-start.17
  146.5 15.6 %all-to-all-start.15 = ((f32[16,32,128]{2,1,0:T(8,128)}), f32[16,32,128]{2,1,0:T(8,128)}, u32[]{:S(2)}, u32[]{:S(2)}) async-start(f32[16,32,128]{2,1,0:T(8,128)} %copy-done.16), calls=%async_computation.15 | async-start | bytes 524288 | tf_op jit(solution)/shard_map/all_to_all | solution.py:514
  150.8 0.8 copy-start.18
  163.8 15.1 %all-to-all-start.16 = ((f32[16,32,128]{2,1,0:T(8,128)}), f32[16,32,128]{2,1,0:T(8,128)S(1)}, u32[]{:S(2)}, u32[]{:S(2)}) async-start(f32[16,32,128]{2,1,0:T(8,128)} %get-tuple-element.94), calls=%async_computation.16 | async-start | bytes 524288 | tf_op jit(solution)/shard_map/all_to_all | solution.py:514
  167.2 6.2 %collective-permute-start.5 = (f32[16,128]{1,0:T(8,128)S(1)}, f32[16,128]{1,0:T(8,128)S(1)}, u32[]{:S(2)}, u32[]{:S(2)}) collective-permute-start(f32[16,128]{1,0:T(8,128)S(1)} %get-tuple-element.100), channel_id=1, source_target_pairs={{0,0},{1,16},{2,32},{3,48},{4,64},{5,80},{6,96},{7,112},{8,128},{9... | collective-permute-start | bytes 24584 | tf_op jit(solution)/shard_map/ppermute | solution.py:552
  180.2 25.9 %all-to-all-start.17 = ((f32[32,40,128]{2,1,0:T(8,128)}), f32[32,40,128]{2,1,0:T(8,128)S(1)}, u32[]{:S(2)}, u32[]{:S(2)}) async-start(f32[32,40,128]{2,1,0:T(8,128)} %inner.5), calls=%async_computation.17 | async-start | bytes 1310720 | tf_op jit(solution)/shard_map/all_to_all | solution.py:514
  187.4 1.0 copy-start.8
  200.3 0.8 copy-start.5
  206.1 1.1 copy-start.6
  234.5 20.1 %all-to-all-start.1 = ((f32[32,24,128]{2,1,0:T(8,128)}), f32[32,24,128]{2,1,0:T(8,128)S(1)}, u32[]{:S(2)}, u32[]{:S(2)}) async-start(f32[32,24,128]{2,1,0:T(8,128)} %get-tuple-element.21), calls=%async_computation.1 | async-start | bytes 786432 | tf_op jit(solution)/shard_map/cond/branch_0_fun/all_to_all | solution.py:514
  285.7 17.3 %all-to-all-start.3 = ((f32[32,24,128]{2,1,0:T(8,128)}), f32[32,24,128]{2,1,0:T(8,128)S(1)}, u32[]{:S(2)}, u32[]{:S(2)}) async-start(f32[32,24,128]{2,1,0:T(8,128)} %pad_maximum_fusion), calls=%async_computation.3 | async-start | bytes 786432 | tf_op jit(solution)/shard_map/cond/branch_0_fun/all_to_all | solution.py:514
  290.7 12.3 %collective-permute-start = (f32[48,128]{1,0:T(8,128)S(1)}, f32[48,128]{1,0:T(8,128)S(1)}, u32[]{:S(2)}, u32[]{:S(2)}) collective-permute-start(f32[48,128]{1,0:T(8,128)S(1)} %slice_bitcast_fusion.raw_ref), channel_id=1, source_target_pairs={{0,0},{1,16},{2,32},{3,48},{4,64},{5,80},{6,96},{7,112},{8,128},{9... | collective-permute-start | bytes 73736 | tf_op jit(solution)/shard_map/cond/branch_0_fun/ppermute | solution.py:628
  304.2 34.3 %all-to-all-start.4 = ((f32[32,72,128]{2,1,0:T(8,128)}), f32[32,72,128]{2,1,0:T(8,128)S(1)}, u32[]{:S(2)}, u32[]{:S(2)}) async-start(f32[32,72,128]{2,1,0:T(8,128)} %get-tuple-element.24), calls=%async_computation.4 | async-start | bytes 2359296 | tf_op jit(solution)/shard_map/cond/branch_0_fun/all_to_all | solution.py:514
  312.6 28.1 %collective-permute-start.1 = (f32[16,128]{1,0:T(8,128)S(1)}, f32[16,128]{1,0:T(8,128)S(1)}, u32[]{:S(2)}, u32[]{:S(2)}) collective-permute-start(f32[16,128]{1,0:T(8,128)S(1)} %get-tuple-element.27), channel_id=1, source_target_pairs={{0,0},{16,1},{32,2},{48,3},{64,4},{80,5},{96,6},{112,7},{128,8},{1... | collective-permute-start | bytes 24584 | tf_op jit(solution)/shard_map/cond/branch_0_fun/ppermute | solution.py:552
  342.1 23.5 %all-to-all-start.5 = ((f32[16,40,128]{2,1,0:T(8,128)}), f32[16,40,128]{2,1,0:T(8,128)S(1)}, u32[]{:S(2)}, u32[]{:S(2)}) async-start(f32[16,40,128]{2,1,0:T(8,128)} %inner.3), calls=%async_computation.5 | async-start | bytes 655360 | tf_op jit(solution)/shard_map/cond/branch_0_fun/all_to_all | solution.py:514
  359.3 0.8 copy-start.10
  365.6 1.0 copy-start.11
  370.8 0.8 copy-start
  371.6 13.8 %all-to-all-start.6 = ((f32[16,24,128]{2,1,0:T(8,128)}), f32[16,24,128]{2,1,0:T(8,128)}, u32[]{:S(2)}, u32[]{:S(2)}) async-start(f32[16,24,128]{2,1,0:T(8,128)} %get-tuple-element.34), calls=%async_computation.6 | async-start | bytes 393216 | tf_op jit(solution)/shard_map/cond/branch_0_fun/all_to_all | solution.py:514
  377.4 0.7 copy-start.14
  385.4 1.0 copy-start.15
  395.1 0.7 copy-start.3
  415.5 17.9 %all-to-all-start.8 = ((f32[32,24,128]{2,1,0:T(8,128)}), f32[32,24,128]{2,1,0:T(8,128)S(1)}, u32[]{:S(2)}, u32[]{:S(2)}) async-start(f32[32,24,128]{2,1,0:T(8,128)} %get-tuple-element.38), calls=%async_computation.8 | async-start | bytes 786432 | tf_op jit(solution)/shard_map/cond/branch_0_fun/all_to_all | solution.py:514
  422.1 11.3 %collective-permute-start.2 = (f32[16,128]{1,0:T(8,128)S(1)}, f32[16,128]{1,0:T(8,128)S(1)}, u32[]{:S(2)}, u32[]{:S(2)}) collective-permute-start(f32[16,128]{1,0:T(8,128)S(1)} %get-tuple-element.41), channel_id=1, source_target_pairs={{0,0},{16,1},{32,2},{48,3},{64,4},{80,5},{96,6},{112,7},{128,8},{1... | collective-permute-start | bytes 24584 | tf_op jit(solution)/shard_map/cond/branch_0_fun/ppermute | solution.py:552
  434.0 0.7 copy-start.2
  434.8 24.1 %all-to-all-start.9 = ((f32[16,40,128]{2,1,0:T(8,128)}), f32[16,40,128]{2,1,0:T(8,128)}, u32[]{:S(2)}, u32[]{:S(2)}) async-start(f32[16,40,128]{2,1,0:T(8,128)} %copy-done.2), calls=%async_computation.9 | async-start | bytes 655360 | tf_op jit(solution)/shard_map/cond/branch_0_fun/all_to_all | solution.py:514
  444.5 4.3 copy-start.1
  444.5 4.3 copy-start.4
  457.3 0.8 copy-start.9
  458.1 0.7 copy-start.12
  458.9 1.0 copy-start.13
  466.9 1.3 copy-start.19

commit v4 on v3

--- a/solution.py
+++ b/solution.py
@@ -234,11 +234,13 @@
     def top(x):
         return jnp.where(index == 0, x[2 * NB : 3 * NB], 0.0)
 
+    grams = tn(beside(once, last), once)
+    dots = tn(beside(vec, wide), once)
     put_pairs(
         small_ref,
         [
-            beside(tn(once, once), tn(last, once)),
-            beside(tn(vec, once), tn(wide, once)),
+            beside(grams[:NB], grams[NB:]),
+            beside(dots[:NB], dots[NB:]),
             beside(top(once), top(vec)),
             beside(top(wide), jnp.zeros((NB, NB), jnp.float32)),
         ],
@@ -348,8 +350,8 @@
     first_factor(False, chunk, half, at, col_ref[0], gathered_ref, panel, outs)
 
 
-def second_panel(following, vec, wide, wide_top, lower, index):
-    return below(following - nt(vec, wide_top) - nt(wide, lower), index, 2 * NB)
+def second_panel(following, pair, tops, index):
+    return below(following - nt(pair, tops), index, 2 * NB)
 
 
 def first_cols(
@@ -363,9 +365,10 @@
     tops_ref[1] = wide_top
     vec = state_ref[:, :NB]
     wide = state_ref[:, NB:] - nn(vec, half)
-    pair_ref[...] = beside(wide, vec)
+    pair = beside(wide, vec)
+    pair_ref[...] = pair
     following = pair_raw(raw_ref, chunk, at)[:, NB:]
-    panel = second_panel(following, vec, wide, wide_top, lower, index)
+    panel = second_panel(following, pair, beside(lower, wide_top), index)
     spare = jnp.zeros((panel.shape[0] - NB, NB), jnp.float32)
     panel_ref[...] = beside(panel, jnp.concatenate([small_ref[FACTOR], spare], axis=0))
     return panel, vec, wide
@@ -404,8 +407,10 @@
     following = pair_raw(raw_ref, chunk)[:, NB:]
     vec = vectors_of(once_ref[...], row_ref[0], NB, small_ref[PICK], small_ref[COEF])
     wide = nn(following, small_ref[PICK_T]) - nn(image, small_ref[COEF_T]) - nn(vec, tops_ref[0])
-    pair_ref[...] = beside(vec, wide)
-    panel_ref[...] = second_panel(following, vec, wide, tops_ref[1], small_ref[LOWER], row_ref[0])
+    pair = beside(vec, wide)
+    pair_ref[...] = pair
+    tops = beside(tops_ref[1], small_ref[LOWER])
+    panel_ref[...] = second_panel(following, pair, tops, row_ref[0])
 
 
 def second_small(near, half, gathered_ref, old_ref, panel_ref, small_ref, factors_ref):
@@ -677,15 +682,13 @@
                 statics=(chunk, half, at), scalars=2, small=True,
             )
             left = call(last_kernel, "last", [pair_shape_r], got, state_r)
-            return current - nt(left, right), vectors, factors
+            return current, left, right, vectors, factors
 
         ready, fine = plain()
-
-        def finish(current, left, right, vectors, factors):
-            return current - nt(left, right), vectors, factors
-
-        banded, vectors, factors = lax.cond(fine, finish, lambda *_: careful(), *ready)
-        return banded, vectors.transpose(0, 2, 1), factors
+        current, left, right, vectors, factors = lax.cond(
+            fine, lambda *given: given, lambda *_: careful(), *ready
+        )
+        return current - nt(left, right), vectors.transpose(0, 2, 1), factors
 
     return jax.shard_map(
         local,

time: 475 us -> 475 us (level)
  transfers between devices with their start and end apart: 20 -> 20, of which waited for: 16 -> 16; matrix products, arithmetic and copies ran while one was open for 2% -> 3% of each run, Pallas kernels for 8% -> 9%
where the time goes in v4:
time: 475 us; the launch traced here: 469 us
  waiting for transfers between devices  128 us (27%)
  starting transfers between devices  123 us (26%)
  blocking collectives  89.4 us (19%)
  Pallas kernels  82.5 us (17%)
  matrix products  25.6 us (5%)
  local copies, waits for them, and re-layouts  16 us (3%)
    all_to_all x14, waiting for transfers between devices, swap(): return lax.all_to_all(x, axis, 0, 0)  97.7 us
    all_to_all x14, starting transfers between devices, swap(): return lax.all_to_all(x, axis, 0, 0)  93.4 us
    all_to_all x4, blocking collectives, swap(): return lax.all_to_all(x, axis, 0, 0)  89.4 us
    pallas_call x23, Pallas kernels, call(): pl.pallas_call(functools.partial(kernel, *statics), out_shape=out_shape,...  80.6 us
    ppermute x4, waiting for transfers between devices, image_round(): lax.ppermute(image_chunk, ('row', 'col'), targets)  30 us
    ppermute x4, starting transfers between devices, image_round(): lax.ppermute(image_chunk, ('row', 'col'), targets)  22.6 us
    dot_general x5, matrix products, nt(): lax.dot_general(a, b, (((1,), (1,)), ((), ())), precision=precise, prefer...  16.6 us
  transfers between devices with their start and end apart: 20, of which 16 were waited for; matrix products, arithmetic and copies ran while one was open for 3% of the time, Pallas kernels for 9%

profile of v4, /device:TPU:1, one launch (start us, length us, event | category | flops | bytes accessed | tf_op | source)
XLA Modules:
  0.0 468.7 jit_solution(11550582042603979269)
XLA Ops:
  2.5 26.4 %all_to_all.83 = f32[16,48,128]{2,1,0:T(8,128)S(1)} all-to-all(f32[16,48,128]{2,1,0:T(8,128)} %plain_start.1), channel_id=1, replica_groups=mesh['row'=32,'col'=16] {'col'}, dimensions={0} | all-to-all | bytes 786432 | tf_op jit(solution)/shard_map/all_to_all | solution.py:519
  29.7 3.5 all-to-all-start.11
  33.1 14.0 %all-to-all-done.11.raw_ref.raw_r_ref = f32[16,48,128]{2,1,0:T(8,128)S(1)} async-done(((f32[16,48,128]{2,1,0:T(8,128)}), f32[16,48,128]{2,1,0:T(8,128)S(1)}, u32[]{:S(2)}, u32[]{:S(2)}) %all-to-all-start.11) | async-done | bytes 393248 | tf_op jit(solution)/shard_map/all_to_all | solution.py:519
  51.9 9.7 %all-to-all-start.12 = ((f32[32,24,128]{2,1,0:T(8,128)}), f32[32,24,128]{2,1,0:T(8,128)S(1)}, u32[]{:S(2)}, u32[]{:S(2)}) async-start(f32[32,24,128]{2,1,0:T(8,128)} %pad_maximum_fusion.2), calls=%async_computation.12 | async-start | bytes 786432 | tf_op jit(solution)/shard_map/all_to_all | solution.py:519
  64.4 12.1 %all-to-all-done.12.got_ref = f32[32,24,128]{2,1,0:T(8,128)S(1)} async-done(((f32[32,24,128]{2,1,0:T(8,128)}), f32[32,24,128]{2,1,0:T(8,128)S(1)}, u32[]{:S(2)}, u32[]{:S(2)}) %all-to-all-start.12) | async-done | bytes 393248 | tf_op jit(solution)/shard_map/all_to_all | solution.py:519
  77.6 5.8 %all-to-all-start.13 = ((f32[32,72,128]{2,1,0:T(8,128)}), f32[32,72,128]{2,1,0:T(8,128)S(1)}, u32[]{:S(2)}, u32[]{:S(2)}) async-start(f32[32,72,128]{2,1,0:T(8,128)} %get-tuple-element.80), calls=%async_computation.13 | async-start | bytes 2359296 | tf_op jit(solution)/shard_map/all_to_all | solution.py:519
  83.4 6.4 %collective-permute-start.4 = (f32[16,128]{1,0:T(8,128)S(1)}, f32[16,128]{1,0:T(8,128)S(1)}, u32[]{:S(2)}, u32[]{:S(2)}) collective-permute-start(f32[16,128]{1,0:T(8,128)S(1)} %get-tuple-element.82), channel_id=1, source_target_pairs={{0,0},{16,1},{32,2},{48,3},{64,4},{80,5},{96,6},{112,7},{128,8},{1... | collective-permute-start | bytes 24584 | tf_op jit(solution)/shard_map/ppermute | solution.py:557
  89.8 21.7 %collective-permute-done.4.chunk_ref = f32[16,128]{1,0:T(8,128)S(1)} collective-permute-done((f32[16,128]{1,0:T(8,128)S(1)}, f32[16,128]{1,0:T(8,128)S(1)}, u32[]{:S(2)}, u32[]{:S(2)}) %collective-permute-start.4) | collective-permute-done | bytes 8224 | tf_op jit(solution)/shard_map/ppermute | solution.py:557
  112.9 10.2 %all-to-all-start.14 = ((f32[16,40,128]{2,1,0:T(8,128)}), f32[16,40,128]{2,1,0:T(8,128)S(1)}, u32[]{:S(2)}, u32[]{:S(2)}) async-start(f32[16,40,128]{2,1,0:T(8,128)} %plain_inner.1), calls=%async_computation.14 | async-start | bytes 655360 | tf_op jit(solution)/shard_map/all_to_all | solution.py:519
  123.1 9.3 %plain_factor.1 = (f32[8,64,64]{2,1,0:T(8,128)S(1)}, f32[1024,128]{1,0:T(8,128)S(1)}, s32[1]{0:T(128)}) custom-call(s32[1]{0:T(128)} %bitcast.6.col_ref, f32[32,72,128]{2,1,0:T(8,128)S(1)} %all-to-all-done.13.gathered_ref.raw_ref.old_ref), custom_call_target="tpu_custom_call" | custom-call | flops 16777216 | bytes 4194304 | tf_op jit(solution)/shard_map/plain_factor/pallas_call | solution.py:505
  132.5 3.6 all-to-all-done.14.got_ref
  136.1 7.8 %plain_cols.1 = (f32[1024,128]{1,0:T(8,128)S(1)}, f32[1024,128]{1,0:T(8,128)S(1)}, f32[2,64,64]{2,1,0:T(8,128)S(1)}, f32[16,32,128]{2,1,0:T(8,128)S(1)}) custom-call(s32[1]{0:T(128)} %bitcast.6.col_ref, f32[16,40,128]{2,1,0:T(8,128)S(1)} %all-to-all-done.14.got_ref, f32[8,64,64]{2,1,0:T(8,128)S(1)} %get-tuple-element.83.small_ref, ...), custom_call_target="tpu_custom_call" | custom-call | flops 16777216 | bytes 4194304 | tf_op jit(solution)/shard_map/plain_cols/pallas_call | solution.py:505
  146.0 4.3 all-to-all-start.15
  153.0 4.7 %convolution_subtract_fusion.2 = f32[512,1024]{1,0:T(8,128)} fusion(f32[512,1024]{1,0:T(8,128)} %matrix_ref.3, f32[512,128]{1,0:T(8,128)S(1)} %get-tuple-element.94.pair_r_ref, f32[1024,128]{1,0:T(8,128)S(1)} %get-tuple-element.88.pair_c_ref), kind=kOutput, calls=%fused_computation.11 | convolution fusion | flops 805830656 | bytes 4980736 | tf_op jit(solution)/shard_map/dot_general | solution.py:27
  157.7 3.9 all-to-all-done.15.got_ref
  163.3 3.4 all-to-all-start.16
  166.8 3.7 collective-permute-start.5
  172.9 5.5 %all-to-all-done.16.gathered_ref = f32[16,32,128]{2,1,0:T(8,128)S(1)} async-done(((f32[16,32,128]{2,1,0:T(8,128)}), f32[16,32,128]{2,1,0:T(8,128)S(1)}, u32[]{:S(2)}, u32[]{:S(2)}) %all-to-all-start.16) | async-done | bytes 262176 | tf_op jit(solution)/shard_map/all_to_all | solution.py:519
  179.7 7.2 %all-to-all-start.17 = ((f32[32,40,128]{2,1,0:T(8,128)}), f32[32,40,128]{2,1,0:T(8,128)S(1)}, u32[]{:S(2)}, u32[]{:S(2)}) async-start(f32[32,40,128]{2,1,0:T(8,128)} %inner.5), calls=%async_computation.17 | async-start | bytes 1310720 | tf_op jit(solution)/shard_map/all_to_all | solution.py:519
  188.0 11.8 %plain_second.1 = (f32[1152,128]{1,0:T(8,128)S(1)}, f32[512,128]{1,0:T(8,128)}, f32[2,64,512]{2,1,0:T(8,128)}, f32[2,64,64]{2,1,0:T(8,128)}, s32[1]{0:T(128)}) custom-call(s32[1]{0:T(128)} %bitcast.7.index_ref.row_ref, s32[1]{0:T(128)} %bitcast.6.col_ref, f32[16,32,128]{2,1,0:T(8,128)S(1)} %all-to-all-done.16.gathered_ref, ...), custom_call_target="tpu_custom_call" | custom-call | flops 16777216 | bytes 4194304 | tf_op jit(solution)/shard_map/plain_second/pallas_call | solution.py:505
  201.8 3.8 all-to-all-done.17.got_ref
  209.6 253.8 %conditional.1 = ((f32[512,1024]{1,0:T(8,128)}, f32[512,128]{1,0:T(8,128)}, f32[1024,128]{1,0:T(8,128)}, f32[2,64,512]{2,1,0:T(8,128)}, f32[2,64,64]{2,1,0:T(8,128)})) conditional(s32[]{:T(128)} %bitcast.11, (f32[512,1024]{1,0:T(8,128)}, s32[1]{0:T(128)}, s32[]{:T(128)}, s32[1]{0:T(128)}, s32[1024,1]{0,1:T(1,128)S(1)}, /*index=5*/()) %tuple.17, ...), branch_computations={%region_0.1_spmd, %region_1.2_spmd} | conditional | flops 1930364928 | bytes 98622168 | solution.py:688
  211.9 22.2 %all_to_all.80 = f32[16,48,128]{2,1,0:T(8,128)S(1)} all-to-all(f32[16,48,128]{2,1,0:T(8,128)S(1)} %get-tuple-element.20), channel_id=1, replica_groups=mesh['row'=32,'col'=16] {'col'}, dimensions={0} | all-to-all | bytes 786432 | tf_op jit(solution)/shard_map/cond/branch_0_fun/all_to_all | solution.py:519
  234.0 5.1 %all-to-all-start.1 = ((f32[32,24,128]{2,1,0:T(8,128)}), f32[32,24,128]{2,1,0:T(8,128)S(1)}, u32[]{:S(2)}, u32[]{:S(2)}) async-start(f32[32,24,128]{2,1,0:T(8,128)} %get-tuple-element.21), calls=%async_computation.1 | async-start | bytes 786432 | tf_op jit(solution)/shard_map/cond/branch_0_fun/all_to_all | solution.py:519
  239.2 14.9 %all-to-all-done.1.got_ref = f32[32,24,128]{2,1,0:T(8,128)S(1)} async-done(((f32[32,24,128]{2,1,0:T(8,128)}), f32[32,24,128]{2,1,0:T(8,128)S(1)}, u32[]{:S(2)}, u32[]{:S(2)}) %all-to-all-start.1) | async-done | bytes 393248 | tf_op jit(solution)/shard_map/cond/branch_0_fun/all_to_all | solution.py:519
  254.1 22.3 %all_to_all.81.raw_ref.raw_r_ref = f32[16,72,128]{2,1,0:T(8,128)S(1)} all-to-all(f32[16,72,128]{2,1,0:T(8,128)S(1)} %relay.1), channel_id=1, replica_groups=mesh['row'=32,'col'=16] {'col'}, dimensions={0} | all-to-all | bytes 1179648 | tf_op jit(solution)/shard_map/cond/branch_0_fun/all_to_all | solution.py:519
  276.5 4.5 first_once.1
  285.2 5.0 %all-to-all-start.3 = ((f32[32,24,128]{2,1,0:T(8,128)}), f32[32,24,128]{2,1,0:T(8,128)S(1)}, u32[]{:S(2)}, u32[]{:S(2)}) async-start(f32[32,24,128]{2,1,0:T(8,128)} %pad_maximum_fusion), calls=%async_computation.3 | async-start | bytes 786432 | tf_op jit(solution)/shard_map/cond/branch_0_fun/all_to_all | solution.py:519
  290.2 3.7 collective-permute-start
  293.9 8.6 %all-to-all-done.3.got_ref = f32[32,24,128]{2,1,0:T(8,128)S(1)} async-done(((f32[32,24,128]{2,1,0:T(8,128)}), f32[32,24,128]{2,1,0:T(8,128)S(1)}, u32[]{:S(2)}, u32[]{:S(2)}) %all-to-all-start.3) | async-done | bytes 393248 | tf_op jit(solution)/shard_map/cond/branch_0_fun/all_to_all | solution.py:519
  303.7 8.4 %all-to-all-start.4 = ((f32[32,72,128]{2,1,0:T(8,128)}), f32[32,72,128]{2,1,0:T(8,128)S(1)}, u32[]{:S(2)}, u32[]{:S(2)}) async-start(f32[32,72,128]{2,1,0:T(8,128)} %get-tuple-element.24), calls=%async_computation.4 | async-start | bytes 2359296 | tf_op jit(solution)/shard_map/cond/branch_0_fun/all_to_all | solution.py:519
  312.1 7.3 %collective-permute-start.1 = (f32[16,128]{1,0:T(8,128)S(1)}, f32[16,128]{1,0:T(8,128)S(1)}, u32[]{:S(2)}, u32[]{:S(2)}) collective-permute-start(f32[16,128]{1,0:T(8,128)S(1)} %get-tuple-element.27), channel_id=1, source_target_pairs={{0,0},{16,1},{32,2},{48,3},{64,4},{80,5},{96,6},{112,7},{128,8},{1... | collective-permute-start | bytes 24584 | tf_op jit(solution)/shard_map/cond/branch_0_fun/ppermute | solution.py:557
  319.4 18.6 %all-to-all-done.4.gathered_ref.raw_ref.old_ref = f32[32,72,128]{2,1,0:T(8,128)S(1)} async-done(((f32[32,72,128]{2,1,0:T(8,128)}), f32[32,72,128]{2,1,0:T(8,128)S(1)}, u32[]{:S(2)}, u32[]{:S(2)}) %all-to-all-start.4) | async-done | bytes 1179680 | tf_op jit(solution)/shard_map/cond/branch_0_fun/all_to_all | solution.py:519
  341.6 10.4 %all-to-all-start.5 = ((f32[16,40,128]{2,1,0:T(8,128)}), f32[16,40,128]{2,1,0:T(8,128)S(1)}, u32[]{:S(2)}, u32[]{:S(2)}) async-start(f32[16,40,128]{2,1,0:T(8,128)} %inner.3), calls=%async_computation.5 | async-start | bytes 655360 | tf_op jit(solution)/shard_map/cond/branch_0_fun/all_to_all | solution.py:519
  352.0 6.8 %first_factor.1 = (f32[8,64,64]{2,1,0:T(8,128)S(1)}, f32[1024,128]{1,0:T(8,128)S(1)}, s32[1]{0:T(128)}) custom-call(s32[1]{0:T(128)} %get-tuple-element.28.col_ref, f32[32,72,128]{2,1,0:T(8,128)S(1)} %all-to-all-done.4.gathered_ref.raw_ref.old_ref, f32[1024,64]{1,0:T(8,128)S(1)} %fusion.5.once_ref.once_c_ref), custom_call_target="tpu_custom_call" | custom-call | flops 16777216 | bytes 4194304 | tf_op jit(solution)/shard_map/cond/branch_0_fun/first_factor/pallas_call | solution.py:505
  359.6 5.5 %all-to-all-done.5.got_ref = f32[16,40,128]{2,1,0:T(8,128)S(1)} async-done(((f32[16,40,128]{2,1,0:T(8,128)}), f32[16,40,128]{2,1,0:T(8,128)S(1)}, u32[]{:S(2)}, u32[]{:S(2)}) %all-to-all-start.5) | async-done | bytes 327712 | tf_op jit(solution)/shard_map/cond/branch_0_fun/all_to_all | solution.py:519
  366.1 4.2 first_cols.1
  371.1 4.1 all-to-all-start.6
  377.7 7.1 %all-to-all-done.6.got_ref = f32[16,24,128]{2,1,0:T(8,128)} async-done(((f32[16,24,128]{2,1,0:T(8,128)}), f32[16,24,128]{2,1,0:T(8,128)}, u32[]{:S(2)}, u32[]{:S(2)}) %all-to-all-start.6) | async-done | bytes 196640 | tf_op jit(solution)/shard_map/cond/branch_0_fun/all_to_all | solution.py:519
  385.8 5.7 %second_once.1 = (f32[64,64]{1,0:T(8,128)S(1)}, f32[512,64]{1,0:T(8,128)S(1)}, f32[32,8,128]{2,1,0:T(8,128)S(1)}) custom-call(s32[1]{0:T(128)} %get-tuple-element.19.index_ref.row_ref, f32[16,24,128]{2,1,0:T(8,128)} %all-to-all-done.6.got_ref, f32[16,72,128]{2,1,0:T(8,128)S(1)} %all_to_all.81.raw_ref.raw_r_ref, f32[512,64]{1,0:T(8,128)S(1)} %copy-done.14, ...), custom_call_target="tpu_custom_call" | custom-call | flops 16777216 | bytes 4194304 | tf_op jit(solution)/shard_map/cond/branch_0_fun/second_once/pallas_call | solution.py:505
  395.7 18.5 %all_to_all.82.got_ref = f32[32,24,128]{2,1,0:T(8,128)S(1)} all-to-all(f32[32,24,128]{2,1,0:T(8,128)S(1)} %pad_maximum_fusion.1), channel_id=1, replica_groups=mesh['row'=32,'col'=16] {'row'}, dimensions={0} | all-to-all | bytes 786432 | tf_op jit(solution)/shard_map/cond/branch_0_fun/all_to_all | solution.py:519
  415.0 6.5 %all-to-all-start.8 = ((f32[32,24,128]{2,1,0:T(8,128)}), f32[32,24,128]{2,1,0:T(8,128)S(1)}, u32[]{:S(2)}, u32[]{:S(2)}) async-start(f32[32,24,128]{2,1,0:T(8,128)} %get-tuple-element.38), calls=%async_computation.8 | async-start | bytes 786432 | tf_op jit(solution)/shard_map/cond/branch_0_fun/all_to_all | solution.py:519
  421.6 5.2 %collective-permute-start.2 = (f32[16,128]{1,0:T(8,128)S(1)}, f32[16,128]{1,0:T(8,128)S(1)}, u32[]{:S(2)}, u32[]{:S(2)}) collective-permute-start(f32[16,128]{1,0:T(8,128)S(1)} %get-tuple-element.41), channel_id=1, source_target_pairs={{0,0},{16,1},{32,2},{48,3},{64,4},{80,5},{96,6},{112,7},{128,8},{1... | collective-permute-start | bytes 24584 | tf_op jit(solution)/shard_map/cond/branch_0_fun/ppermute | solution.py:557
  428.4 4.4 collective-permute-done.2.chunk_ref
  434.3 9.8 %all-to-all-start.9 = ((f32[16,40,128]{2,1,0:T(8,128)}), f32[16,40,128]{2,1,0:T(8,128)}, u32[]{:S(2)}, u32[]{:S(2)}) async-start(f32[16,40,128]{2,1,0:T(8,128)} %copy-done.2), calls=%async_computation.9 | async-start | bytes 655360 | tf_op jit(solution)/shard_map/cond/branch_0_fun/all_to_all | solution.py:519
  444.1 4.8 %convolution_subtract_fusion = f32[512,1024]{1,0:T(8,128)} fusion(f32[512,1024]{1,0:T(8,128)} %get-tuple-element.18, f32[512,128]{1,0:T(8,128)S(1)} %get-tuple-element.32.pair_ref.pair_r_ref, f32[1024,128]{1,0:T(8,128)S(1)} %get-tuple-element.33.pair_c_ref), kind=kOutput, calls=%fused_computation | convolution fusion | flops 805830656 | bytes 4980736 | tf_op jit(solution)/shard_map/cond/branch_0_fun/dot_general | solution.py:27
  448.9 9.3 %second_factor.1 = (f32[1024,128]{1,0:T(8,128)}, f32[640,128]{1,0:T(8,128)S(1)}, f32[2,64,512]{2,1,0:T(8,128)}, f32[2,64,64]{2,1,0:T(8,128)}) custom-call(s32[1]{0:T(128)} %get-tuple-element.19.index_ref.row_ref, s32[1]{0:T(128)} %get-tuple-element.28.col_ref, f32[32,24,128]{2,1,0:T(8,128)S(1)} %all-to-all-done.8.gathered_ref, ...), custom_call_target="tpu_custom_call" | custom-call | flops 16777216 | bytes 4194304 | tf_op jit(solution)/shard_map/cond/branch_0_fun/second_factor/pallas_call | solution.py:505
  463.4 5.0 %convolution_subtract_fusion.1 = f32[512,1024]{1,0:T(8,128)} fusion(f32[512,1024]{1,0:T(8,128)} %get-tuple-element.102, f32[512,128]{1,0:T(8,128)} %get-tuple-element.103, f32[1024,128]{1,0:T(8,128)} %get-tuple-element.104), kind=kOutput, calls=%fused_computation.10 | convolution fusion | flops 805830656 | bytes 4980736 | tf_op jit(solution)/shard_map/dot_general | solution.py:27
  (82 shorter events, 59.1 us)
Async XLA Ops:
  29.7 17.4 %all-to-all-start.11 = ((f32[16,48,128]{2,1,0:T(8,128)}), f32[16,48,128]{2,1,0:T(8,128)S(1)}, u32[]{:S(2)}, u32[]{:S(2)}) async-start(f32[16,48,128]{2,1,0:T(8,128)} %broadcast_in_dim.23), calls=%async_computation.11 | async-start | bytes 786432 | tf_op jit(solution)/shard_map/all_to_all | solution.py:519
  51.9 24.6 %all-to-all-start.12 = ((f32[32,24,128]{2,1,0:T(8,128)}), f32[32,24,128]{2,1,0:T(8,128)S(1)}, u32[]{:S(2)}, u32[]{:S(2)}) async-start(f32[32,24,128]{2,1,0:T(8,128)} %pad_maximum_fusion.2), calls=%async_computation.12 | async-start | bytes 786432 | tf_op jit(solution)/shard_map/all_to_all | solution.py:519
  61.5 14.9 %collective-permute-start.3 = (f32[48,128]{1,0:T(8,128)S(1)}, f32[48,128]{1,0:T(8,128)S(1)}, u32[]{:S(2)}, u32[]{:S(2)}) collective-permute-start(f32[48,128]{1,0:T(8,128)S(1)} %slice_bitcast_fusion.1), channel_id=1, source_target_pairs={{0,0},{1,16},{2,32},{3,48},{4,64},{5,80},{6,96},{7,112},{8,128},{9... | collective-permute-start | bytes 73736 | tf_op jit(solution)/shard_map/ppermute | solution.py:577
  77.6 34.0 %all-to-all-start.13 = ((f32[32,72,128]{2,1,0:T(8,128)}), f32[32,72,128]{2,1,0:T(8,128)S(1)}, u32[]{:S(2)}, u32[]{:S(2)}) async-start(f32[32,72,128]{2,1,0:T(8,128)} %get-tuple-element.80), calls=%async_computation.13 | async-start | bytes 2359296 | tf_op jit(solution)/shard_map/all_to_all | solution.py:519
  83.4 28.1 %collective-permute-start.4 = (f32[16,128]{1,0:T(8,128)S(1)}, f32[16,128]{1,0:T(8,128)S(1)}, u32[]{:S(2)}, u32[]{:S(2)}) collective-permute-start(f32[16,128]{1,0:T(8,128)S(1)} %get-tuple-element.82), channel_id=1, source_target_pairs={{0,0},{16,1},{32,2},{48,3},{64,4},{80,5},{96,6},{112,7},{128,8},{1... | collective-permute-start | bytes 24584 | tf_op jit(solution)/shard_map/ppermute | solution.py:557
  112.9 23.1 %all-to-all-start.14 = ((f32[16,40,128]{2,1,0:T(8,128)}), f32[16,40,128]{2,1,0:T(8,128)S(1)}, u32[]{:S(2)}, u32[]{:S(2)}) async-start(f32[16,40,128]{2,1,0:T(8,128)} %plain_inner.1), calls=%async_computation.14 | async-start | bytes 655360 | tf_op jit(solution)/shard_map/all_to_all | solution.py:519
  143.9 0.8 copy-start.7
  144.7 0.7 copy-start.15
  145.4 0.6 copy-start.16
  146.0 15.6 %all-to-all-start.15 = ((f32[16,32,128]{2,1,0:T(8,128)}), f32[16,32,128]{2,1,0:T(8,128)}, u32[]{:S(2)}, u32[]{:S(2)}) async-start(f32[16,32,128]{2,1,0:T(8,128)} %copy-done.15), calls=%async_computation.15 | async-start | bytes 524288 | tf_op jit(solution)/shard_map/all_to_all | solution.py:519
  150.3 0.8 copy-start.17
  163.3 15.1 %all-to-all-start.16 = ((f32[16,32,128]{2,1,0:T(8,128)}), f32[16,32,128]{2,1,0:T(8,128)S(1)}, u32[]{:S(2)}, u32[]{:S(2)}) async-start(f32[16,32,128]{2,1,0:T(8,128)} %get-tuple-element.91), calls=%async_computation.16 | async-start | bytes 524288 | tf_op jit(solution)/shard_map/all_to_all | solution.py:519
  166.8 6.2 %collective-permute-start.5 = (f32[16,128]{1,0:T(8,128)S(1)}, f32[16,128]{1,0:T(8,128)S(1)}, u32[]{:S(2)}, u32[]{:S(2)}) collective-permute-start(f32[16,128]{1,0:T(8,128)S(1)} %get-tuple-element.98), channel_id=1, source_target_pairs={{0,0},{1,16},{2,32},{3,48},{4,64},{5,80},{6,96},{7,112},{8,128},{9... | collective-permute-start | bytes 24584 | tf_op jit(solution)/shard_map/ppermute | solution.py:557
  179.7 25.9 %all-to-all-start.17 = ((f32[32,40,128]{2,1,0:T(8,128)}), f32[32,40,128]{2,1,0:T(8,128)S(1)}, u32[]{:S(2)}, u32[]{:S(2)}) async-start(f32[32,40,128]{2,1,0:T(8,128)} %inner.5), calls=%async_computation.17 | async-start | bytes 1310720 | tf_op jit(solution)/shard_map/all_to_all | solution.py:519
  187.0 1.0 copy-start.8
  199.8 0.8 copy-start.5
  205.6 1.1 copy-start.6
  234.0 20.0 %all-to-all-start.1 = ((f32[32,24,128]{2,1,0:T(8,128)}), f32[32,24,128]{2,1,0:T(8,128)S(1)}, u32[]{:S(2)}, u32[]{:S(2)}) async-start(f32[32,24,128]{2,1,0:T(8,128)} %get-tuple-element.21), calls=%async_computation.1 | async-start | bytes 786432 | tf_op jit(solution)/shard_map/cond/branch_0_fun/all_to_all | solution.py:519
  285.2 17.3 %all-to-all-start.3 = ((f32[32,24,128]{2,1,0:T(8,128)}), f32[32,24,128]{2,1,0:T(8,128)S(1)}, u32[]{:S(2)}, u32[]{:S(2)}) async-start(f32[32,24,128]{2,1,0:T(8,128)} %pad_maximum_fusion), calls=%async_computation.3 | async-start | bytes 786432 | tf_op jit(solution)/shard_map/cond/branch_0_fun/all_to_all | solution.py:519
  290.2 12.3 %collective-permute-start = (f32[48,128]{1,0:T(8,128)S(1)}, f32[48,128]{1,0:T(8,128)S(1)}, u32[]{:S(2)}, u32[]{:S(2)}) collective-permute-start(f32[48,128]{1,0:T(8,128)S(1)} %slice_bitcast_fusion.raw_ref), channel_id=1, source_target_pairs={{0,0},{1,16},{2,32},{3,48},{4,64},{5,80},{6,96},{7,112},{8,128},{9... | collective-permute-start | bytes 73736 | tf_op jit(solution)/shard_map/cond/branch_0_fun/ppermute | solution.py:633
  303.7 34.3 %all-to-all-start.4 = ((f32[32,72,128]{2,1,0:T(8,128)}), f32[32,72,128]{2,1,0:T(8,128)S(1)}, u32[]{:S(2)}, u32[]{:S(2)}) async-start(f32[32,72,128]{2,1,0:T(8,128)} %get-tuple-element.24), calls=%async_computation.4 | async-start | bytes 2359296 | tf_op jit(solution)/shard_map/cond/branch_0_fun/all_to_all | solution.py:519
  312.1 28.1 %collective-permute-start.1 = (f32[16,128]{1,0:T(8,128)S(1)}, f32[16,128]{1,0:T(8,128)S(1)}, u32[]{:S(2)}, u32[]{:S(2)}) collective-permute-start(f32[16,128]{1,0:T(8,128)S(1)} %get-tuple-element.27), channel_id=1, source_target_pairs={{0,0},{16,1},{32,2},{48,3},{64,4},{80,5},{96,6},{112,7},{128,8},{1... | collective-permute-start | bytes 24584 | tf_op jit(solution)/shard_map/cond/branch_0_fun/ppermute | solution.py:557
  341.6 23.5 %all-to-all-start.5 = ((f32[16,40,128]{2,1,0:T(8,128)}), f32[16,40,128]{2,1,0:T(8,128)S(1)}, u32[]{:S(2)}, u32[]{:S(2)}) async-start(f32[16,40,128]{2,1,0:T(8,128)} %inner.3), calls=%async_computation.5 | async-start | bytes 655360 | tf_op jit(solution)/shard_map/cond/branch_0_fun/all_to_all | solution.py:519
  358.8 0.8 copy-start.9
  365.0 1.0 copy-start.10
  370.3 0.8 copy-start
  371.1 13.8 %all-to-all-start.6 = ((f32[16,24,128]{2,1,0:T(8,128)}), f32[16,24,128]{2,1,0:T(8,128)}, u32[]{:S(2)}, u32[]{:S(2)}) async-start(f32[16,24,128]{2,1,0:T(8,128)} %get-tuple-element.34), calls=%async_computation.6 | async-start | bytes 393216 | tf_op jit(solution)/shard_map/cond/branch_0_fun/all_to_all | solution.py:519
  377.0 0.7 copy-start.13
  384.9 1.0 copy-start.14
  394.6 0.7 copy-start.3
  415.0 17.9 %all-to-all-start.8 = ((f32[32,24,128]{2,1,0:T(8,128)}), f32[32,24,128]{2,1,0:T(8,128)S(1)}, u32[]{:S(2)}, u32[]{:S(2)}) async-start(f32[32,24,128]{2,1,0:T(8,128)} %get-tuple-element.38), calls=%async_computation.8 | async-start | bytes 786432 | tf_op jit(solution)/shard_map/cond/branch_0_fun/all_to_all | solution.py:519
  421.6 11.3 %collective-permute-start.2 = (f32[16,128]{1,0:T(8,128)S(1)}, f32[16,128]{1,0:T(8,128)S(1)}, u32[]{:S(2)}, u32[]{:S(2)}) collective-permute-start(f32[16,128]{1,0:T(8,128)S(1)} %get-tuple-element.41), channel_id=1, source_target_pairs={{0,0},{16,1},{32,2},{48,3},{64,4},{80,5},{96,6},{112,7},{128,8},{1... | collective-permute-start | bytes 24584 | tf_op jit(solution)/shard_map/cond/branch_0_fun/ppermute | solution.py:557
  433.5 0.8 copy-start.2
  434.3 24.6 %all-to-all-start.9 = ((f32[16,40,128]{2,1,0:T(8,128)}), f32[16,40,128]{2,1,0:T(8,128)}, u32[]{:S(2)}, u32[]{:S(2)}) async-start(f32[16,40,128]{2,1,0:T(8,128)} %copy-done.2), calls=%async_computation.9 | async-start | bytes 655360 | tf_op jit(solution)/shard_map/cond/branch_0_fun/all_to_all | solution.py:519
  444.1 4.8 %copy-start.1 = (f32[1024,128]{1,0:T(8,128)S(1)}, f32[1024,128]{1,0:T(8,128)}, u32[]{:S(2)}) copy-start(f32[1024,128]{1,0:T(8,128)} %copy-done) | copy-start | bytes 1572868 | tf_op jit(solution)/shard_map/cond
  444.1 4.8 %copy-start.4 = (f32[512,64]{1,0:T(8,128)S(1)}, f32[512,64]{1,0:T(8,128)}, u32[]{:S(2)}) copy-start(f32[512,64]{1,0:T(8,128)} %copy-done.3) | copy-start | bytes 393220 | tf_op jit(solution)/shard_map/cond
  458.2 0.7 copy-start.11
  458.9 1.0 copy-start.12

commit v5 on v4

--- a/solution.py
+++ b/solution.py
@@ -688,7 +688,11 @@
         current, left, right, vectors, factors = lax.cond(
             fine, lambda *given: given, lambda *_: careful(), *ready
         )
-        return current - nt(left, right), vectors.transpose(0, 2, 1), factors
+        change = lax.dot_general(
+            left, right, (((1,), (1,)), ((), ())),
+            precision=lax.Precision.HIGH, preferred_element_type=jnp.float32,
+        )
+        return current - change, vectors.transpose(0, 2, 1), factors
 
     return jax.shard_map(
         local,

time: 475 us -> 474 us (level)
    dot_general x5 -> x4, matrix products: 16.6 us -> 11.7 us  [nt(): lax.dot_general(a, b, (((1,), (1,)), ((), ())), precision=precise, prefer...]
where the time goes in v5:
time: 474 us; the launch traced here: 468 us
  waiting for transfers between devices  128 us (27%)
  starting transfers between devices  123 us (26%)
  blocking collectives  89.4 us (19%)
  Pallas kernels  82.5 us (17%)
  matrix products  24.8 us (5%)
  local copies, waits for them, and re-layouts  16 us (3%)
    all_to_all x14, waiting for transfers between devices, swap(): return lax.all_to_all(x, axis, 0, 0)  97.7 us
    all_to_all x14, starting transfers between devices, swap(): return lax.all_to_all(x, axis, 0, 0)  93.4 us
    all_to_all x4, blocking collectives, swap(): return lax.all_to_all(x, axis, 0, 0)  89.4 us
    pallas_call x23, Pallas kernels, call(): pl.pallas_call(functools.partial(kernel, *statics), out_shape=out_shape,...  80.6 us
    ppermute x4, waiting for transfers between devices, image_round(): lax.ppermute(image_chunk, ('row', 'col'), targets)  30 us
    ppermute x4, starting transfers between devices, image_round(): lax.ppermute(image_chunk, ('row', 'col'), targets)  22.6 us
    dot_general x4, matrix products, nt(): lax.dot_general(a, b, (((1,), (1,)), ((), ())), precision=precise, prefer...  11.7 us
  transfers between devices with their start and end apart: 20, of which 16 were waited for; matrix products, arithmetic and copies ran while one was open for 3% of the time, Pallas kernels for 9%

profile of v5, /device:TPU:1, one launch (start us, length us, event | category | flops | bytes accessed | tf_op | source)
XLA Modules:
  0.0 467.8 jit_solution(13755038186321823147)
XLA Ops:
  2.5 26.4 %all_to_all.83 = f32[16,48,128]{2,1,0:T(8,128)S(1)} all-to-all(f32[16,48,128]{2,1,0:T(8,128)} %plain_start.1), channel_id=1, replica_groups=mesh['row'=32,'col'=16] {'col'}, dimensions={0} | all-to-all | bytes 786432 | tf_op jit(solution)/shard_map/all_to_all | solution.py:519
  29.7 3.5 all-to-all-start.11
  33.1 14.0 %all-to-all-done.11.raw_ref.raw_r_ref = f32[16,48,128]{2,1,0:T(8,128)S(1)} async-done(((f32[16,48,128]{2,1,0:T(8,128)}), f32[16,48,128]{2,1,0:T(8,128)S(1)}, u32[]{:S(2)}, u32[]{:S(2)}) %all-to-all-start.11) | async-done | bytes 393248 | tf_op jit(solution)/shard_map/all_to_all | solution.py:519
  51.9 9.7 %all-to-all-start.12 = ((f32[32,24,128]{2,1,0:T(8,128)}), f32[32,24,128]{2,1,0:T(8,128)S(1)}, u32[]{:S(2)}, u32[]{:S(2)}) async-start(f32[32,24,128]{2,1,0:T(8,128)} %pad_maximum_fusion.2), calls=%async_computation.12 | async-start | bytes 786432 | tf_op jit(solution)/shard_map/all_to_all | solution.py:519
  64.4 12.1 %all-to-all-done.12.got_ref = f32[32,24,128]{2,1,0:T(8,128)S(1)} async-done(((f32[32,24,128]{2,1,0:T(8,128)}), f32[32,24,128]{2,1,0:T(8,128)S(1)}, u32[]{:S(2)}, u32[]{:S(2)}) %all-to-all-start.12) | async-done | bytes 393248 | tf_op jit(solution)/shard_map/all_to_all | solution.py:519
  77.6 5.8 %all-to-all-start.13 = ((f32[32,72,128]{2,1,0:T(8,128)}), f32[32,72,128]{2,1,0:T(8,128)S(1)}, u32[]{:S(2)}, u32[]{:S(2)}) async-start(f32[32,72,128]{2,1,0:T(8,128)} %get-tuple-element.80), calls=%async_computation.13 | async-start | bytes 2359296 | tf_op jit(solution)/shard_map/all_to_all | solution.py:519
  83.4 6.4 %collective-permute-start.4 = (f32[16,128]{1,0:T(8,128)S(1)}, f32[16,128]{1,0:T(8,128)S(1)}, u32[]{:S(2)}, u32[]{:S(2)}) collective-permute-start(f32[16,128]{1,0:T(8,128)S(1)} %get-tuple-element.82), channel_id=1, source_target_pairs={{0,0},{16,1},{32,2},{48,3},{64,4},{80,5},{96,6},{112,7},{128,8},{1... | collective-permute-start | bytes 24584 | tf_op jit(solution)/shard_map/ppermute | solution.py:557
  89.8 21.7 %collective-permute-done.4.chunk_ref = f32[16,128]{1,0:T(8,128)S(1)} collective-permute-done((f32[16,128]{1,0:T(8,128)S(1)}, f32[16,128]{1,0:T(8,128)S(1)}, u32[]{:S(2)}, u32[]{:S(2)}) %collective-permute-start.4) | collective-permute-done | bytes 8224 | tf_op jit(solution)/shard_map/ppermute | solution.py:557
  112.9 10.2 %all-to-all-start.14 = ((f32[16,40,128]{2,1,0:T(8,128)}), f32[16,40,128]{2,1,0:T(8,128)S(1)}, u32[]{:S(2)}, u32[]{:S(2)}) async-start(f32[16,40,128]{2,1,0:T(8,128)} %plain_inner.1), calls=%async_computation.14 | async-start | bytes 655360 | tf_op jit(solution)/shard_map/all_to_all | solution.py:519
  123.1 9.3 %plain_factor.1 = (f32[8,64,64]{2,1,0:T(8,128)S(1)}, f32[1024,128]{1,0:T(8,128)S(1)}, s32[1]{0:T(128)}) custom-call(s32[1]{0:T(128)} %bitcast.6.col_ref, f32[32,72,128]{2,1,0:T(8,128)S(1)} %all-to-all-done.13.gathered_ref.raw_ref.old_ref), custom_call_target="tpu_custom_call" | custom-call | flops 16777216 | bytes 4194304 | tf_op jit(solution)/shard_map/plain_factor/pallas_call | solution.py:505
  132.5 3.6 all-to-all-done.14.got_ref
  136.1 7.8 %plain_cols.1 = (f32[1024,128]{1,0:T(8,128)S(1)}, f32[1024,128]{1,0:T(8,128)S(1)}, f32[2,64,64]{2,1,0:T(8,128)S(1)}, f32[16,32,128]{2,1,0:T(8,128)S(1)}) custom-call(s32[1]{0:T(128)} %bitcast.6.col_ref, f32[16,40,128]{2,1,0:T(8,128)S(1)} %all-to-all-done.14.got_ref, f32[8,64,64]{2,1,0:T(8,128)S(1)} %get-tuple-element.83.small_ref, ...), custom_call_target="tpu_custom_call" | custom-call | flops 16777216 | bytes 4194304 | tf_op jit(solution)/shard_map/plain_cols/pallas_call | solution.py:505
  146.0 4.3 all-to-all-start.15
  153.0 4.7 %convolution_subtract_fusion.2 = f32[512,1024]{1,0:T(8,128)} fusion(f32[512,1024]{1,0:T(8,128)} %matrix_ref.3, f32[512,128]{1,0:T(8,128)S(1)} %get-tuple-element.94.pair_r_ref, f32[1024,128]{1,0:T(8,128)S(1)} %get-tuple-element.88.pair_c_ref), kind=kOutput, calls=%fused_computation.11 | convolution fusion | flops 805830656 | bytes 4980736 | tf_op jit(solution)/shard_map/dot_general | solution.py:27
  157.7 3.9 all-to-all-done.15.got_ref
  163.3 3.4 all-to-all-start.16
  166.8 3.7 collective-permute-start.5
  172.9 5.5 %all-to-all-done.16.gathered_ref = f32[16,32,128]{2,1,0:T(8,128)S(1)} async-done(((f32[16,32,128]{2,1,0:T(8,128)}), f32[16,32,128]{2,1,0:T(8,128)S(1)}, u32[]{:S(2)}, u32[]{:S(2)}) %all-to-all-start.16) | async-done | bytes 262176 | tf_op jit(solution)/shard_map/all_to_all | solution.py:519
  179.7 7.2 %all-to-all-start.17 = ((f32[32,40,128]{2,1,0:T(8,128)}), f32[32,40,128]{2,1,0:T(8,128)S(1)}, u32[]{:S(2)}, u32[]{:S(2)}) async-start(f32[32,40,128]{2,1,0:T(8,128)} %inner.5), calls=%async_computation.17 | async-start | bytes 1310720 | tf_op jit(solution)/shard_map/all_to_all | solution.py:519
  188.0 11.8 %plain_second.1 = (f32[1152,128]{1,0:T(8,128)S(1)}, f32[512,128]{1,0:T(8,128)}, f32[2,64,512]{2,1,0:T(8,128)}, f32[2,64,64]{2,1,0:T(8,128)}, s32[1]{0:T(128)}) custom-call(s32[1]{0:T(128)} %bitcast.7.index_ref.row_ref, s32[1]{0:T(128)} %bitcast.6.col_ref, f32[16,32,128]{2,1,0:T(8,128)S(1)} %all-to-all-done.16.gathered_ref, ...), custom_call_target="tpu_custom_call" | custom-call | flops 16777216 | bytes 4194304 | tf_op jit(solution)/shard_map/plain_second/pallas_call | solution.py:505
  201.8 3.8 all-to-all-done.17.got_ref
  209.6 253.8 %conditional.1 = ((f32[512,1024]{1,0:T(8,128)}, f32[512,128]{1,0:T(8,128)}, f32[1024,128]{1,0:T(8,128)}, f32[2,64,512]{2,1,0:T(8,128)}, f32[2,64,64]{2,1,0:T(8,128)})) conditional(s32[]{:T(128)} %bitcast.11, (f32[512,1024]{1,0:T(8,128)}, s32[1]{0:T(128)}, s32[]{:T(128)}, s32[1]{0:T(128)}, s32[1024,1]{0,1:T(1,128)S(1)}, /*index=5*/()) %tuple.17, ...), branch_computations={%region_0.1_spmd, %region_1.2_spmd} | conditional | flops 1930364928 | bytes 98622168 | solution.py:688
  211.9 22.2 %all_to_all.80 = f32[16,48,128]{2,1,0:T(8,128)S(1)} all-to-all(f32[16,48,128]{2,1,0:T(8,128)S(1)} %get-tuple-element.20), channel_id=1, replica_groups=mesh['row'=32,'col'=16] {'col'}, dimensions={0} | all-to-all | bytes 786432 | tf_op jit(solution)/shard_map/cond/branch_0_fun/all_to_all | solution.py:519
  234.0 5.1 %all-to-all-start.1 = ((f32[32,24,128]{2,1,0:T(8,128)}), f32[32,24,128]{2,1,0:T(8,128)S(1)}, u32[]{:S(2)}, u32[]{:S(2)}) async-start(f32[32,24,128]{2,1,0:T(8,128)} %get-tuple-element.21), calls=%async_computation.1 | async-start | bytes 786432 | tf_op jit(solution)/shard_map/cond/branch_0_fun/all_to_all | solution.py:519
  239.2 14.9 %all-to-all-done.1.got_ref = f32[32,24,128]{2,1,0:T(8,128)S(1)} async-done(((f32[32,24,128]{2,1,0:T(8,128)}), f32[32,24,128]{2,1,0:T(8,128)S(1)}, u32[]{:S(2)}, u32[]{:S(2)}) %all-to-all-start.1) | async-done | bytes 393248 | tf_op jit(solution)/shard_map/cond/branch_0_fun/all_to_all | solution.py:519
  254.1 22.3 %all_to_all.81.raw_ref.raw_r_ref = f32[16,72,128]{2,1,0:T(8,128)S(1)} all-to-all(f32[16,72,128]{2,1,0:T(8,128)S(1)} %relay.1), channel_id=1, replica_groups=mesh['row'=32,'col'=16] {'col'}, dimensions={0} | all-to-all | bytes 1179648 | tf_op jit(solution)/shard_map/cond/branch_0_fun/all_to_all | solution.py:519
  276.5 4.5 first_once.1
  285.2 5.0 %all-to-all-start.3 = ((f32[32,24,128]{2,1,0:T(8,128)}), f32[32,24,128]{2,1,0:T(8,128)S(1)}, u32[]{:S(2)}, u32[]{:S(2)}) async-start(f32[32,24,128]{2,1,0:T(8,128)} %pad_maximum_fusion), calls=%async_computation.3 | async-start | bytes 786432 | tf_op jit(solution)/shard_map/cond/branch_0_fun/all_to_all | solution.py:519
  290.2 3.7 collective-permute-start
  293.9 8.6 %all-to-all-done.3.got_ref = f32[32,24,128]{2,1,0:T(8,128)S(1)} async-done(((f32[32,24,128]{2,1,0:T(8,128)}), f32[32,24,128]{2,1,0:T(8,128)S(1)}, u32[]{:S(2)}, u32[]{:S(2)}) %all-to-all-start.3) | async-done | bytes 393248 | tf_op jit(solution)/shard_map/cond/branch_0_fun/all_to_all | solution.py:519
  303.7 8.4 %all-to-all-start.4 = ((f32[32,72,128]{2,1,0:T(8,128)}), f32[32,72,128]{2,1,0:T(8,128)S(1)}, u32[]{:S(2)}, u32[]{:S(2)}) async-start(f32[32,72,128]{2,1,0:T(8,128)} %get-tuple-element.24), calls=%async_computation.4 | async-start | bytes 2359296 | tf_op jit(solution)/shard_map/cond/branch_0_fun/all_to_all | solution.py:519
  312.1 7.3 %collective-permute-start.1 = (f32[16,128]{1,0:T(8,128)S(1)}, f32[16,128]{1,0:T(8,128)S(1)}, u32[]{:S(2)}, u32[]{:S(2)}) collective-permute-start(f32[16,128]{1,0:T(8,128)S(1)} %get-tuple-element.27), channel_id=1, source_target_pairs={{0,0},{16,1},{32,2},{48,3},{64,4},{80,5},{96,6},{112,7},{128,8},{1... | collective-permute-start | bytes 24584 | tf_op jit(solution)/shard_map/cond/branch_0_fun/ppermute | solution.py:557
  319.4 18.6 %all-to-all-done.4.gathered_ref.raw_ref.old_ref = f32[32,72,128]{2,1,0:T(8,128)S(1)} async-done(((f32[32,72,128]{2,1,0:T(8,128)}), f32[32,72,128]{2,1,0:T(8,128)S(1)}, u32[]{:S(2)}, u32[]{:S(2)}) %all-to-all-start.4) | async-done | bytes 1179680 | tf_op jit(solution)/shard_map/cond/branch_0_fun/all_to_all | solution.py:519
  341.6 10.4 %all-to-all-start.5 = ((f32[16,40,128]{2,1,0:T(8,128)}), f32[16,40,128]{2,1,0:T(8,128)S(1)}, u32[]{:S(2)}, u32[]{:S(2)}) async-start(f32[16,40,128]{2,1,0:T(8,128)} %inner.3), calls=%async_computation.5 | async-start | bytes 655360 | tf_op jit(solution)/shard_map/cond/branch_0_fun/all_to_all | solution.py:519
  352.0 6.8 %first_factor.1 = (f32[8,64,64]{2,1,0:T(8,128)S(1)}, f32[1024,128]{1,0:T(8,128)S(1)}, s32[1]{0:T(128)}) custom-call(s32[1]{0:T(128)} %get-tuple-element.28.col_ref, f32[32,72,128]{2,1,0:T(8,128)S(1)} %all-to-all-done.4.gathered_ref.raw_ref.old_ref, f32[1024,64]{1,0:T(8,128)S(1)} %fusion.5.once_ref.once_c_ref), custom_call_target="tpu_custom_call" | custom-call | flops 16777216 | bytes 4194304 | tf_op jit(solution)/shard_map/cond/branch_0_fun/first_factor/pallas_call | solution.py:505
  359.6 5.5 %all-to-all-done.5.got_ref = f32[16,40,128]{2,1,0:T(8,128)S(1)} async-done(((f32[16,40,128]{2,1,0:T(8,128)}), f32[16,40,128]{2,1,0:T(8,128)S(1)}, u32[]{:S(2)}, u32[]{:S(2)}) %all-to-all-start.5) | async-done | bytes 327712 | tf_op jit(solution)/shard_map/cond/branch_0_fun/all_to_all | solution.py:519
  366.1 4.2 first_cols.1
  371.1 4.1 all-to-all-start.6
  377.7 7.1 %all-to-all-done.6.got_ref = f32[16,24,128]{2,1,0:T(8,128)} async-done(((f32[16,24,128]{2,1,0:T(8,128)}), f32[16,24,128]{2,1,0:T(8,128)}, u32[]{:S(2)}, u32[]{:S(2)}) %all-to-all-start.6) | async-done | bytes 196640 | tf_op jit(solution)/shard_map/cond/branch_0_fun/all_to_all | solution.py:519
  385.8 5.7 %second_once.1 = (f32[64,64]{1,0:T(8,128)S(1)}, f32[512,64]{1,0:T(8,128)S(1)}, f32[32,8,128]{2,1,0:T(8,128)S(1)}) custom-call(s32[1]{0:T(128)} %get-tuple-element.19.index_ref.row_ref, f32[16,24,128]{2,1,0:T(8,128)} %all-to-all-done.6.got_ref, f32[16,72,128]{2,1,0:T(8,128)S(1)} %all_to_all.81.raw_ref.raw_r_ref, f32[512,64]{1,0:T(8,128)S(1)} %copy-done.14, ...), custom_call_target="tpu_custom_call" | custom-call | flops 16777216 | bytes 4194304 | tf_op jit(solution)/shard_map/cond/branch_0_fun/second_once/pallas_call | solution.py:505
  395.7 18.5 %all_to_all.82.got_ref = f32[32,24,128]{2,1,0:T(8,128)S(1)} all-to-all(f32[32,24,128]{2,1,0:T(8,128)S(1)} %pad_maximum_fusion.1), channel_id=1, replica_groups=mesh['row'=32,'col'=16] {'row'}, dimensions={0} | all-to-all | bytes 786432 | tf_op jit(solution)/shard_map/cond/branch_0_fun/all_to_all | solution.py:519
  415.0 6.5 %all-to-all-start.8 = ((f32[32,24,128]{2,1,0:T(8,128)}), f32[32,24,128]{2,1,0:T(8,128)S(1)}, u32[]{:S(2)}, u32[]{:S(2)}) async-start(f32[32,24,128]{2,1,0:T(8,128)} %get-tuple-element.38), calls=%async_computation.8 | async-start | bytes 786432 | tf_op jit(solution)/shard_map/cond/branch_0_fun/all_to_all | solution.py:519
  421.6 5.2 %collective-permute-start.2 = (f32[16,128]{1,0:T(8,128)S(1)}, f32[16,128]{1,0:T(8,128)S(1)}, u32[]{:S(2)}, u32[]{:S(2)}) collective-permute-start(f32[16,128]{1,0:T(8,128)S(1)} %get-tuple-element.41), channel_id=1, source_target_pairs={{0,0},{16,1},{32,2},{48,3},{64,4},{80,5},{96,6},{112,7},{128,8},{1... | collective-permute-start | bytes 24584 | tf_op jit(solution)/shard_map/cond/branch_0_fun/ppermute | solution.py:557
  428.4 4.4 collective-permute-done.2.chunk_ref
  434.3 9.8 %all-to-all-start.9 = ((f32[16,40,128]{2,1,0:T(8,128)}), f32[16,40,128]{2,1,0:T(8,128)}, u32[]{:S(2)}, u32[]{:S(2)}) async-start(f32[16,40,128]{2,1,0:T(8,128)} %copy-done.2), calls=%async_computation.9 | async-start | bytes 655360 | tf_op jit(solution)/shard_map/cond/branch_0_fun/all_to_all | solution.py:519
  444.1 4.8 %convolution_subtract_fusion = f32[512,1024]{1,0:T(8,128)} fusion(f32[512,1024]{1,0:T(8,128)} %get-tuple-element.18, f32[512,128]{1,0:T(8,128)S(1)} %get-tuple-element.32.pair_ref.pair_r_ref, f32[1024,128]{1,0:T(8,128)S(1)} %get-tuple-element.33.pair_c_ref), kind=kOutput, calls=%fused_computation | convolution fusion | flops 805830656 | bytes 4980736 | tf_op jit(solution)/shard_map/cond/branch_0_fun/dot_general | solution.py:27
  448.9 9.3 %second_factor.1 = (f32[1024,128]{1,0:T(8,128)}, f32[640,128]{1,0:T(8,128)S(1)}, f32[2,64,512]{2,1,0:T(8,128)}, f32[2,64,64]{2,1,0:T(8,128)}) custom-call(s32[1]{0:T(128)} %get-tuple-element.19.index_ref.row_ref, s32[1]{0:T(128)} %get-tuple-element.28.col_ref, f32[32,24,128]{2,1,0:T(8,128)S(1)} %all-to-all-done.8.gathered_ref, ...), custom_call_target="tpu_custom_call" | custom-call | flops 16777216 | bytes 4194304 | tf_op jit(solution)/shard_map/cond/branch_0_fun/second_factor/pallas_call | solution.py:505
  463.4 4.2 convolution_subtract_fusion.1
  (82 shorter events, 59.1 us)
Async XLA Ops:
  29.7 17.4 %all-to-all-start.11 = ((f32[16,48,128]{2,1,0:T(8,128)}), f32[16,48,128]{2,1,0:T(8,128)S(1)}, u32[]{:S(2)}, u32[]{:S(2)}) async-start(f32[16,48,128]{2,1,0:T(8,128)} %broadcast_in_dim.23), calls=%async_computation.11 | async-start | bytes 786432 | tf_op jit(solution)/shard_map/all_to_all | solution.py:519
  51.9 24.6 %all-to-all-start.12 = ((f32[32,24,128]{2,1,0:T(8,128)}), f32[32,24,128]{2,1,0:T(8,128)S(1)}, u32[]{:S(2)}, u32[]{:S(2)}) async-start(f32[32,24,128]{2,1,0:T(8,128)} %pad_maximum_fusion.2), calls=%async_computation.12 | async-start | bytes 786432 | tf_op jit(solution)/shard_map/all_to_all | solution.py:519
  61.5 14.9 %collective-permute-start.3 = (f32[48,128]{1,0:T(8,128)S(1)}, f32[48,128]{1,0:T(8,128)S(1)}, u32[]{:S(2)}, u32[]{:S(2)}) collective-permute-start(f32[48,128]{1,0:T(8,128)S(1)} %slice_bitcast_fusion.1), channel_id=1, source_target_pairs={{0,0},{1,16},{2,32},{3,48},{4,64},{5,80},{6,96},{7,112},{8,128},{9... | collective-permute-start | bytes 73736 | tf_op jit(solution)/shard_map/ppermute | solution.py:577
  77.6 34.0 %all-to-all-start.13 = ((f32[32,72,128]{2,1,0:T(8,128)}), f32[32,72,128]{2,1,0:T(8,128)S(1)}, u32[]{:S(2)}, u32[]{:S(2)}) async-start(f32[32,72,128]{2,1,0:T(8,128)} %get-tuple-element.80), calls=%async_computation.13 | async-start | bytes 2359296 | tf_op jit(solution)/shard_map/all_to_all | solution.py:519
  83.4 28.1 %collective-permute-start.4 = (f32[16,128]{1,0:T(8,128)S(1)}, f32[16,128]{1,0:T(8,128)S(1)}, u32[]{:S(2)}, u32[]{:S(2)}) collective-permute-start(f32[16,128]{1,0:T(8,128)S(1)} %get-tuple-element.82), channel_id=1, source_target_pairs={{0,0},{16,1},{32,2},{48,3},{64,4},{80,5},{96,6},{112,7},{128,8},{1... | collective-permute-start | bytes 24584 | tf_op jit(solution)/shard_map/ppermute | solution.py:557
  112.9 23.1 %all-to-all-start.14 = ((f32[16,40,128]{2,1,0:T(8,128)}), f32[16,40,128]{2,1,0:T(8,128)S(1)}, u32[]{:S(2)}, u32[]{:S(2)}) async-start(f32[16,40,128]{2,1,0:T(8,128)} %plain_inner.1), calls=%async_computation.14 | async-start | bytes 655360 | tf_op jit(solution)/shard_map/all_to_all | solution.py:519
  143.9 0.8 copy-start.7
  144.7 0.7 copy-start.15
  145.4 0.6 copy-start.16
  146.0 15.6 %all-to-all-start.15 = ((f32[16,32,128]{2,1,0:T(8,128)}), f32[16,32,128]{2,1,0:T(8,128)}, u32[]{:S(2)}, u32[]{:S(2)}) async-start(f32[16,32,128]{2,1,0:T(8,128)} %copy-done.15), calls=%async_computation.15 | async-start | bytes 524288 | tf_op jit(solution)/shard_map/all_to_all | solution.py:519
  150.3 0.8 copy-start.17
  163.3 15.1 %all-to-all-start.16 = ((f32[16,32,128]{2,1,0:T(8,128)}), f32[16,32,128]{2,1,0:T(8,128)S(1)}, u32[]{:S(2)}, u32[]{:S(2)}) async-start(f32[16,32,128]{2,1,0:T(8,128)} %get-tuple-element.91), calls=%async_computation.16 | async-start | bytes 524288 | tf_op jit(solution)/shard_map/all_to_all | solution.py:519
  166.8 6.2 %collective-permute-start.5 = (f32[16,128]{1,0:T(8,128)S(1)}, f32[16,128]{1,0:T(8,128)S(1)}, u32[]{:S(2)}, u32[]{:S(2)}) collective-permute-start(f32[16,128]{1,0:T(8,128)S(1)} %get-tuple-element.98), channel_id=1, source_target_pairs={{0,0},{1,16},{2,32},{3,48},{4,64},{5,80},{6,96},{7,112},{8,128},{9... | collective-permute-start | bytes 24584 | tf_op jit(solution)/shard_map/ppermute | solution.py:557
  179.7 25.9 %all-to-all-start.17 = ((f32[32,40,128]{2,1,0:T(8,128)}), f32[32,40,128]{2,1,0:T(8,128)S(1)}, u32[]{:S(2)}, u32[]{:S(2)}) async-start(f32[32,40,128]{2,1,0:T(8,128)} %inner.5), calls=%async_computation.17 | async-start | bytes 1310720 | tf_op jit(solution)/shard_map/all_to_all | solution.py:519
  187.0 1.0 copy-start.8
  199.8 0.8 copy-start.5
  205.6 1.1 copy-start.6
  234.0 20.0 %all-to-all-start.1 = ((f32[32,24,128]{2,1,0:T(8,128)}), f32[32,24,128]{2,1,0:T(8,128)S(1)}, u32[]{:S(2)}, u32[]{:S(2)}) async-start(f32[32,24,128]{2,1,0:T(8,128)} %get-tuple-element.21), calls=%async_computation.1 | async-start | bytes 786432 | tf_op jit(solution)/shard_map/cond/branch_0_fun/all_to_all | solution.py:519
  285.2 17.3 %all-to-all-start.3 = ((f32[32,24,128]{2,1,0:T(8,128)}), f32[32,24,128]{2,1,0:T(8,128)S(1)}, u32[]{:S(2)}, u32[]{:S(2)}) async-start(f32[32,24,128]{2,1,0:T(8,128)} %pad_maximum_fusion), calls=%async_computation.3 | async-start | bytes 786432 | tf_op jit(solution)/shard_map/cond/branch_0_fun/all_to_all | solution.py:519
  290.2 12.3 %collective-permute-start = (f32[48,128]{1,0:T(8,128)S(1)}, f32[48,128]{1,0:T(8,128)S(1)}, u32[]{:S(2)}, u32[]{:S(2)}) collective-permute-start(f32[48,128]{1,0:T(8,128)S(1)} %slice_bitcast_fusion.raw_ref), channel_id=1, source_target_pairs={{0,0},{1,16},{2,32},{3,48},{4,64},{5,80},{6,96},{7,112},{8,128},{9... | collective-permute-start | bytes 73736 | tf_op jit(solution)/shard_map/cond/branch_0_fun/ppermute | solution.py:633
  303.7 34.3 %all-to-all-start.4 = ((f32[32,72,128]{2,1,0:T(8,128)}), f32[32,72,128]{2,1,0:T(8,128)S(1)}, u32[]{:S(2)}, u32[]{:S(2)}) async-start(f32[32,72,128]{2,1,0:T(8,128)} %get-tuple-element.24), calls=%async_computation.4 | async-start | bytes 2359296 | tf_op jit(solution)/shard_map/cond/branch_0_fun/all_to_all | solution.py:519
  312.1 28.1 %collective-permute-start.1 = (f32[16,128]{1,0:T(8,128)S(1)}, f32[16,128]{1,0:T(8,128)S(1)}, u32[]{:S(2)}, u32[]{:S(2)}) collective-permute-start(f32[16,128]{1,0:T(8,128)S(1)} %get-tuple-element.27), channel_id=1, source_target_pairs={{0,0},{16,1},{32,2},{48,3},{64,4},{80,5},{96,6},{112,7},{128,8},{1... | collective-permute-start | bytes 24584 | tf_op jit(solution)/shard_map/cond/branch_0_fun/ppermute | solution.py:557
  341.6 23.5 %all-to-all-start.5 = ((f32[16,40,128]{2,1,0:T(8,128)}), f32[16,40,128]{2,1,0:T(8,128)S(1)}, u32[]{:S(2)}, u32[]{:S(2)}) async-start(f32[16,40,128]{2,1,0:T(8,128)} %inner.3), calls=%async_computation.5 | async-start | bytes 655360 | tf_op jit(solution)/shard_map/cond/branch_0_fun/all_to_all | solution.py:519
  358.8 0.8 copy-start.9
  365.0 1.0 copy-start.10
  370.3 0.8 copy-start
  371.1 13.8 %all-to-all-start.6 = ((f32[16,24,128]{2,1,0:T(8,128)}), f32[16,24,128]{2,1,0:T(8,128)}, u32[]{:S(2)}, u32[]{:S(2)}) async-start(f32[16,24,128]{2,1,0:T(8,128)} %get-tuple-element.34), calls=%async_computation.6 | async-start | bytes 393216 | tf_op jit(solution)/shard_map/cond/branch_0_fun/all_to_all | solution.py:519
  377.0 0.7 copy-start.13
  384.9 1.0 copy-start.14
  394.6 0.7 copy-start.3
  415.0 17.9 %all-to-all-start.8 = ((f32[32,24,128]{2,1,0:T(8,128)}), f32[32,24,128]{2,1,0:T(8,128)S(1)}, u32[]{:S(2)}, u32[]{:S(2)}) async-start(f32[32,24,128]{2,1,0:T(8,128)} %get-tuple-element.38), calls=%async_computation.8 | async-start | bytes 786432 | tf_op jit(solution)/shard_map/cond/branch_0_fun/all_to_all | solution.py:519
  421.6 11.3 %collective-permute-start.2 = (f32[16,128]{1,0:T(8,128)S(1)}, f32[16,128]{1,0:T(8,128)S(1)}, u32[]{:S(2)}, u32[]{:S(2)}) collective-permute-start(f32[16,128]{1,0:T(8,128)S(1)} %get-tuple-element.41), channel_id=1, source_target_pairs={{0,0},{16,1},{32,2},{48,3},{64,4},{80,5},{96,6},{112,7},{128,8},{1... | collective-permute-start | bytes 24584 | tf_op jit(solution)/shard_map/cond/branch_0_fun/ppermute | solution.py:557
  433.5 0.8 copy-start.2
  434.3 24.6 %all-to-all-start.9 = ((f32[16,40,128]{2,1,0:T(8,128)}), f32[16,40,128]{2,1,0:T(8,128)}, u32[]{:S(2)}, u32[]{:S(2)}) async-start(f32[16,40,128]{2,1,0:T(8,128)} %copy-done.2), calls=%async_computation.9 | async-start | bytes 655360 | tf_op jit(solution)/shard_map/cond/branch_0_fun/all_to_all | solution.py:519
  444.1 4.8 %copy-start.1 = (f32[1024,128]{1,0:T(8,128)S(1)}, f32[1024,128]{1,0:T(8,128)}, u32[]{:S(2)}) copy-start(f32[1024,128]{1,0:T(8,128)} %copy-done) | copy-start | bytes 1572868 | tf_op jit(solution)/shard_map/cond
  444.1 4.8 %copy-start.4 = (f32[512,64]{1,0:T(8,128)S(1)}, f32[512,64]{1,0:T(8,128)}, u32[]{:S(2)}) copy-start(f32[512,64]{1,0:T(8,128)} %copy-done.3) | copy-start | bytes 393220 | tf_op jit(solution)/shard_map/cond
  458.2 0.7 copy-start.11
  458.9 1.0 copy-start.12
